TPU v7x, 32 devices: a whole 2x2x4 slice. The times are simulated.
32 devices in a mesh: row: 8 (over z, x), col: 2 (over y), depth: 2 (over core).
Axes of the slice: x: 2, y: 2, z: 4, core: 2. Of those that a mesh axis runs over, the one named last changes fastest.
Arguments:
- tokens: bfloat16 [64, 8192], P('row', ('col', 'depth')), may hold values from -6 to 6
- grad_out: bfloat16 [64, 8192], P('row', ('col', 'depth')), may hold values from -6 to 6
- gate_weight: bfloat16 [8192, 28672], P(('col', 'depth'), 'row'), may hold values from -0.0625 to 0.0625
- up_weight: bfloat16 [8192, 28672], P(('col', 'depth'), 'row'), may hold values from -0.0625 to 0.0625
- down_weight: bfloat16 [28672, 8192], P('row', ('col', 'depth')), may hold values from -0.03125 to 0.03125
Outputs:
- layer_out: bfloat16 [64, 8192], P('row', ('col', 'depth'))
- grad_tokens: bfloat16 [64, 8192], P('row', ('col', 'depth'))
- grad_gate: bfloat16 [8192, 28672], P(('col', 'depth'), 'row')
- grad_up: bfloat16 [8192, 28672], P(('col', 'depth'), 'row')
- grad_down: bfloat16 [28672, 8192], P('row', ('col', 'depth'))
All inputs are finite; a program needn't handle non-finite values.
Results may differ from a plain program's by a relative error of at most 0.0049.
Values may be sent and summed in bfloat16 or wider, within the bound.
No kernel may reach another device: no remote copies, remote signals or barrier semaphores. Data moves between devices by JAX's collectives and lax.ppermute only.
A program may use at most 256 MiB of HBM per device.

v0:
```python
import jax
import jax.numpy as jnp
from jax import lax
from jax.sharding import PartitionSpec as P


def contract_rows(left, right):
    return lax.dot_general(
        left, right, (((0,), (0,)), ((), ())), preferred_element_type=jnp.float32
    )


def contract_cols(left, right):
    return lax.dot_general(
        left, right, (((1,), (1,)), ((), ())), preferred_element_type=jnp.float32
    )


def gate_grads(d_hidden, gate_pre, up_proj):
    sigmoid_gate = jax.nn.sigmoid(gate_pre)
    d_gate = (d_hidden * up_proj * sigmoid_gate * (1.0 + gate_pre * (1.0 - sigmoid_gate))).astype(
        jnp.bfloat16
    )
    d_up = (d_hidden * gate_pre * sigmoid_gate).astype(jnp.bfloat16)
    return (d_gate, d_up)


def per_device(tokens, grad_out, gate_weight, up_weight, down_weight):
    width_ff = gate_weight.shape[1]
    own_rows = tokens.shape[0]
    tok_all, grad_all = (
        lax.all_gather(tokens, "row", axis=0, tiled=True),
        lax.all_gather(grad_out, "row", axis=0, tiled=True),
    )
    all_rows = tok_all.shape[0]
    share_rows = all_rows // lax.axis_size(("col", "depth"))
    w_both = jnp.concatenate([gate_weight, up_weight], axis=1)

    def ff_sums(term_fn):
        return lax.psum_scatter(
            term_fn(jnp.int32(0), share_rows * lax.axis_size(("col", "depth"))),
            ("col", "depth"),
            scatter_dimension=0,
            tiled=True,
        )

    def ff_panel(operand):
        return lax.all_gather(operand, ("col", "depth"), axis=0, tiled=True)

    def feature_sums(term_fn):
        return lax.psum_scatter(
            term_fn(jnp.int32(0), own_rows * lax.axis_size("row")),
            "row",
            scatter_dimension=0,
            tiled=True,
        )

    def gate_term(offset, length):
        return jnp.dot(tok_all, w_both, preferred_element_type=jnp.float32)

    gate_up = ff_sums(gate_term)
    gate_pre = gate_up[:, :width_ff]
    up_proj = gate_up[:, width_ff:]
    hidden = (gate_pre * jax.nn.sigmoid(gate_pre) * up_proj).astype(jnp.bfloat16)
    hid_all = ff_panel(hidden)

    def out_term(offset, length):
        return jnp.dot(hid_all, down_weight, preferred_element_type=jnp.float32)

    layer_out = feature_sums(out_term).astype(jnp.bfloat16)

    def back_term(offset, length):
        return contract_cols(grad_all, down_weight)

    d_hidden = ff_sums(back_term)
    d_gate, d_up = gate_grads(d_hidden, gate_pre, up_proj)
    d_all = ff_panel(jnp.concatenate([d_gate, d_up], axis=1))

    def input_term(offset, length):
        return contract_cols(d_all, w_both)

    grad_tokens = feature_sums(input_term).astype(jnp.bfloat16)
    grad_down = contract_rows(hid_all, grad_all).astype(jnp.bfloat16)
    grad_both = contract_rows(tok_all, d_all).astype(jnp.bfloat16)
    return (layer_out, grad_tokens, grad_both[:, :width_ff], grad_both[:, width_ff:], grad_down)


def solution(mesh):
    placed = (
        P("row", ("col", "depth")),
        P("row", ("col", "depth")),
        P(("col", "depth"), "row"),
        P(("col", "depth"), "row"),
        P("row", ("col", "depth")),
    )
    return jax.shard_map(
        per_device,
        mesh=mesh,
        in_specs=placed,
        out_specs=(
            P("row", ("col", "depth")),
            P("row", ("col", "depth")),
            P(("col", "depth"), "row"),
            P(("col", "depth"), "row"),
            P("row", ("col", "depth")),
        ),
        check_vma=False,
    )
```

profile of v0, /device:TPU:0, one launch (start us, length us, event | category | flops | bytes accessed | tf_op | source)
XLA Modules:
  0.0 332.2 jit_solution(8976693728166571091)
XLA Ops:
  7.2 0.0 copy-start
  7.2 0.0 reduce-scatter.9.cloned.1.call-start
  7.2 32.7 %all_gather.14 = bf16[64,2048]{1,0:T(8,128)(2,1)S(1)} all-gather(bf16[8,2048]{1,0:T(8,128)(2,1)} %param.6), channel_id=1, replica_groups=mesh['row'=8,'col'=2,'depth'=2] {'row'}, dimensions={0}, use_global_device_ids=true | all-gather | bytes 294912 | tf_op jit(solution)/shard_map/all_gather | solution.py:33
  40.0 10.6 %fusion.2 = f32[64,3584]{1,0:T(8,128)} fusion(bf16[64,2048]{1,0:T(8,128)(2,1)S(1)} %all_gather.14, bf16[3584,2048]{1,0:T(8,128)(2,1)} %param.9), kind=kOutput, calls=%fused_computation.12 | convolution fusion | flops 939524096 | bytes 15859712 | tf_op jit(solution)/shard_map/dot_general | solution.py:14
  50.6 0.0 slice-start
  50.6 0.0 reduce-scatter.9.cloned.1.call-update
  50.6 0.0 reduce-scatter.5.cloned.1.call-start
  50.7 0.0 copy-done
  50.7 30.9 %all_gather.12 = bf16[64,2048]{1,0:T(8,128)(2,1)S(1)} all-gather(bf16[8,2048]{1,0:T(8,128)(2,1)S(1)} %copy-done), channel_id=1, replica_groups=mesh['row'=8,'col'=2,'depth'=2] {'row'}, dimensions={0}, use_global_device_ids=true | all-gather | bytes 294912 | tf_op jit(solution)/shard_map/all_gather | solution.py:32
  81.6 0.0 slice-start.1
  81.6 0.0 slice-start.2
  81.6 0.0 slice-start.3
  81.6 15.3 %constant_dynamic-update-slice_fusion.1 = bf16[2048,7168]{1,0:T(8,128)(2,1)} fusion(bf16[2048,3584]{1,0:T(8,128)(2,1)} %param.7), kind=kLoop, calls=%fused_computation.9 | loop fusion | bytes 29360128
  96.8 0.0 slice-done
  96.9 0.0 slice-done.1
  96.9 0.0 slice-done.2
  96.9 0.0 slice-done.3
  96.9 6.3 %constant_dynamic-update-slice_fusion = bf16[2048,7168]{1,0:T(8,128)(2,1)} fusion(bf16[2048,7168]{1,0:T(8,128)(2,1)} %constant_dynamic-update-slice_fusion.1, bf16[2048,3584]{1,0:T(8,128)(2,1)S(1)} %bitcast.17), kind=kLoop, calls=%fused_computation.8 | loop fusion | bytes 29360128 | tf_op jit(solution)/shard_map/concatenate | solution.py:37
  103.1 13.2 %convolution_bitcast_fusion = f32[64,7168]{1,0:T(8,128)} fusion(bf16[64,2048]{1,0:T(8,128)(2,1)S(1)} %all_gather.12, bf16[2048,7168]{1,0:T(8,128)(2,1)} %constant_dynamic-update-slice_fusion), kind=kOutput, calls=%fused_computation.2 | convolution fusion | flops 1879048192 | bytes 31457280 | tf_op jit(solution)/shard_map/dot_general | solution.py:59
  116.4 0.0 reduce-scatter.5.cloned.1.call-update
  116.4 0.0 reduce-scatter.7.cloned.1.call-start
  116.4 0.0 reduce-scatter.9.cloned.1.call-done
  116.5 30.9 %reduce-scatter.5.cloned.1.call-done = f32[16,7168]{1,0:T(8,128)} async-done(((f32[64,7168]{1,0:T(8,128)}), f32[16,7168]{1,0:T(8,128)}) %reduce-scatter.5.cloned.1.call-update) | async-done | bytes 458768 | tf_op jit(solution)/shard_map/reduce_scatter | solution.py:40
  147.3 1.3 multiply_convert_fusion.1
  148.6 6.4 %all_gather.13 = bf16[64,3584]{1,0:T(8,128)(2,1)S(1)} all-gather(bf16[16,3584]{1,0:T(8,128)(2,1)S(1)} %get-tuple-element.14), channel_id=1, replica_groups=mesh['row'=8,'col'=2,'depth'=2] {'col','depth'}, dimensions={0}, use_global_device_ids=true | all-gather | bytes 573440 | tf_op jit(solution)/shard_map/all_gather | solution.py:48
  155.0 8.6 %fusion.1 = f32[64,2048]{1,0:T(8,128)} fusion(bf16[64,3584]{1,0:T(8,128)(2,1)S(1)} %all_gather.13, bf16[3584,2048]{1,0:T(8,128)(2,1)} %param.9), kind=kOutput, calls=%fused_computation.11 | convolution fusion | flops 939524096 | bytes 15663104 | tf_op jit(solution)/shard_map/dot_general | solution.py:68
  163.7 0.0 reduce-scatter.7.cloned.1.call-update
  163.7 0.0 reduce-scatter.11.cloned.1.call-start
  163.8 9.6 %all_gather.15 = bf16[64,7168]{1,0:T(8,128)(2,1)S(1)} all-gather(bf16[16,7168]{1,0:T(8,128)(2,1)S(1)} %pad_maximum_fusion), channel_id=1, replica_groups=mesh['row'=8,'col'=2,'depth'=2] {'col','depth'}, dimensions={0}, use_global_device_ids=true | all-gather | bytes 1146880 | tf_op jit(solution)/shard_map/all_gather | solution.py:48
  173.4 13.6 %convert_bitcast_fusion = bf16[2048,7168]{0,1:T(8,128)(2,1)} fusion(bf16[64,7168]{1,0:T(8,128)(2,1)S(1)} %all_gather.15, bf16[64,2048]{1,0:T(8,128)(2,1)S(1)} %all_gather.12), kind=kOutput, calls=%fused_computation | convolution fusion | flops 1893728256 | bytes 30539776 | tf_op jit(solution)/shard_map/dot_general | solution.py:8
  187.0 22.5 %fusion = (bf16[2048,3584]{0,1:T(8,128)(2,1)}, bf16[2048,3584]{0,1:T(8,128)(2,1)}) fusion(bf16[2048,7168]{0,1:T(8,128)(2,1)} %convert_bitcast_fusion), kind=kLoop, calls=%fused_computation.10 | loop fusion | bytes 58720256 | tf_op jit(solution)/shard_map/slice | solution.py:85
  209.4 18.7 %copy.10 = bf16[2048,3584]{1,0:T(8,128)(2,1)} copy(bf16[2048,3584]{0,1:T(8,128)(2,1)} %get-tuple-element.11) | data formatting | bytes 29360128
  228.1 18.6 %copy.11 = bf16[2048,3584]{1,0:T(8,128)(2,1)} copy(bf16[2048,3584]{0,1:T(8,128)(2,1)} %get-tuple-element.10) | data formatting | bytes 29360128
  246.7 15.0 %fusion.3 = f32[64,2048]{1,0:T(8,128)} fusion(bf16[64,7168]{1,0:T(8,128)(2,1)S(1)} %all_gather.15, bf16[2048,7168]{1,0:T(8,128)(2,1)} %constant_dynamic-update-slice_fusion), kind=kOutput, calls=%fused_computation.13 | convolution fusion | flops 1879048192 | bytes 30801920 | tf_op jit(solution)/shard_map/dot_general | solution.py:14
  261.7 0.0 reduce-scatter.11.cloned.1.call-update
  261.8 7.6 %convolution_convert_fusion = bf16[3584,2048]{1,0:T(8,128)(2,1)} fusion(bf16[64,3584]{1,0:T(8,128)(2,1)S(1)} %all_gather.13, bf16[64,2048]{1,0:T(8,128)(2,1)S(1)} %all_gather.14), kind=kOutput, calls=%fused_computation.1 | convolution fusion | flops 946864128 | bytes 15400960 | tf_op jit(solution)/shard_map/dot_general | solution.py:8
  269.3 0.0 reduce-scatter.7.cloned.1.call-done
  269.3 1.5 convert_element_type.25
  270.8 53.4 %reduce-scatter.11.cloned.1.call-done = f32[8,2048]{1,0:T(8,128)} async-done(((f32[64,2048]{1,0:T(8,128)}), f32[8,2048]{1,0:T(8,128)}) %reduce-scatter.11.cloned.1.call-update) | async-done | bytes 65552 | tf_op jit(solution)/shard_map/reduce_scatter | solution.py:51
  324.2 1.5 convert_element_type.28
  (2 shorter events, 0.0 us)
Async XLA Ops:
  7.2 43.5 %copy-start = (bf16[8,2048]{1,0:T(8,128)(2,1)S(1)}, bf16[8,2048]{1,0:T(8,128)(2,1)}, u32[]{:S(2)}) copy-start(bf16[8,2048]{1,0:T(8,128)(2,1)} %param.5) | copy-start | bytes 98308
  7.2 109.3 %reduce-scatter.9.cloned.1.call-start = ((), (), s32[]{:S(2)}) async-start(), calls=%async_computation.6 | async-start | bytes 1146880 | tf_op jit(solution)/shard_map/reduce_scatter | solution.py:40
  50.6 46.2 %slice-start = ((s8[14680064]{0:T(1024)(128)(4,1)}), s8[2097152]{0:T(1024)(128)(4,1)S(1)}, s32[]{:S(2)}) async-start(s8[14680064]{0:T(1024)(128)(4,1)} %bitcast.16), calls=%async_computation.8 | async-start | bytes 4194304
  50.6 96.7 %reduce-scatter.5.cloned.1.call-start = ((), (), s32[]{:S(2)}) async-start(), calls=%async_computation.4 | async-start | bytes 2293760 | tf_op jit(solution)/shard_map/reduce_scatter | solution.py:40
  81.6 15.3 %slice-start.1 = ((s8[14680064]{0:T(1024)(128)(4,1)}), s8[4194304]{0:T(1024)(128)(4,1)S(1)}, s32[]{:S(2)}) async-start(s8[14680064]{0:T(1024)(128)(4,1)} %bitcast.16), calls=%async_computation.9 | async-start | bytes 8388608
  81.6 15.3 %slice-start.2 = ((s8[14680064]{0:T(1024)(128)(4,1)}), s8[4194304]{0:T(1024)(128)(4,1)S(1)}, s32[]{:S(2)}) async-start(s8[14680064]{0:T(1024)(128)(4,1)} %bitcast.16), calls=%async_computation.10 | async-start | bytes 8388608
  81.6 15.3 %slice-start.3 = ((s8[14680064]{0:T(1024)(128)(4,1)}), s8[4194304]{0:T(1024)(128)(4,1)S(1)}, s32[]{:S(2)}) async-start(s8[14680064]{0:T(1024)(128)(4,1)} %bitcast.16), calls=%async_computation.11 | async-start | bytes 8388608
  116.4 152.9 %reduce-scatter.7.cloned.1.call-start = ((), (), s32[]{:S(2)}) async-start(), calls=%async_computation.5 | async-start | bytes 589824 | tf_op jit(solution)/shard_map/reduce_scatter | solution.py:51
  163.7 160.5 %reduce-scatter.11.cloned.1.call-start = ((), (), s32[]{:S(2)}) async-start(), calls=%async_computation.7 | async-start | bytes 589824 | tf_op jit(solution)/shard_map/reduce_scatter | solution.py:51
Sparse Core Ops, SparseCore 0:
  50.8 25.0 reduce-scatter.8
  116.5 30.7 reduce-scatter.4
  163.8 62.2 reduce-scatter.6
  261.9 62.2 reduce-scatter.10
where the time goes:
time: 333 us; the launch traced here: 332 us
  waiting for transfers between devices  84.3 us (25%)
  local copies, waits for them, and re-layouts  81.3 us (24%)
  blocking collectives  79.6 us (24%)
  matrix products  68.7 us (21%)
  between operations  13.8 us (4%)
  other arithmetic  4.22 us (1%)
    reduce_scatter x2, waiting for transfers between devices, feature_sums(): lax.psum_scatter(term_fn(jnp.int32(0), own_rows * lax.axis_size('row')),...  53.4 us
    unnamed x13, local copies, waits for them, and re-layouts  52.6 us
    all_gather x1, blocking collectives, per_device(): lax.all_gather(grad_out, 'row', axis=0, tiled=True)  32.7 us
    all_gather x1, blocking collectives, per_device(): lax.all_gather(tokens, 'row', axis=0, tiled=True)  30.9 us
    reduce_scatter x2, waiting for transfers between devices, ff_sums(): lax.psum_scatter(term_fn(jnp.int32(0), share_rows * lax.axis_size(('col',...  30.9 us
    dot_general x2, matrix products, contract_cols(): lax.dot_general(left, right, (((1,), (1,)), ((), ())), preferred_element_...  25.7 us
    slice x1, local copies, waits for them, and re-layouts, per_device(): grad_both[:, width_ff:]  22.5 us
    dot_general x2, matrix products, contract_rows(): lax.dot_general(left, right, (((0,), (0,)), ((), ())), preferred_element_...  21.2 us
  transfers between devices with their start and end apart: 4, of which 2 were waited for; matrix products, arithmetic and copies ran while one was open for 40% of the time, Pallas kernels for 0%

commit v1 on v0

v1 whole, which is shorter than its diff:
```python
import functools

import jax
import jax.numpy as jnp
from jax import lax
from jax.experimental import pallas as pl
from jax.experimental.pallas import tpu as pltpu
from jax.sharding import PartitionSpec as P

BF16 = jnp.bfloat16
F32 = jnp.float32
IN_VMEM = pl.BlockSpec(memory_space=pltpu.VMEM)
IN_SMEM = pl.BlockSpec(memory_space=pltpu.SMEM)
ANYWHERE = pl.BlockSpec(memory_space=pl.ANY)
MIB = 1 << 20


def params(mib):
    return pltpu.CompilerParams(vmem_limit_bytes=mib * MIB)


def cost(flops=0, moved=0, exps=0):
    return pl.CostEstimate(flops=flops, bytes_accessed=moved, transcendentals=exps)


def in_vmem(array):
    return pltpu.with_memory_space_constraint(array, pltpu.VMEM)


def in_hbm(array):
    return pltpu.with_memory_space_constraint(array, pltpu.HBM)


def swap(array, axis, distance):
    size = lax.axis_size(axis)
    return lax.ppermute(array, axis, [(i, i ^ distance) for i in range(size)])


def tile_of(extent, largest):
    best = 128
    for tile in range(128, largest + 1, 128):
        if extent % tile == 0:
            best = tile
    return best


def contract_cols(left, right):
    return lax.dot_general(left, right, (((1,), (1,)), ((), ())), preferred_element_type=F32)


def contract_rows(left, right):
    return lax.dot_general(left, right, (((0,), (0,)), ((), ())), preferred_element_type=F32)


def through(arrays, first_input, first_output):
    shapes = [pltpu.VMEM(a.shape, a.dtype) for a in arrays]
    return shapes, {first_input + i: first_output + i for i in range(len(arrays))}


def load(weight, held, after=()):
    parts = 4
    step = weight.shape[0] // parts

    def kernel(src, *refs):
        dst, sem = refs[len(held) + len(after)], refs[-1]
        copies = []
        for i in range(parts):
            rows = pl.ds(i * step, step)
            copies.append(pltpu.make_async_copy(src.at[rows], dst.at[rows], sem.at[i]))
            copies[-1].start()
        for copy in copies:
            copy.wait()

    shapes, aliases = through(held, 1, 1)
    return pl.pallas_call(
        kernel,
        out_shape=[pltpu.VMEM(weight.shape, weight.dtype)] + shapes,
        in_specs=[ANYWHERE] + [IN_VMEM] * len(held) + [ANYWHERE] * len(after),
        out_specs=[IN_VMEM] * (1 + len(held)),
        scratch_shapes=[pltpu.SemaphoreType.DMA((parts,))],
        input_output_aliases=aliases,
        compiler_params=params(3),
        cost_estimate=cost(moved=weight.size * 2),
        name="load_weight",
    )(in_hbm(weight), *[in_vmem(a) for a in held], *after)


def join(own, near):
    own_rows, features = own[0].shape

    def kernel(*refs):
        for g in range(2):
            both = [refs[g][...].astype(F32), refs[2 + g][...].astype(F32)]
            rows = slice(2 * g * own_rows, 2 * (g + 1) * own_rows)
            refs[4][rows, :] = jnp.concatenate(both, axis=0).astype(BF16)

    return pl.pallas_call(
        kernel,
        out_shape=pltpu.VMEM((4 * own_rows, features), BF16),
        in_specs=[IN_VMEM] * 4,
        out_specs=IN_VMEM,
        compiler_params=params(3),
        name="join",
    )(*own, *near)


def unpack(blocks, held):
    n, w = len(blocks), len(held)
    rows, features = blocks[0].shape
    half = rows // 2

    def kernel(*refs):
        for b in range(n):
            for g in range(2):
                refs[n + w + g][b * half : (b + 1) * half, :] = refs[b][g * half : (g + 1) * half, :]

    shapes, aliases = through(held, n, 2)
    results = pl.pallas_call(
        kernel,
        out_shape=[pltpu.VMEM((n * half, features), BF16)] * 2 + shapes,
        in_specs=[IN_VMEM] * (n + w),
        out_specs=[IN_VMEM] * (2 + w),
        input_output_aliases=aliases,
        compiler_params=params(3),
        name="unpack",
    )(*blocks, *[in_vmem(a) for a in held])
    return results[0], results[1], results[2:]


def first_products(place, x, weights, used, offset, width, groups, transposed):
    total = x.shape[0]
    share = total // groups
    n, w = len(used), len(weights)

    def kernel(place_ref, x_ref, *refs):
        outs, acc = refs[w : w + groups], refs[-1]
        for g in range(n):
            weight = refs[used[g]]
            if transposed:
                acc[...] = contract_cols(x_ref[...], weight[offset : offset + width, :])
            else:
                acc[...] = jnp.dot(
                    x_ref[...], weight[:, offset : offset + width], preferred_element_type=F32
                )
            for j in range(groups):
                at = pl.multiple_of((place_ref[0] ^ j) * share, share)
                outs[j][g] = acc[pl.ds(at, share), :]

    results = pl.pallas_call(
        kernel,
        out_shape=[pltpu.VMEM((n, share, width), F32)] * groups
        + [pltpu.VMEM(a.shape, a.dtype) for a in weights],
        in_specs=[IN_SMEM] + [IN_VMEM] * (1 + w),
        out_specs=[IN_VMEM] * (groups + w),
        scratch_shapes=[pltpu.VMEM((total, width), F32)],
        input_output_aliases={2 + i: groups + i for i in range(w)},
        compiler_params=params(3),
        name="first_products",
    )(place, x, *[in_vmem(a) for a in weights])
    return results[:groups], results[groups:]


def core_sum(parts, weights):
    n, w = len(parts), len(weights)

    def kernel(*refs):
        total = refs[0][...]
        for ref in refs[1:n]:
            total = total + ref[...]
        refs[n + w][...] = total
        refs[n + w + 1][...] = total.astype(BF16)

    shape = parts[0].shape
    results = pl.pallas_call(
        kernel,
        out_shape=[pltpu.VMEM(shape, F32), pltpu.VMEM(shape, BF16)]
        + [pltpu.VMEM(a.shape, a.dtype) for a in weights],
        in_specs=[IN_VMEM] * (n + w),
        out_specs=[IN_VMEM] * (2 + w),
        input_output_aliases={n + i: 2 + i for i in range(w)},
        compiler_params=params(3),
        name="core_sum",
    )(*parts, *[in_vmem(a) for a in weights])
    return results[:2], results[2:]


def activations(gate_up, back, offset, width, weights):
    n, w = len(gate_up), len(weights)
    share = gate_up[0].shape[1]

    def kernel(*refs):
        gu, bk, out = refs[:n], refs[n : 2 * n], refs[2 * n + w]

        def added(group, g, cols):
            total = group[0][g, :, cols]
            for ref in group[1:]:
                total = total + ref[g, :, cols].astype(F32)
            return total

        gate_pre = added(gu, 0, slice(None))
        up_proj = added(gu, 1, slice(None))
        d_hidden = added(bk, 0, slice(offset, offset + width))
        sigmoid_gate = 1.0 / (1.0 + jnp.exp(-gate_pre))
        activated = gate_pre * sigmoid_gate
        out[0] = (activated * up_proj).astype(BF16)
        out[1] = (
            d_hidden * up_proj * sigmoid_gate * (1.0 + gate_pre * (1.0 - sigmoid_gate))
        ).astype(BF16)
        out[2] = (d_hidden * activated).astype(BF16)

    results = pl.pallas_call(
        kernel,
        out_shape=[pltpu.VMEM((3, share, width), BF16)]
        + [pltpu.VMEM(a.shape, a.dtype) for a in weights],
        in_specs=[IN_VMEM] * (2 * n + w),
        out_specs=[IN_VMEM] * (1 + w),
        input_output_aliases={2 * n + i: 1 + i for i in range(w)},
        compiler_params=params(3),
        name="activations",
    )(*gate_up, *back, *[in_vmem(a) for a in weights])
    return results[0], results[1:]


def second_products(place, shares, weights, offset, width, before, last, own_rows):
    groups = len(shares)
    share = shares[0].shape[1]
    total = share * groups
    features = weights[0].shape[0]
    blocks = total // own_rows

    def kernel(place_ref, *refs):
        share_refs = refs[:groups]
        gate_ref, up_ref, down_ref = refs[groups : groups + 3]
        before_refs = refs[groups + 3 : groups + 3 + len(before)]
        rest = refs[groups + 3 + len(before) :]
        laid = rest[0]
        for j in range(groups):
            at = pl.multiple_of((place_ref[0] ^ j) * share, share)
            laid[:, pl.ds(at, share), :] = share_refs[j][...]
        cols = slice(offset, offset + width)
        out = jnp.dot(laid[0], down_ref[cols, :], preferred_element_type=F32)
        back = contract_cols(laid[1], gate_ref[:, cols]) + contract_cols(laid[2], up_ref[:, cols])
        if before:
            out = out + before_refs[0][0]
            back = back + before_refs[0][1]
        if not last:
            rest[1][0] = out
            rest[1][1] = back
        else:
            keep, send = rest[1:3]
            for b in range(blocks):
                rows = slice(b * own_rows, (b + 1) * own_rows)
                both = jnp.concatenate([out[rows], back[rows]], axis=0)
                if b % 2:
                    send[b // 2] = both.astype(BF16)
                else:
                    keep[b // 2] = both

    if last:
        sums = [
            pltpu.VMEM((blocks // 2, 2 * own_rows, features), F32),
            pltpu.VMEM((blocks // 2, 2 * own_rows, features), BF16),
        ]
    else:
        sums = [pltpu.VMEM((2, total, features), F32)]
    kept = [] if last else [pltpu.VMEM(w.shape, w.dtype) for w in weights]
    results = pl.pallas_call(
        kernel,
        out_shape=[pltpu.VMEM((3, total, width), BF16)] + sums + kept,
        in_specs=[IN_SMEM] + [IN_VMEM] * (groups + 3 + len(before)),
        out_specs=[IN_VMEM] * (1 + len(sums) + len(kept)),
        input_output_aliases={1 + groups + g: 1 + len(sums) + g for g in range(len(kept))},
        compiler_params=params(3),
        name="second_products",
    )(place, *shares, *[in_vmem(w) for w in weights], *before)
    return results[0], results[1 : 1 + len(sums)], results[1 + len(sums) :]


def row_sum(keep, near, after):
    n = keep.shape[0]

    def kernel(keep_ref, near_ref, *refs):
        refs = refs[len(after) :]
        refs[0][...] = keep_ref[0] + near_ref[0].astype(F32)
        for j in range(1, n):
            refs[j][...] = (keep_ref[j] + near_ref[j].astype(F32)).astype(BF16)

    shape = keep.shape[1:]
    results = pl.pallas_call(
        kernel,
        out_shape=[pltpu.VMEM(shape, F32)] + [pltpu.VMEM(shape, BF16)] * (n - 1),
        in_specs=[IN_VMEM] * 2 + [ANYWHERE] * len(after),
        out_specs=[IN_VMEM] * n,
        compiler_params=params(3),
        name="row_sum",
    )(keep, near, *[in_hbm(a) for a in after])
    return results[0], results[1:]


def last_sum(total, far, after):
    n = len(far)
    both, features = total.shape

    def kernel(total_ref, *refs):
        outs = refs[n + len(after) :]
        value = total_ref[...]
        for ref in refs[:n]:
            value = value + ref[...].astype(F32)
        outs[0][...] = value[: both // 2].astype(BF16)
        outs[1][...] = value[both // 2 :].astype(BF16)

    return pl.pallas_call(
        kernel,
        out_shape=[jax.ShapeDtypeStruct((both // 2, features), BF16)] * 2,
        in_specs=[IN_VMEM] * (1 + n) + [ANYWHERE] * len(after),
        out_specs=[IN_VMEM] * 2,
        compiler_params=params(3),
        name="last_sum",
    )(total, *far, *[in_hbm(a) for a in after])


def outer_rows(x, laid, which, offsets, after=()):
    features = x.shape[1]
    widths = [a.shape[2] for a in laid]
    hidden = sum(widths)
    tile = tile_of(features, 256)
    slots = min(4, features // tile)
    n = len(laid)

    def kernel(x_ref, *refs):
        laid_refs = refs[:n]
        out, stage, sems = refs[n + len(after) :]

        def sent(slot, at):
            return pltpu.make_async_copy(stage.at[slot], out.at[pl.ds(at, tile)], sems.at[slot])

        @pl.loop(0, features // tile)
        def _(i):
            slot = lax.rem(i, slots)

            @pl.when(i >= slots)
            def _():
                sent(slot, 0).wait()

            at = pl.multiple_of(i * tile, tile)
            left = x_ref[:, pl.ds(at, tile)]
            for c in range(n):
                step = tile_of(widths[c], 512)
                for s in range(0, widths[c], step):
                    stage[slot, :, offsets[c] + s : offsets[c] + s + step] = contract_rows(
                        left, laid_refs[c][which, :, s : s + step]
                    ).astype(BF16)
            sent(slot, at).start()

        for slot in range(slots):
            sent(slot, 0).wait()

    return pl.pallas_call(
        kernel,
        out_shape=jax.ShapeDtypeStruct((features, hidden), BF16),
        in_specs=[IN_VMEM] * (1 + n) + [ANYWHERE] * len(after),
        out_specs=ANYWHERE,
        scratch_shapes=[
            pltpu.VMEM((slots, tile, hidden), BF16),
            pltpu.SemaphoreType.DMA((slots,)),
        ],
        compiler_params=params(12),
        cost_estimate=cost(moved=features * hidden * 2),
        name="outer_rows",
    )(x, *laid, *after)


def outer_down(grad, laid, offsets, after=()):
    features = grad.shape[1]
    widths = [a.shape[2] for a in laid]
    hidden = sum(widths)
    tiles = [tile_of(w, 256) for w in widths]
    tile = min(tiles)
    n = len(laid)
    slots = min(4, min(w // tile for w in widths))
    step = tile_of(features, 512)

    def kernel(grad_ref, *refs):
        laid_refs = refs[:n]
        out, stage, sems = refs[n + len(after) :]

        def sent(slot, at):
            return pltpu.make_async_copy(stage.at[slot], out.at[pl.ds(at, tile)], sems.at[slot])

        for c in range(n):

            @pl.loop(0, widths[c] // tile)
            def _(i):
                slot = lax.rem(i + offsets[c] // tile, slots)

                if c:
                    sent(slot, 0).wait()
                else:

                    @pl.when(i >= slots)
                    def _():
                        sent(slot, 0).wait()

                at = pl.multiple_of(i * tile, tile)
                left = laid_refs[c][0, :, pl.ds(at, tile)]
                for s in range(0, features, step):
                    stage[slot, :, s : s + step] = contract_rows(
                        left, grad_ref[:, s : s + step]
                    ).astype(BF16)
                sent(slot, offsets[c] + at).start()

        for slot in range(slots):
            sent(slot, 0).wait()

    return pl.pallas_call(
        kernel,
        out_shape=jax.ShapeDtypeStruct((hidden, features), BF16),
        in_specs=[IN_VMEM] * (1 + n) + [ANYWHERE] * len(after),
        out_specs=ANYWHERE,
        scratch_shapes=[
            pltpu.VMEM((slots, tile, features), BF16),
            pltpu.SemaphoreType.DMA((slots,)),
        ],
        compiler_params=params(12),
        cost_estimate=cost(moved=features * hidden * 2),
        name="outer_down",
    )(grad, *laid, *after)


def per_device(tokens, grad_out, gate_weight, up_weight, down_weight):
    own_rows = tokens.shape[0]
    rows, cores, chips = (lax.axis_size(a) for a in ("row", "depth", "col"))
    hidden = gate_weight.shape[1]
    place = lax.axis_index("depth").astype(jnp.int32).reshape(1)

    own = [tokens, grad_out]
    near = [swap(a, "row", 1) for a in own]
    (down,) = load(down_weight, [])
    pair = join(own, near)
    blocks = [pair] + [swap(pair, "row", k) for k in range(2, rows, 2)]
    gate, down = load(gate_weight, [down], (pair,))
    up, gate, down = load(up_weight, [gate, down])
    tok_all, grad_all, weights = unpack(blocks, [gate, up, down])

    def over_cores(parts):
        return [parts[0]] + [swap(parts[j], "depth", j) for j in range(1, cores)]

    def over_chips(total, rounded):
        return [total] + [swap(rounded, "col", k) for k in range(1, chips)]

    tiles = hidden // 128
    cut = 128 * (tiles // 2)
    spans = [(0, cut), (cut, hidden - cut)]
    offsets = [s[0] for s in spans]

    part_back, weights = first_products(place, grad_all, weights, [2], 0, hidden, cores, True)
    part_back = over_cores(part_back)
    parts = []
    for c, (offset, width) in enumerate(spans):
        part, weights = first_products(
            place, tok_all, weights, [0, 1], offset, width, cores, False
        )
        parts.append(over_cores(part))
        if not c:
            sums, weights = core_sum(part_back, weights)
            back = over_chips(*sums)
    gate_up = []
    for part in parts:
        sums, weights = core_sum(part, weights)
        gate_up.append(over_chips(*sums))

    laid, before = [], []
    for c, (offset, width) in enumerate(spans):
        acts, weights = activations(gate_up[c], back, offset, width, weights)
        shares = [acts] + [swap(acts, "depth", j) for j in range(1, cores)]
        here, before, weights = second_products(
            place, shares, weights, offset, width, before, c == len(spans) - 1, own_rows
        )
        laid.append(here)

    keep, send = before
    near = swap(send, "row", 1)
    grad_down = outer_down(grad_all, laid, offsets, (send,))
    total, rounded = row_sum(keep, near, (grad_down,))
    far = [swap(rounded[j - 1], "row", 2 * j) for j in range(1, rows // 2)]
    grad_gate = outer_rows(tok_all, laid, 1, offsets, (total,))
    grad_up = outer_rows(tok_all, laid, 2, offsets, (in_hbm(grad_gate),))
    layer_out, grad_tokens = last_sum(total, far, (grad_up,))
    return layer_out, grad_tokens, grad_gate, grad_up, grad_down


def solution(mesh):
    acts = P("row", ("col", "depth"))
    wide = P(("col", "depth"), "row")
    return jax.shard_map(
        per_device,
        mesh=mesh,
        in_specs=(acts, acts, wide, wide, acts),
        out_specs=(acts, acts, wide, wide, acts),
        check_vma=False,
    )
```

time: 333 us -> 96.6 us (0.29)
  local copies, waits for them, and re-layouts: 81.3 us -> 1.52 us
  blocking collectives: 79.6 us -> 0 us
  matrix products: 68.7 us -> 0 us
  waiting for transfers between devices: 84.3 us -> 17.5 us
  Pallas kernels: 0 us -> 59.5 us
  starting transfers between devices: 0.16 us -> 17 us
  between operations: 13.8 us -> 0.83 us
  other arithmetic: 4.22 us -> 0 us
    reduce_scatter x4 -> x0, waiting for transfers between devices: 84.2 us -> none  [the longest x2 53.4 us: feature_sums(): lax.psum_scatter(term_fn(jnp.int32(0), own_rows * lax.axis_size('row')),...]
    all_gather x4 -> x0, blocking collectives: 79.6 us -> none  [the longest x1 32.7 us: per_device(): lax.all_gather(grad_out, 'row', axis=0, tiled=True)]
    dot_general x6 -> x0, matrix products: 68.7 us -> none  [the longest x2 25.7 us: contract_cols(): lax.dot_general(left, right, (((1,), (1,)), ((), ())), preferred_element_...]
    pallas_call x0 -> x20, Pallas kernels: none -> 59.5 us  [the longest x3 15.8 us: load(): pl.pallas_call(kernel, out_shape=[pltpu.VMEM(weight.shape, weight.dtype)]...]
    unnamed x13 -> x4, local copies, waits for them, and re-layouts: 52.6 us -> 1.52 us
    slice x1 -> x0, local copies, waits for them, and re-layouts: 22.5 us -> none  [per_device(): grad_both[:, width_ff:]]
    ppermute x0 -> x17, waiting for transfers between devices: none -> 17.5 us  [swap(): return lax.ppermute(array, axis, [(i, i ^ distance) for i in range(size)])]
    ppermute x0 -> x17, starting transfers between devices: none -> 17 us  [swap(): return lax.ppermute(array, axis, [(i, i ^ distance) for i in range(size)])]
  transfers between devices with their start and end apart: 4 -> 17, of which waited for: 2 -> 8; matrix products, arithmetic and copies ran while one was open for 40% -> 0% of each run, Pallas kernels for 0% -> 50%
where the time goes in v1:
time: 96.6 us; the launch traced here: 96.3 us
  Pallas kernels  59.5 us (62%)
  waiting for transfers between devices  17.5 us (18%)
  starting transfers between devices  17 us (18%)
  local copies, waits for them, and re-layouts  1.52 us (2%)
    ppermute x17, waiting for transfers between devices, swap(): return lax.ppermute(array, axis, [(i, i ^ distance) for i in range(size)])  17.5 us
    ppermute x17, starting transfers between devices, swap(): return lax.ppermute(array, axis, [(i, i ^ distance) for i in range(size)])  17 us
    pallas_call x3, Pallas kernels, load(): pl.pallas_call(kernel, out_shape=[pltpu.VMEM(weight.shape, weight.dtype)]...  15.8 us
    pallas_call x2, Pallas kernels, outer_rows(): pl.pallas_call(kernel, out_shape=jax.ShapeDtypeStruct((features, hidden),...  13.2 us
    pallas_call x2, Pallas kernels, second_products(): pl.pallas_call(kernel, out_shape=[pltpu.VMEM((3, total, width), BF16)] +...  11.8 us
    pallas_call x3, Pallas kernels, first_products(): pl.pallas_call(kernel, out_shape=[pltpu.VMEM((n, share, width), F32)] * g...  9.95 us
    pallas_call x1, Pallas kernels, outer_down(): pl.pallas_call(kernel, out_shape=jax.ShapeDtypeStruct((hidden, features),...  7.43 us
  transfers between devices with their start and end apart: 17, of which 8 were waited for; matrix products, arithmetic and copies ran while one was open for 0% of the time, Pallas kernels for 50%

profile of v1, /device:TPU:0, one launch (start us, length us, event | category | flops | bytes accessed | tf_op | source)
XLA Modules:
  0.0 96.3 jit_solution(14146603144666702463)
XLA Ops:
  0.6 3.0 %collective-permute-start = (bf16[8,2048]{1,0:T(8,128)(2,1)}, bf16[8,2048]{1,0:T(8,128)(2,1)S(1)}, u32[]{:S(2)}, u32[]{:S(2)}) collective-permute-start(bf16[8,2048]{1,0:T(8,128)(2,1)} %refs_0_.1), channel_id=1, source_target_pairs={{0,4},{4,0},{8,12},{12,8},{16,20},{20,16},{24,28},{28,24},{1,5},{5... | collective-permute-start | bytes 98312 | tf_op jit(solution)/shard_map/ppermute | solution.py:36
  3.6 0.1 collective-permute-start.1
  3.7 2.0 %collective-permute-done.refs_2_ = bf16[8,2048]{1,0:T(8,128)(2,1)S(1)} collective-permute-done((bf16[8,2048]{1,0:T(8,128)(2,1)}, bf16[8,2048]{1,0:T(8,128)(2,1)S(1)}, u32[]{:S(2)}, u32[]{:S(2)}) %collective-permute-start) | collective-permute-done | bytes 32800 | tf_op jit(solution)/shard_map/ppermute | solution.py:36
  5.7 2.0 %collective-permute-done.1.refs_3_ = bf16[8,2048]{1,0:T(8,128)(2,1)S(1)} collective-permute-done((bf16[8,2048]{1,0:T(8,128)(2,1)}, bf16[8,2048]{1,0:T(8,128)(2,1)S(1)}, u32[]{:S(2)}, u32[]{:S(2)}) %collective-permute-start.1) | collective-permute-done | bytes 32800 | tf_op jit(solution)/shard_map/ppermute | solution.py:36
  7.8 0.0 copy-start
  7.8 0.8 copy-done
  8.5 0.0 copy-start.1
  8.5 0.8 copy-done.1
  9.3 3.7 %collective-permute-start.4 = (bf16[32,2048]{1,0:T(8,128)(2,1)S(1)}, bf16[32,2048]{1,0:T(8,128)(2,1)S(1)}, u32[]{:S(2)}, u32[]{:S(2)}) collective-permute-start(bf16[32,2048]{1,0:T(8,128)(2,1)S(1)} %join.1.refs_1_.refs_0_), channel_id=1, source_target_pairs={{0,24},{4,28},{8,16},{12,20},{16,8},{20,12},{24,0},{28,4},{1,25},{... | collective-permute-start | bytes 393224 | tf_op jit(solution)/shard_map/ppermute | solution.py:36
  13.0 0.0 collective-permute-start.3
  13.0 0.8 collective-permute-start.2
  13.7 5.3 %load_weight.3.refs_0_ = bf16[3584,2048]{1,0:T(8,128)(2,1)S(1)} custom-call(bf16[3584,2048]{1,0:T(8,128)(2,1)} %src.3), custom_call_target="tpu_custom_call" | custom-call | bytes 14680064 | tf_op jit(solution)/shard_map/load_weight/pallas_call | solution.py:75
  19.0 5.3 %load_weight.4 = (bf16[2048,3584]{1,0:T(8,128)(2,1)S(1)}, bf16[3584,2048]{1,0:T(8,128)(2,1)S(1)}) custom-call(bf16[2048,3584]{1,0:T(8,128)(2,1)} %src.4, bf16[3584,2048]{1,0:T(8,128)(2,1)S(1)} %load_weight.3.refs_0_, bf16[32,2048]{1,0:T(8,128)(2,1)S(1)} %join.1.refs_1_.refs_0_), custom_call_target="tpu_custom_call", output_to_operand_aliasing={{1}: (1, {})} | custom-call | bytes 14680064 | tf_op jit(solution)/shard_map/load_weight/pallas_call | solution.py:75
  24.3 5.3 %load_weight.5 = (bf16[2048,3584]{1,0:T(8,128)(2,1)S(1)}, bf16[2048,3584]{1,0:T(8,128)(2,1)S(1)}, bf16[3584,2048]{1,0:T(8,128)(2,1)S(1)}) custom-call(bf16[2048,3584]{1,0:T(8,128)(2,1)} %src.5, bf16[2048,3584]{1,0:T(8,128)(2,1)S(1)} %get-tuple-element.67.refs_0_, ...), custom_call_target="tpu_custom_call", output_to_operand_aliasing={{1}: (1, {}), {2}: (2, {})} | custom-call | bytes 14680064 | tf_op jit(solution)/shard_map/load_weight/pallas_call | solution.py:75
  29.6 0.0 collective-permute-done.4.refs_3_
  29.6 0.0 collective-permute-done.3.refs_2_
  29.6 0.0 collective-permute-done.2.refs_1_
  29.7 4.6 %first_products.3 = (f32[1,32,3584]{2,1,0:T(8,128)S(1)}, f32[1,32,3584]{2,1,0:T(8,128)S(1)}, bf16[2048,3584]{1,0:T(8,128)(2,1)S(1)}, bf16[2048,3584]{1,0:T(8,128)(2,1)S(1)}, bf16[3584,2048]{1,0:T(8,128)(2,1)S(1)}) custom-call(s32[1]{0:T(128)} %bitcast.place_ref, ...), custom_call_target="tpu_custom_call", output_to_operand_aliasing={{2}: (2, {}), {3}: (3, {}), {4}: (4, {})} | custom-call | tf_op jit(solution)/shard_map/first_products/pallas_call | solution.py:149
  34.3 0.1 collective-permute-start.5
  34.4 2.7 %first_products.4 = (f32[2,32,1792]{2,1,0:T(8,128)S(1)}, f32[2,32,1792]{2,1,0:T(8,128)S(1)}, bf16[2048,3584]{1,0:T(8,128)(2,1)S(1)}, bf16[2048,3584]{1,0:T(8,128)(2,1)S(1)}, bf16[3584,2048]{1,0:T(8,128)(2,1)S(1)}) custom-call(s32[1]{0:T(128)} %bitcast.place_ref, ...), custom_call_target="tpu_custom_call", output_to_operand_aliasing={{2}: (2, {}), {3}: (3, {}), {4}: (4, {})} | custom-call | tf_op jit(solution)/shard_map/first_products/pallas_call | solution.py:149
  37.1 0.6 collective-permute-start.7
  37.6 0.0 collective-permute-done.5.refs_1_
  37.6 0.1 core_sum.3
  37.7 2.7 %first_products.5 = (f32[2,32,1792]{2,1,0:T(8,128)S(1)}, f32[2,32,1792]{2,1,0:T(8,128)S(1)}, bf16[2048,3584]{1,0:T(8,128)(2,1)S(1)}, bf16[2048,3584]{1,0:T(8,128)(2,1)S(1)}, bf16[3584,2048]{1,0:T(8,128)(2,1)S(1)}) custom-call(s32[1]{0:T(128)} %bitcast.place_ref, ...), custom_call_target="tpu_custom_call", output_to_operand_aliasing={{2}: (2, {}), {3}: (3, {}), {4}: (4, {})} | custom-call | tf_op jit(solution)/shard_map/first_products/pallas_call | solution.py:149
  40.4 0.1 collective-permute-start.6
  40.5 1.6 %collective-permute-start.9 = (bf16[1,32,3584]{2,1,0:T(8,128)(2,1)S(1)}, bf16[1,32,3584]{2,1,0:T(8,128)(2,1)S(1)}, u32[]{:S(2)}, u32[]{:S(2)}) collective-permute-start(bf16[1,32,3584]{2,1,0:T(8,128)(2,1)S(1)} %get-tuple-element.101), channel_id=1, source_target_pairs={{0,2},{2,0},{1,3},{3,1},{4,6},{6,4},{5,7},{7,5},{8,10},{10,8},{9,1... | collective-permute-start | bytes 688136 | tf_op jit(solution)/shard_map/ppermute | solution.py:36
  42.0 0.0 collective-permute-done.7.refs_1_
  42.0 0.1 core_sum.4
  42.1 0.6 collective-permute-start.10
  42.7 0.0 collective-permute-done.6.refs_1_
  42.7 0.1 core_sum.5
  42.7 6.2 %collective-permute-done.9.refs_3_ = bf16[1,32,3584]{2,1,0:T(8,128)(2,1)S(1)} collective-permute-done((bf16[1,32,3584]{2,1,0:T(8,128)(2,1)S(1)}, bf16[1,32,3584]{2,1,0:T(8,128)(2,1)S(1)}, u32[]{:S(2)}, u32[]{:S(2)}) %collective-permute-start.9) | collective-permute-done | bytes 229408 | tf_op jit(solution)/shard_map/ppermute | solution.py:36
  48.9 4.5 %collective-permute-done.10.refs_1_ = bf16[2,32,1792]{2,1,0:T(8,128)(2,1)S(1)} collective-permute-done((bf16[2,32,1792]{2,1,0:T(8,128)(2,1)S(1)}, bf16[2,32,1792]{2,1,0:T(8,128)(2,1)S(1)}, u32[]{:S(2)}, u32[]{:S(2)}) %collective-permute-start.10) | collective-permute-done | bytes 229408 | tf_op jit(solution)/shard_map/ppermute | solution.py:36
  53.4 0.2 activations.2
  53.6 0.1 collective-permute-start.11
  53.6 1.6 %collective-permute-start.8 = (bf16[2,32,1792]{2,1,0:T(8,128)(2,1)S(1)}, bf16[2,32,1792]{2,1,0:T(8,128)(2,1)S(1)}, u32[]{:S(2)}, u32[]{:S(2)}) collective-permute-start(bf16[2,32,1792]{2,1,0:T(8,128)(2,1)S(1)} %get-tuple-element.99), channel_id=1, source_target_pairs={{0,2},{2,0},{1,3},{3,1},{4,6},{6,4},{5,7},{7,5},{8,10},{10,8},{9,1... | collective-permute-start | bytes 688136 | tf_op jit(solution)/shard_map/ppermute | solution.py:36
  55.2 0.1 collective-permute-done.11.refs_1_
  55.3 5.8 %second_products.2 = (bf16[3,64,1792]{2,1,0:T(8,128)(2,1)S(1)}, f32[2,64,2048]{2,1,0:T(8,128)S(1)}, bf16[2048,3584]{1,0:T(8,128)(2,1)S(1)}, bf16[2048,3584]{1,0:T(8,128)(2,1)S(1)}, bf16[3584,2048]{1,0:T(8,128)(2,1)S(1)}) custom-call(s32[1]{0:T(128)} %bitcast.place_ref, ...), custom_call_target="tpu_custom_call", output_to_operand_aliasing={{2}: (3, {}), {3}: (4, {}), {4}: (5, {})} | custom-call | tf_op jit(solution)/shard_map/second_products/pallas_call | solution.py:267
  61.1 0.5 collective-permute-done.8.refs_1_
  61.7 0.2 activations.3
  61.8 0.1 collective-permute-start.12
  61.9 1.6 %collective-permute-done.12.refs_1_ = bf16[3,32,1792]{2,1,0:T(8,128)(2,1)S(1)} collective-permute-done((bf16[3,32,1792]{2,1,0:T(8,128)(2,1)S(1)}, bf16[3,32,1792]{2,1,0:T(8,128)(2,1)S(1)}, u32[]{:S(2)}, u32[]{:S(2)}) %collective-permute-start.12) | collective-permute-done | bytes 344096 | tf_op jit(solution)/shard_map/ppermute | solution.py:36
  63.6 6.0 %second_products.3 = (bf16[3,64,1792]{2,1,0:T(8,128)(2,1)S(1)}, f32[4,16,2048]{2,1,0:T(8,128)S(1)}, bf16[4,16,2048]{2,1,0:T(8,128)(2,1)S(1)}) custom-call(s32[1]{0:T(128)} %bitcast.place_ref, bf16[3,32,1792]{2,1,0:T(8,128)(2,1)S(1)} %get-tuple-element.114.refs_0_, bf16[3,32,1792]{2,1,0:T(8,128)(2,1)S(1)} %collective-permute-done.12.refs_1_, ...), custom_call_target="tpu_custom_call" | custom-call | tf_op jit(solution)/shard_map/second_products/pallas_call | solution.py:267
  69.5 0.5 collective-permute-start.13
  70.0 7.4 %outer_down.1.refs_0_ = bf16[3584,2048]{1,0:T(8,128)(2,1)} custom-call(bf16[64,2048]{1,0:T(8,128)(2,1)S(1)} %get-tuple-element.73.x_ref.grad_ref, bf16[3,64,1792]{2,1,0:T(8,128)(2,1)S(1)} %get-tuple-element.121.refs_0_, bf16[3,64,1792]{2,1,0:T(8,128)(2,1)S(1)} %get-tuple-element.122.refs_1_, bf16[4,16,2048]{2,1,0:T(8,128)(2,1)S(1)} %get-tuple-element.120.refs_2_), custom_call_target="tpu_custom_call" | custom-call | bytes 14680064 | tf_op jit(solution)/shard_map/outer_down/pallas_call | solution.py:415
  77.4 0.5 collective-permute-done.13.near_ref
  77.9 0.1 row_sum.1
  78.0 1.3 %collective-permute-start.14 = (bf16[16,2048]{1,0:T(8,128)(2,1)S(1)}, bf16[16,2048]{1,0:T(8,128)(2,1)S(1)}, u32[]{:S(2)}, u32[]{:S(2)}) collective-permute-start(bf16[16,2048]{1,0:T(8,128)(2,1)S(1)} %get-tuple-element.124), channel_id=1, source_target_pairs={{0,8},{4,12},{8,0},{12,4},{16,24},{20,28},{24,16},{28,20},{1,9},{5... | collective-permute-start | bytes 196616 | tf_op jit(solution)/shard_map/ppermute | solution.py:36
  79.3 2.9 %collective-permute-start.15 = (bf16[16,2048]{1,0:T(8,128)(2,1)S(1)}, bf16[16,2048]{1,0:T(8,128)(2,1)S(1)}, u32[]{:S(2)}, u32[]{:S(2)}) collective-permute-start(bf16[16,2048]{1,0:T(8,128)(2,1)S(1)} %get-tuple-element.125), channel_id=1, source_target_pairs={{0,16},{4,20},{8,24},{12,28},{16,0},{20,4},{24,8},{28,12},{1,17},{... | collective-permute-start | bytes 196616 | tf_op jit(solution)/shard_map/ppermute | solution.py:36
  82.2 0.2 collective-permute-start.16
  82.4 6.6 %outer_rows.2.refs_2_ = bf16[2048,3584]{1,0:T(8,128)(2,1)} custom-call(bf16[64,2048]{1,0:T(8,128)(2,1)S(1)} %get-tuple-element.72.x_ref, bf16[3,64,1792]{2,1,0:T(8,128)(2,1)S(1)} %get-tuple-element.121.refs_0_, bf16[3,64,1792]{2,1,0:T(8,128)(2,1)S(1)} %get-tuple-element.122.refs_1_, f32[16,2048]{1,0:T(8,128)S(1)} %get-tuple-element.123.refs_2_.total_ref), custom_call_target="tpu_custom_call" | custom-call | bytes 14680064 | tf_op jit(solution)/shard_map/outer_rows/pallas_call | solution.py:358
  89.0 6.6 %outer_rows.3.refs_3_ = bf16[2048,3584]{1,0:T(8,128)(2,1)} custom-call(bf16[64,2048]{1,0:T(8,128)(2,1)S(1)} %get-tuple-element.72.x_ref, bf16[3,64,1792]{2,1,0:T(8,128)(2,1)S(1)} %get-tuple-element.121.refs_0_, bf16[3,64,1792]{2,1,0:T(8,128)(2,1)S(1)} %get-tuple-element.122.refs_1_, bf16[2048,3584]{1,0:T(8,128)(2,1)} %outer_rows.2.refs_2_), custom_call_target="tpu_custom_call" | custom-call | bytes 14680064 | tf_op jit(solution)/shard_map/outer_rows/pallas_call | solution.py:358
  95.6 0.0 collective-permute-done.14.refs_0_
  95.6 0.0 collective-permute-done.15.refs_1_
  95.7 0.0 collective-permute-done.16.refs_2_
  95.7 0.6 last_sum.1
  (2 shorter events, 0.0 us)
Async XLA Ops:
  0.6 5.1 %collective-permute-start = (bf16[8,2048]{1,0:T(8,128)(2,1)}, bf16[8,2048]{1,0:T(8,128)(2,1)S(1)}, u32[]{:S(2)}, u32[]{:S(2)}) collective-permute-start(bf16[8,2048]{1,0:T(8,128)(2,1)} %refs_0_.1), channel_id=1, source_target_pairs={{0,4},{4,0},{8,12},{12,8},{16,20},{20,16},{24,28},{28,24},{1,5},{5... | collective-permute-start | bytes 98312 | tf_op jit(solution)/shard_map/ppermute | solution.py:36
  3.6 4.1 %collective-permute-start.1 = (bf16[8,2048]{1,0:T(8,128)(2,1)}, bf16[8,2048]{1,0:T(8,128)(2,1)S(1)}, u32[]{:S(2)}, u32[]{:S(2)}) collective-permute-start(bf16[8,2048]{1,0:T(8,128)(2,1)} %refs_1_.1), channel_id=1, source_target_pairs={{0,4},{4,0},{8,12},{12,8},{16,20},{20,16},{24,28},{28,24},{1,5},{5... | collective-permute-start | bytes 98312 | tf_op jit(solution)/shard_map/ppermute | solution.py:36
  7.8 0.8 copy-start
  8.5 0.8 copy-start.1
  9.3 20.3 %collective-permute-start.4 = (bf16[32,2048]{1,0:T(8,128)(2,1)S(1)}, bf16[32,2048]{1,0:T(8,128)(2,1)S(1)}, u32[]{:S(2)}, u32[]{:S(2)}) collective-permute-start(bf16[32,2048]{1,0:T(8,128)(2,1)S(1)} %join.1.refs_1_.refs_0_), channel_id=1, source_target_pairs={{0,24},{4,28},{8,16},{12,20},{16,8},{20,12},{24,0},{28,4},{1,25},{... | collective-permute-start | bytes 393224 | tf_op jit(solution)/shard_map/ppermute | solution.py:36
  13.0 16.7 %collective-permute-start.3 = (bf16[32,2048]{1,0:T(8,128)(2,1)S(1)}, bf16[32,2048]{1,0:T(8,128)(2,1)S(1)}, u32[]{:S(2)}, u32[]{:S(2)}) collective-permute-start(bf16[32,2048]{1,0:T(8,128)(2,1)S(1)} %join.1.refs_1_.refs_0_), channel_id=1, source_target_pairs={{0,16},{4,20},{8,24},{12,28},{16,0},{20,4},{24,8},{28,12},{1,17},{... | collective-permute-start | bytes 393224 | tf_op jit(solution)/shard_map/ppermute | solution.py:36
  13.0 16.7 %collective-permute-start.2 = (bf16[32,2048]{1,0:T(8,128)(2,1)S(1)}, bf16[32,2048]{1,0:T(8,128)(2,1)S(1)}, u32[]{:S(2)}, u32[]{:S(2)}) collective-permute-start(bf16[32,2048]{1,0:T(8,128)(2,1)S(1)} %join.1.refs_1_.refs_0_), channel_id=1, source_target_pairs={{0,8},{4,12},{8,0},{12,4},{16,24},{20,28},{24,16},{28,20},{1,9},{5... | collective-permute-start | bytes 393224 | tf_op jit(solution)/shard_map/ppermute | solution.py:36
  34.3 3.3 %collective-permute-start.5 = (f32[1,32,3584]{2,1,0:T(8,128)S(1)}, f32[1,32,3584]{2,1,0:T(8,128)S(1)}, u32[]{:S(2)}, u32[]{:S(2)}) collective-permute-start(f32[1,32,3584]{2,1,0:T(8,128)S(1)} %get-tuple-element.78), channel_id=1, source_target_pairs={{0,1},{1,0},{2,3},{3,2},{4,5},{5,4},{6,7},{7,6},{8,9},{9,8},{10,11... | collective-permute-start | bytes 1376264 | tf_op jit(solution)/shard_map/ppermute | solution.py:36
  37.1 5.0 %collective-permute-start.7 = (f32[2,32,1792]{2,1,0:T(8,128)S(1)}, f32[2,32,1792]{2,1,0:T(8,128)S(1)}, u32[]{:S(2)}, u32[]{:S(2)}) collective-permute-start(f32[2,32,1792]{2,1,0:T(8,128)S(1)} %get-tuple-element.91), channel_id=1, source_target_pairs={{0,1},{1,0},{2,3},{3,2},{4,5},{5,4},{6,7},{7,6},{8,9},{9,8},{10,11... | collective-permute-start | bytes 1376264 | tf_op jit(solution)/shard_map/ppermute | solution.py:36
  40.4 2.3 %collective-permute-start.6 = (f32[2,32,1792]{2,1,0:T(8,128)S(1)}, f32[2,32,1792]{2,1,0:T(8,128)S(1)}, u32[]{:S(2)}, u32[]{:S(2)}) collective-permute-start(f32[2,32,1792]{2,1,0:T(8,128)S(1)} %get-tuple-element.89), channel_id=1, source_target_pairs={{0,1},{1,0},{2,3},{3,2},{4,5},{5,4},{6,7},{7,6},{8,9},{9,8},{10,11... | collective-permute-start | bytes 1376264 | tf_op jit(solution)/shard_map/ppermute | solution.py:36
  40.5 8.5 %collective-permute-start.9 = (bf16[1,32,3584]{2,1,0:T(8,128)(2,1)S(1)}, bf16[1,32,3584]{2,1,0:T(8,128)(2,1)S(1)}, u32[]{:S(2)}, u32[]{:S(2)}) collective-permute-start(bf16[1,32,3584]{2,1,0:T(8,128)(2,1)S(1)} %get-tuple-element.101), channel_id=1, source_target_pairs={{0,2},{2,0},{1,3},{3,1},{4,6},{6,4},{5,7},{7,5},{8,10},{10,8},{9,1... | collective-permute-start | bytes 688136 | tf_op jit(solution)/shard_map/ppermute | solution.py:36
  42.1 11.3 %collective-permute-start.10 = (bf16[2,32,1792]{2,1,0:T(8,128)(2,1)S(1)}, bf16[2,32,1792]{2,1,0:T(8,128)(2,1)S(1)}, u32[]{:S(2)}, u32[]{:S(2)}) collective-permute-start(bf16[2,32,1792]{2,1,0:T(8,128)(2,1)S(1)} %get-tuple-element.103), channel_id=1, source_target_pairs={{0,2},{2,0},{1,3},{3,1},{4,6},{6,4},{5,7},{7,5},{8,10},{10,8},{9,1... | collective-permute-start | bytes 688136 | tf_op jit(solution)/shard_map/ppermute | solution.py:36
  53.6 1.7 %collective-permute-start.11 = (bf16[3,32,1792]{2,1,0:T(8,128)(2,1)S(1)}, bf16[3,32,1792]{2,1,0:T(8,128)(2,1)S(1)}, u32[]{:S(2)}, u32[]{:S(2)}) collective-permute-start(bf16[3,32,1792]{2,1,0:T(8,128)(2,1)S(1)} %get-tuple-element.107.refs_0_), channel_id=1, source_target_pairs={{0,1},{1,0},{2,3},{3,2},{4,5},{5,4},{6,7},{7,6},{8,9},{9,8},{10,11... | collective-permute-start | bytes 1032200 | tf_op jit(solution)/shard_map/ppermute | solution.py:36
  53.6 8.0 %collective-permute-start.8 = (bf16[2,32,1792]{2,1,0:T(8,128)(2,1)S(1)}, bf16[2,32,1792]{2,1,0:T(8,128)(2,1)S(1)}, u32[]{:S(2)}, u32[]{:S(2)}) collective-permute-start(bf16[2,32,1792]{2,1,0:T(8,128)(2,1)S(1)} %get-tuple-element.99), channel_id=1, source_target_pairs={{0,2},{2,0},{1,3},{3,1},{4,6},{6,4},{5,7},{7,5},{8,10},{10,8},{9,1... | collective-permute-start | bytes 688136 | tf_op jit(solution)/shard_map/ppermute | solution.py:36
  61.8 1.7 %collective-permute-start.12 = (bf16[3,32,1792]{2,1,0:T(8,128)(2,1)S(1)}, bf16[3,32,1792]{2,1,0:T(8,128)(2,1)S(1)}, u32[]{:S(2)}, u32[]{:S(2)}) collective-permute-start(bf16[3,32,1792]{2,1,0:T(8,128)(2,1)S(1)} %get-tuple-element.114.refs_0_), channel_id=1, source_target_pairs={{0,1},{1,0},{2,3},{3,2},{4,5},{5,4},{6,7},{7,6},{8,9},{9,8},{10,11... | collective-permute-start | bytes 1032200 | tf_op jit(solution)/shard_map/ppermute | solution.py:36
  69.5 8.4 %collective-permute-start.13 = (bf16[4,16,2048]{2,1,0:T(8,128)(2,1)S(1)}, bf16[4,16,2048]{2,1,0:T(8,128)(2,1)S(1)}, u32[]{:S(2)}, u32[]{:S(2)}) collective-permute-start(bf16[4,16,2048]{2,1,0:T(8,128)(2,1)S(1)} %get-tuple-element.120.refs_2_), channel_id=1, source_target_pairs={{0,4},{4,0},{8,12},{12,8},{16,20},{20,16},{24,28},{28,24},{1,5},{5... | collective-permute-start | bytes 786440 | tf_op jit(solution)/shard_map/ppermute | solution.py:36
  78.0 17.6 %collective-permute-start.14 = (bf16[16,2048]{1,0:T(8,128)(2,1)S(1)}, bf16[16,2048]{1,0:T(8,128)(2,1)S(1)}, u32[]{:S(2)}, u32[]{:S(2)}) collective-permute-start(bf16[16,2048]{1,0:T(8,128)(2,1)S(1)} %get-tuple-element.124), channel_id=1, source_target_pairs={{0,8},{4,12},{8,0},{12,4},{16,24},{20,28},{24,16},{28,20},{1,9},{5... | collective-permute-start | bytes 196616 | tf_op jit(solution)/shard_map/ppermute | solution.py:36
  79.3 16.3 %collective-permute-start.15 = (bf16[16,2048]{1,0:T(8,128)(2,1)S(1)}, bf16[16,2048]{1,0:T(8,128)(2,1)S(1)}, u32[]{:S(2)}, u32[]{:S(2)}) collective-permute-start(bf16[16,2048]{1,0:T(8,128)(2,1)S(1)} %get-tuple-element.125), channel_id=1, source_target_pairs={{0,16},{4,20},{8,24},{12,28},{16,0},{20,4},{24,8},{28,12},{1,17},{... | collective-permute-start | bytes 196616 | tf_op jit(solution)/shard_map/ppermute | solution.py:36
  82.2 13.4 %collective-permute-start.16 = (bf16[16,2048]{1,0:T(8,128)(2,1)S(1)}, bf16[16,2048]{1,0:T(8,128)(2,1)S(1)}, u32[]{:S(2)}, u32[]{:S(2)}) collective-permute-start(bf16[16,2048]{1,0:T(8,128)(2,1)S(1)} %get-tuple-element.126), channel_id=1, source_target_pairs={{0,24},{4,28},{8,16},{12,20},{16,8},{20,12},{24,0},{28,4},{1,25},{... | collective-permute-start | bytes 196616 | tf_op jit(solution)/shard_map/ppermute | solution.py:36

commit v2 on v1

v2 whole, which is shorter than its diff:
```python
import functools

import jax
import jax.numpy as jnp
from jax import lax
from jax.experimental import pallas as pl
from jax.experimental.pallas import tpu as pltpu
from jax.sharding import PartitionSpec as P

BF16 = jnp.bfloat16
F32 = jnp.float32
IN_VMEM = pl.BlockSpec(memory_space=pltpu.VMEM)
IN_SMEM = pl.BlockSpec(memory_space=pltpu.SMEM)
ANYWHERE = pl.BlockSpec(memory_space=pl.ANY)
MIB = 1 << 20


def params(mib):
    return pltpu.CompilerParams(vmem_limit_bytes=mib * MIB)


def cost(flops=0, moved=0, exps=0):
    return pl.CostEstimate(flops=flops, bytes_accessed=moved, transcendentals=exps)


def in_vmem(array):
    return pltpu.with_memory_space_constraint(array, pltpu.VMEM)


def in_hbm(array):
    return pltpu.with_memory_space_constraint(array, pltpu.HBM)


def swap(array, axis, distance):
    size = lax.axis_size(axis)
    return lax.ppermute(array, axis, [(i, i ^ distance) for i in range(size)])


def tile_of(extent, largest):
    best = 128
    for tile in range(128, largest + 1, 128):
        if extent % tile == 0:
            best = tile
    return best


def contract_cols(left, right):
    return lax.dot_general(left, right, (((1,), (1,)), ((), ())), preferred_element_type=F32)


def contract_rows(left, right):
    return lax.dot_general(left, right, (((0,), (0,)), ((), ())), preferred_element_type=F32)


def through(arrays, first_input, first_output):
    shapes = [pltpu.VMEM(a.shape, a.dtype) for a in arrays]
    return shapes, {first_input + i: first_output + i for i in range(len(arrays))}


def make_room(weight, held):
    shapes, aliases = through(held, 0, 1)
    results = pl.pallas_call(
        lambda *refs: None,
        out_shape=[pltpu.VMEM(weight.shape, weight.dtype)] + shapes,
        in_specs=[IN_VMEM] * len(held),
        out_specs=[IN_VMEM] * (1 + len(held)),
        input_output_aliases=aliases,
        compiler_params=params(4),
        name="make_room",
    )(*[in_vmem(a) for a in held])
    return results[0], results[1:]


def load(weight, held, after=()):
    parts = 4
    step = weight.shape[0] // parts

    def kernel(src, *refs):
        dst, sem = refs[len(held) + len(after)], refs[-1]
        copies = []
        for i in range(parts):
            rows = pl.ds(i * step, step)
            copies.append(pltpu.make_async_copy(src.at[rows], dst.at[rows], sem.at[i]))
            copies[-1].start()
        for copy in copies:
            copy.wait()

    shapes, aliases = through(held, 1, 1)
    results = pl.pallas_call(
        kernel,
        out_shape=[pltpu.VMEM(weight.shape, weight.dtype)] + shapes,
        in_specs=[ANYWHERE] + [IN_VMEM] * len(held) + [ANYWHERE] * len(after),
        out_specs=[IN_VMEM] * (1 + len(held)),
        scratch_shapes=[pltpu.SemaphoreType.DMA((parts,))],
        input_output_aliases=aliases,
        compiler_params=params(4),
        cost_estimate=cost(moved=weight.size * 2),
        name="load_weight",
    )(in_hbm(weight), *[in_vmem(a) for a in held], *after)
    return results[0], results[1:]


def pack(tokens, grad_out):
    own_rows, features = tokens.shape

    def kernel(tok_ref, grad_ref, out, stage, sems):
        copies = [
            pltpu.make_async_copy(ref, stage.at[i], sems.at[i])
            for i, ref in enumerate((tok_ref, grad_ref))
        ]
        for copy in copies:
            copy.start()
        for copy in copies:
            copy.wait()
        both = [stage[0].astype(F32), stage[1].astype(F32)]
        out[...] = jnp.concatenate(both, axis=0).astype(BF16)

    return pl.pallas_call(
        kernel,
        out_shape=pltpu.VMEM((2 * own_rows, features), BF16),
        in_specs=[ANYWHERE] * 2,
        out_specs=IN_VMEM,
        scratch_shapes=[
            pltpu.VMEM((2, own_rows, features), BF16),
            pltpu.SemaphoreType.DMA((2,)),
        ],
        compiler_params=params(4),
        name="pack",
    )(in_hbm(tokens), in_hbm(grad_out))


def join(own, near):
    both, features = own.shape
    own_rows = both // 2

    def kernel(own_ref, near_ref, out):
        pair = [own_ref[...].astype(F32), near_ref[...].astype(F32)]
        for g in range(2):
            half = slice(g * own_rows, (g + 1) * own_rows)
            out[g * both : (g + 1) * both, :] = jnp.concatenate(
                [p[half] for p in pair], axis=0
            ).astype(BF16)

    return pl.pallas_call(
        kernel,
        out_shape=pltpu.VMEM((2 * both, features), BF16),
        in_specs=[IN_VMEM] * 2,
        out_specs=IN_VMEM,
        compiler_params=params(4),
        name="join",
    )(own, near)


def unpack(blocks, held):
    n, w = len(blocks), len(held)
    rows, features = blocks[0].shape
    half = rows // 2

    def kernel(*refs):
        for b in range(n):
            for g in range(2):
                refs[n + w + g][b * half : (b + 1) * half, :] = refs[b][g * half : (g + 1) * half, :]

    shapes, aliases = through(held, n, 2)
    results = pl.pallas_call(
        kernel,
        out_shape=[pltpu.VMEM((n * half, features), BF16)] * 2 + shapes,
        in_specs=[IN_VMEM] * (n + w),
        out_specs=[IN_VMEM] * (2 + w),
        input_output_aliases=aliases,
        compiler_params=params(4),
        name="unpack",
    )(*blocks, *[in_vmem(a) for a in held])
    return results[0], results[1], results[2:]


def back_products(place, x, source, weights, groups):
    total = x.shape[0]
    share = total // groups
    hidden = source.shape[0]
    tile = tile_of(hidden, 1024)
    n, w = hidden // tile, len(weights)

    def kernel(place_ref, x_ref, src, *refs):
        outs, dst, acc, sems = refs[w : w + groups], refs[2 * w + groups - 1], refs[-2], refs[-1]
        spans = [slice(b * tile, (b + 1) * tile) for b in range(n)]
        copies = [
            pltpu.make_async_copy(src.at[spans[b]], dst.at[spans[b]], sems.at[b]) for b in range(n)
        ]
        for copy in copies:
            copy.start()
        for b in range(n):
            copies[b].wait()
            acc[...] = contract_cols(x_ref[...], dst[spans[b], :])
            for j in range(groups):
                at = pl.multiple_of((place_ref[0] ^ j) * share, share)
                outs[j][:, spans[b]] = acc[pl.ds(at, share), :]

    shapes, aliases = through(weights, 3, groups)
    results = pl.pallas_call(
        kernel,
        out_shape=[pltpu.VMEM((share, hidden), F32)] * groups + shapes,
        in_specs=[IN_SMEM, IN_VMEM, ANYWHERE] + [IN_VMEM] * w,
        out_specs=[IN_VMEM] * (groups + w),
        scratch_shapes=[pltpu.VMEM((total, tile), F32), pltpu.SemaphoreType.DMA((n,))],
        input_output_aliases=aliases,
        compiler_params=params(4),
        name="back_products",
    )(place, x, in_hbm(source), *[in_vmem(a) for a in weights])
    return results[:groups], results[groups:]


def first_products(place, x, weights, used, offset, width, groups):
    total = x.shape[0]
    share = total // groups
    n, w = len(used), len(weights)

    def kernel(place_ref, x_ref, *refs):
        outs, acc = refs[w : w + groups], refs[-1]
        for g in range(n):
            acc[...] = jnp.dot(
                x_ref[...],
                refs[used[g]][:, offset : offset + width],
                preferred_element_type=F32,
            )
            for j in range(groups):
                at = pl.multiple_of((place_ref[0] ^ j) * share, share)
                outs[j][:, g * width : (g + 1) * width] = acc[pl.ds(at, share), :]

    shapes, aliases = through(weights, 2, groups)
    results = pl.pallas_call(
        kernel,
        out_shape=[pltpu.VMEM((share, n * width), F32)] * groups + shapes,
        in_specs=[IN_SMEM] + [IN_VMEM] * (1 + w),
        out_specs=[IN_VMEM] * (groups + w),
        scratch_shapes=[pltpu.VMEM((total, width), F32)],
        input_output_aliases=aliases,
        compiler_params=params(4),
        name="first_products",
    )(place, x, *[in_vmem(a) for a in weights])
    return results[:groups], results[groups:]


def core_sum(pieces, weights):
    widths = [parts[0].shape[1] for parts in pieces]
    share, columns = pieces[0][0].shape[0], sum(widths)
    flat = [part for parts in pieces for part in parts]
    n, w, groups = len(flat), len(weights), len(pieces[0])

    def kernel(*refs):
        at = 0
        for p, width in enumerate(widths):
            total = refs[p * groups][...]
            for ref in refs[p * groups + 1 : (p + 1) * groups]:
                total = total + ref[...]
            refs[n + w][:, at : at + width] = total
            refs[n + w + 1][:, at : at + width] = total.astype(BF16)
            at += width

    shapes, aliases = through(weights, n, 2)
    results = pl.pallas_call(
        kernel,
        out_shape=[pltpu.VMEM((share, columns), F32), pltpu.VMEM((share, columns), BF16)] + shapes,
        in_specs=[IN_VMEM] * (n + w),
        out_specs=[IN_VMEM] * (2 + w),
        input_output_aliases=aliases,
        compiler_params=params(4),
        name="core_sum",
    )(*flat, *[in_vmem(a) for a in weights])
    return results[:2], results[2:]


def added(refs, cols):
    total = refs[0][:, cols]
    for ref in refs[1:]:
        total = total + ref[:, cols].astype(F32)
    return total


def hidden_units(terms, held):
    n, w = len(terms), len(held)
    share, columns = terms[0].shape
    hidden = columns // 2
    step = tile_of(hidden, 512)

    def kernel(*refs):
        for at in range(0, hidden, step):
            gate_pre = added(refs[:n], slice(at, at + step))
            up_proj = added(refs[:n], slice(hidden + at, hidden + at + step))
            sigmoid_gate = 1.0 / (1.0 + jnp.exp(-gate_pre))
            refs[n + w][:, at : at + step] = (gate_pre * sigmoid_gate * up_proj).astype(BF16)

    shapes, aliases = through(held, n, 1)
    results = pl.pallas_call(
        kernel,
        out_shape=[pltpu.VMEM((share, hidden), BF16)] + shapes,
        in_specs=[IN_VMEM] * (n + w),
        out_specs=[IN_VMEM] * (1 + w),
        input_output_aliases=aliases,
        compiler_params=params(4),
        name="hidden_units",
    )(*terms, *[in_vmem(a) for a in held])
    return results[0], results[1:]


def gate_grads(terms, back_terms, held):
    n, w = len(terms), len(held)
    share, columns = terms[0].shape
    hidden = columns // 2
    step = tile_of(hidden, 512)

    def kernel(*refs):
        out = refs[2 * n + w]
        for at in range(0, hidden, step):
            here, there = slice(at, at + step), slice(hidden + at, hidden + at + step)
            gate_pre, up_proj = added(refs[:n], here), added(refs[:n], there)
            d_hidden = added(refs[n : 2 * n], here)
            sigmoid_gate = 1.0 / (1.0 + jnp.exp(-gate_pre))
            out[:, here] = (
                d_hidden * up_proj * sigmoid_gate * (1.0 + gate_pre * (1.0 - sigmoid_gate))
            ).astype(BF16)
            out[:, there] = (d_hidden * gate_pre * sigmoid_gate).astype(BF16)

    shapes, aliases = through(held, 2 * n, 1)
    results = pl.pallas_call(
        kernel,
        out_shape=[pltpu.VMEM((share, columns), BF16)] + shapes,
        in_specs=[IN_VMEM] * (2 * n + w),
        out_specs=[IN_VMEM] * (1 + w),
        input_output_aliases=aliases,
        compiler_params=params(4),
        name="gate_grads",
    )(*terms, *back_terms, *[in_vmem(a) for a in held])
    return results[0], results[1:]


def lay(place_ref, share_refs, laid):
    share = share_refs[0].shape[0]
    for j, ref in enumerate(share_refs):
        at = pl.multiple_of((place_ref[0] ^ j) * share, share)
        laid[pl.ds(at, share), :] = ref[...]


def output_terms(place, shares, down, held):
    groups, w = len(shares), len(held)
    total = shares[0].shape[0] * groups
    hidden, features = down.shape

    def kernel(place_ref, *refs):
        laid, out = refs[groups + 1 + w : groups + 3 + w]
        lay(place_ref, refs[:groups], laid)
        out[...] = jnp.dot(laid[...], refs[groups][...], preferred_element_type=F32)

    shapes, aliases = through(held, groups + 2, 2)
    results = pl.pallas_call(
        kernel,
        out_shape=[pltpu.VMEM((total, hidden), BF16), pltpu.VMEM((total, features), F32)] + shapes,
        in_specs=[IN_SMEM] + [IN_VMEM] * (groups + 1 + w),
        out_specs=[IN_VMEM] * (2 + w),
        input_output_aliases=aliases,
        compiler_params=params(4),
        name="output_terms",
    )(place, *shares, in_vmem(down), *[in_vmem(a) for a in held])
    return results[0], results[1], results[2:]


def input_terms(place, shares, gate, up, out_terms, own_rows):
    groups = len(shares)
    total = shares[0].shape[0] * groups
    features, hidden = gate.shape
    parts = total // own_rows

    def kernel(place_ref, *refs):
        gate_ref, up_ref, out_ref, laid, keep, send = refs[groups:]
        lay(place_ref, refs[:groups], laid)
        back = contract_cols(laid[:, :hidden], gate_ref[...])
        back = back + contract_cols(laid[:, hidden:], up_ref[...])
        for b in range(parts):
            rows = slice(b * own_rows, (b + 1) * own_rows)
            both = jnp.concatenate([out_ref[rows, :], back[rows]], axis=0)
            if b % 2:
                send[b // 2] = both.astype(BF16)
            else:
                keep[b // 2] = both

    shape = (parts // 2, 2 * own_rows, features)
    return pl.pallas_call(
        kernel,
        out_shape=[
            pltpu.VMEM((total, 2 * hidden), BF16),
            pltpu.VMEM(shape, F32),
            pltpu.VMEM(shape, BF16),
        ],
        in_specs=[IN_SMEM] + [IN_VMEM] * (groups + 3),
        out_specs=[IN_VMEM] * 3,
        compiler_params=params(4),
        name="input_terms",
    )(place, *shares, in_vmem(gate), in_vmem(up), out_terms)


def row_sum(keep, near, after):
    n = keep.shape[0]

    def kernel(keep_ref, near_ref, *refs):
        refs = refs[len(after) :]
        refs[0][...] = keep_ref[0] + near_ref[0].astype(F32)
        for j in range(1, n):
            refs[j][...] = (keep_ref[j] + near_ref[j].astype(F32)).astype(BF16)

    shape = keep.shape[1:]
    results = pl.pallas_call(
        kernel,
        out_shape=[pltpu.VMEM(shape, F32)] + [pltpu.VMEM(shape, BF16)] * (n - 1),
        in_specs=[IN_VMEM] * 2 + [ANYWHERE] * len(after),
        out_specs=[IN_VMEM] * n,
        compiler_params=params(4),
        name="row_sum",
    )(keep, near, *[in_hbm(a) for a in after])
    return results[0], results[1:]


def last_sum(total, far, after):
    n = len(far)
    both, features = total.shape

    def kernel(total_ref, *refs):
        outs = refs[n + len(after) :]
        value = total_ref[...]
        for ref in refs[:n]:
            value = value + ref[...].astype(F32)
        outs[0][...] = value[: both // 2].astype(BF16)
        outs[1][...] = value[both // 2 :].astype(BF16)

    return pl.pallas_call(
        kernel,
        out_shape=[jax.ShapeDtypeStruct((both // 2, features), BF16)] * 2,
        in_specs=[IN_VMEM] * (1 + n) + [ANYWHERE] * len(after),
        out_specs=[IN_VMEM] * 2,
        compiler_params=params(4),
        name="last_sum",
    )(total, *far, *[in_hbm(a) for a in after])


def outer(left, right, first, columns, held=(), after=()):
    rows = left.shape[1]
    w = len(held)
    tile = tile_of(rows, 256 if held else 256)
    slots = min(3 if held else 4, rows // tile)
    step = tile_of(columns, 512)

    def kernel(left_ref, right_ref, *refs):
        out, stage, sems = refs[w + len(after)], refs[-2], refs[-1]

        def sent(slot, at):
            return pltpu.make_async_copy(stage.at[slot], out.at[pl.ds(at, tile)], sems.at[slot])

        @pl.loop(0, rows // tile)
        def _(i):
            slot = lax.rem(i, slots)

            @pl.when(i >= slots)
            def _():
                sent(slot, 0).wait()

            at = pl.multiple_of(i * tile, tile)
            part = left_ref[:, pl.ds(at, tile)]
            for s in range(0, columns, step):
                stage[slot, :, s : s + step] = contract_rows(
                    part, right_ref[:, first + s : first + s + step]
                ).astype(BF16)
            sent(slot, at).start()

        for slot in range(slots):
            sent(slot, 0).wait()

    shapes, aliases = through(held, 2, 1)
    results = pl.pallas_call(
        kernel,
        out_shape=[jax.ShapeDtypeStruct((rows, columns), BF16)] + shapes,
        in_specs=[IN_VMEM] * (2 + w) + [ANYWHERE] * len(after),
        out_specs=[ANYWHERE] + [IN_VMEM] * w,
        scratch_shapes=[
            pltpu.VMEM((slots, tile, columns), BF16),
            pltpu.SemaphoreType.DMA((slots,)),
        ],
        input_output_aliases=aliases,
        compiler_params=params(4 if held else 12),
        cost_estimate=cost(moved=rows * columns * 2),
        name="outer",
    )(left, right, *[in_vmem(a) for a in held], *after)
    return results[0], results[1:]


def per_device(tokens, grad_out, gate_weight, up_weight, down_weight):
    own_rows = tokens.shape[0]
    rows, cores, chips = (lax.axis_size(a) for a in ("row", "depth", "col"))
    hidden = gate_weight.shape[1]
    place = lax.axis_index("depth").astype(jnp.int32).reshape(1)

    own = pack(tokens, grad_out)
    pair = join(own, swap(own, "row", 1))
    blocks = [pair] + [swap(pair, "row", k) for k in range(2, rows, 2)]
    gate, _ = load(gate_weight, [], (pair,))
    up, (gate,) = load(up_weight, [gate])
    down, (gate, up,) = make_room(down_weight, [gate, up])
    tok_all, grad_all, held = unpack(blocks, [gate, up, down])

    def over_cores(parts):
        return [parts[0]] + [swap(parts[j], "depth", j) for j in range(1, cores)]

    def over_chips(sums):
        total, rounded = sums
        return [total] + [swap(rounded, "col", k) for k in range(1, chips)]

    parts, held = first_products(place, tok_all, held, [0, 1], 0, hidden, cores)
    sums, held = core_sum([over_cores(parts)], held)
    terms = over_chips(sums)
    parts, held = back_products(place, grad_all, down_weight, held, cores)
    acts, held = hidden_units(terms, held)
    shares = over_cores([acts] * cores)
    sums, (*held, down) = core_sum([over_cores(parts)], held)
    back_terms = over_chips(sums)
    hid_all, out_terms, held = output_terms(place, shares, down, held)
    grad_down, held = outer(hid_all, grad_all, 0, grad_all.shape[1], held)
    acts, (gate, up) = gate_grads(terms, back_terms, held)
    shares = over_cores([acts] * cores)
    d_all, keep, send = input_terms(place, shares, gate, up, out_terms, own_rows)

    near = swap(send, "row", 1)
    grad_gate, _ = outer(tok_all, d_all, 0, hidden, (), (send,))
    total, rounded = row_sum(keep, near, (grad_gate,))
    far = [swap(rounded[j - 1], "row", 2 * j) for j in range(1, rows // 2)]
    grad_up, _ = outer(tok_all, d_all, hidden, hidden, (), (total,))
    layer_out, grad_tokens = last_sum(total, far, (grad_up,))
    return layer_out, grad_tokens, grad_gate, grad_up, grad_down


def solution(mesh):
    acts = P("row", ("col", "depth"))
    wide = P(("col", "depth"), "row")
    return jax.shard_map(
        per_device,
        mesh=mesh,
        in_specs=(acts, acts, wide, wide, acts),
        out_specs=(acts, acts, wide, wide, acts),
        check_vma=False,
    )
```

time: 96.6 us -> 86.9 us (0.90)
  waiting for transfers between devices: 17.5 us -> 9.93 us
  local copies, waits for them, and re-layouts: 1.52 us -> 0 us
  Pallas kernels: 59.5 us -> 58.2 us
    ppermute x17 -> x14, waiting for transfers between devices: 17.5 us -> 9.93 us  [swap(): return lax.ppermute(array, axis, [(i, i ^ distance) for i in range(size)])]
    pallas_call x3 -> x2, Pallas kernels: 15.8 us -> 10.6 us  [load(): pl.pallas_call(kernel, out_shape=[pltpu.VMEM(weight.shape, weight.dtype)]...]
    pallas_call x14, Pallas kernels: 42.9 us -> 46.9 us  [the longest x3 21 us: outer(): pl.pallas_call(kernel, out_shape=[jax.ShapeDtypeStruct((rows, columns), B...]
    unnamed x4 -> x0, local copies, waits for them, and re-layouts: 1.52 us -> none
    ppermute x17 -> x14, starting transfers between devices: 17 us -> 17.8 us  [swap(): return lax.ppermute(array, axis, [(i, i ^ distance) for i in range(size)])]
  transfers between devices with their start and end apart: 17 -> 14, of which waited for: 8 -> 5; matrix products, arithmetic and copies ran while one was open for 0% -> 0% of each run, Pallas kernels for 50% -> 48%
where the time goes in v2:
time: 86.9 us; the launch traced here: 86.8 us
  Pallas kernels  58.2 us (67%)
  starting transfers between devices  17.8 us (20%)
  waiting for transfers between devices  9.93 us (11%)
    pallas_call x3, Pallas kernels, outer(): pl.pallas_call(kernel, out_shape=[jax.ShapeDtypeStruct((rows, columns), B...  21 us
    ppermute x14, starting transfers between devices, swap(): return lax.ppermute(array, axis, [(i, i ^ distance) for i in range(size)])  17.8 us
    pallas_call x2, Pallas kernels, load(): pl.pallas_call(kernel, out_shape=[pltpu.VMEM(weight.shape, weight.dtype)]...  10.6 us
    ppermute x14, waiting for transfers between devices, swap(): return lax.ppermute(array, axis, [(i, i ^ distance) for i in range(size)])  9.93 us
    pallas_call x1, Pallas kernels, input_terms(): pl.pallas_call(kernel, out_shape=[pltpu.VMEM((total, 2 * hidden), BF16),...  8.95 us
    pallas_call x1, Pallas kernels, back_products(): pl.pallas_call(kernel, out_shape=[pltpu.VMEM((share, hidden), F32)] * gro...  7.56 us
    pallas_call x1, Pallas kernels, first_products(): pl.pallas_call(kernel, out_shape=[pltpu.VMEM((share, n * width), F32)] *...  5.24 us
    pallas_call x1, Pallas kernels, output_terms(): pl.pallas_call(kernel, out_shape=[pltpu.VMEM((total, hidden), BF16), pltp...  2.71 us
  transfers between devices with their start and end apart: 14, of which 5 were waited for; matrix products, arithmetic and copies ran while one was open for 0% of the time, Pallas kernels for 48%

profile of v2, /device:TPU:0, one launch (start us, length us, event | category | flops | bytes accessed | tf_op | source)
XLA Modules:
  0.0 86.8 jit_solution(15064412480066832640)
XLA Ops:
  0.6 0.8 pack.1.own_ref
  1.4 3.0 %collective-permute-start = (bf16[16,2048]{1,0:T(8,128)(2,1)S(1)}, bf16[16,2048]{1,0:T(8,128)(2,1)S(1)}, u32[]{:S(2)}, u32[]{:S(2)}) collective-permute-start(bf16[16,2048]{1,0:T(8,128)(2,1)S(1)} %pack.1.own_ref), channel_id=1, source_target_pairs={{0,4},{4,0},{8,12},{12,8},{16,20},{20,16},{24,28},{28,24},{1,5},{5... | collective-permute-start | bytes 196616 | tf_op jit(solution)/shard_map/ppermute | solution.py:36
  4.4 2.2 %collective-permute-done.near_ref = bf16[16,2048]{1,0:T(8,128)(2,1)S(1)} collective-permute-done((bf16[16,2048]{1,0:T(8,128)(2,1)S(1)}, bf16[16,2048]{1,0:T(8,128)(2,1)S(1)}, u32[]{:S(2)}, u32[]{:S(2)}) %collective-permute-start) | collective-permute-done | bytes 65568 | tf_op jit(solution)/shard_map/ppermute | solution.py:36
  6.7 4.2 %collective-permute-start.3 = (bf16[32,2048]{1,0:T(8,128)(2,1)S(1)}, bf16[32,2048]{1,0:T(8,128)(2,1)S(1)}, u32[]{:S(2)}, u32[]{:S(2)}) collective-permute-start(bf16[32,2048]{1,0:T(8,128)(2,1)S(1)} %join.1.refs_0_), channel_id=1, source_target_pairs={{0,24},{4,28},{8,16},{12,20},{16,8},{20,12},{24,0},{28,4},{1,25},{... | collective-permute-start | bytes 393224 | tf_op jit(solution)/shard_map/ppermute | solution.py:36
  10.9 0.0 collective-permute-start.2
  10.9 0.6 collective-permute-start.1
  11.5 5.3 %load_weight.2.refs_0_ = bf16[2048,3584]{1,0:T(8,128)(2,1)S(1)} custom-call(bf16[2048,3584]{1,0:T(8,128)(2,1)} %src.3, bf16[32,2048]{1,0:T(8,128)(2,1)S(1)} %join.1.refs_0_), custom_call_target="tpu_custom_call" | custom-call | bytes 14680064 | tf_op jit(solution)/shard_map/load_weight/pallas_call | solution.py:89
  16.8 5.3 %load_weight.3 = (bf16[2048,3584]{1,0:T(8,128)(2,1)S(1)}, bf16[2048,3584]{1,0:T(8,128)(2,1)S(1)}) custom-call(bf16[2048,3584]{1,0:T(8,128)(2,1)} %src.4, bf16[2048,3584]{1,0:T(8,128)(2,1)S(1)} %load_weight.2.refs_0_), custom_call_target="tpu_custom_call", output_to_operand_aliasing={{1}: (1, {})} | custom-call | bytes 14680064 | tf_op jit(solution)/shard_map/load_weight/pallas_call | solution.py:89
  22.1 0.0 collective-permute-done.3.refs_3_
  22.1 0.0 collective-permute-done.2.refs_2_
  22.1 0.0 collective-permute-done.1.refs_1_
  22.2 5.2 %first_products.1 = (f32[32,7168]{1,0:T(8,128)S(1)}, f32[32,7168]{1,0:T(8,128)S(1)}, bf16[2048,3584]{1,0:T(8,128)(2,1)S(1)}, bf16[2048,3584]{1,0:T(8,128)(2,1)S(1)}, bf16[3584,2048]{1,0:T(8,128)(2,1)S(1)}) custom-call(s32[1]{0:T(128)} %bitcast.place_ref, ...), custom_call_target="tpu_custom_call", output_to_operand_aliasing={{2}: (2, {}), {3}: (3, {}), {4}: (4, {})} | custom-call | tf_op jit(solution)/shard_map/first_products/pallas_call | solution.py:231
  27.5 0.1 collective-permute-start.4
  27.5 2.5 %collective-permute-done.4.refs_1_ = f32[32,7168]{1,0:T(8,128)S(1)} collective-permute-done((f32[32,7168]{1,0:T(8,128)S(1)}, f32[32,7168]{1,0:T(8,128)S(1)}, u32[]{:S(2)}, u32[]{:S(2)}) %collective-permute-start.4) | collective-permute-done | bytes 917536 | tf_op jit(solution)/shard_map/ppermute | solution.py:36
  30.0 0.1 core_sum.2
  30.1 1.7 %collective-permute-start.5 = (bf16[32,7168]{1,0:T(8,128)(2,1)S(1)}, bf16[32,7168]{1,0:T(8,128)(2,1)S(1)}, u32[]{:S(2)}, u32[]{:S(2)}) collective-permute-start(bf16[32,7168]{1,0:T(8,128)(2,1)S(1)} %get-tuple-element.73), channel_id=1, source_target_pairs={{0,2},{2,0},{1,3},{3,1},{4,6},{6,4},{5,7},{7,5},{8,10},{10,8},{9,1... | collective-permute-start | bytes 1376264 | tf_op jit(solution)/shard_map/ppermute | solution.py:36
  31.8 7.6 %back_products.1 = (f32[32,3584]{1,0:T(8,128)S(1)}, f32[32,3584]{1,0:T(8,128)S(1)}, bf16[2048,3584]{1,0:T(8,128)(2,1)S(1)}, bf16[2048,3584]{1,0:T(8,128)(2,1)S(1)}, bf16[3584,2048]{1,0:T(8,128)(2,1)S(1)}) custom-call(s32[1]{0:T(128)} %bitcast.place_ref, ...), custom_call_target="tpu_custom_call", output_to_operand_aliasing={{2}: (3, {}), {3}: (4, {}), {4}: (5, {})} | custom-call | tf_op jit(solution)/shard_map/back_products/pallas_call | solution.py:200
  39.4 0.1 collective-permute-start.6
  39.5 3.3 %collective-permute-done.5.refs_1_ = bf16[32,7168]{1,0:T(8,128)(2,1)S(1)} collective-permute-done((bf16[32,7168]{1,0:T(8,128)(2,1)S(1)}, bf16[32,7168]{1,0:T(8,128)(2,1)S(1)}, u32[]{:S(2)}, u32[]{:S(2)}) %collective-permute-start.5) | collective-permute-done | bytes 458784 | tf_op jit(solution)/shard_map/ppermute | solution.py:36
  42.7 0.2 hidden_units.1
  42.9 0.1 collective-permute-start.8
  43.0 0.0 collective-permute-done.6.refs_1_
  43.0 0.1 core_sum.3
  43.1 1.7 %collective-permute-start.7 = (bf16[32,3584]{1,0:T(8,128)(2,1)S(1)}, bf16[32,3584]{1,0:T(8,128)(2,1)S(1)}, u32[]{:S(2)}, u32[]{:S(2)}) collective-permute-start(bf16[32,3584]{1,0:T(8,128)(2,1)S(1)} %get-tuple-element.87), channel_id=1, source_target_pairs={{0,2},{2,0},{1,3},{3,1},{4,6},{6,4},{5,7},{7,5},{8,10},{10,8},{9,1... | collective-permute-start | bytes 688136 | tf_op jit(solution)/shard_map/ppermute | solution.py:36
  44.8 0.0 collective-permute-done.8.refs_1_
  44.8 2.7 %output_terms.1 = (bf16[64,3584]{1,0:T(8,128)(2,1)S(1)}, f32[64,2048]{1,0:T(8,128)S(1)}, bf16[2048,3584]{1,0:T(8,128)(2,1)S(1)}, bf16[2048,3584]{1,0:T(8,128)(2,1)S(1)}) custom-call(s32[1]{0:T(128)} %bitcast.place_ref, bf16[32,3584]{1,0:T(8,128)(2,1)S(1)} %get-tuple-element.88.refs_0_, ...), custom_call_target="tpu_custom_call", output_to_operand_aliasing={{2}: (4, {}), {3}: (5, {})} | custom-call | tf_op jit(solution)/shard_map/output_terms/pallas_call | solution.py:355
  47.5 7.8 %outer.3 = (bf16[3584,2048]{1,0:T(8,128)(2,1)}, bf16[2048,3584]{1,0:T(8,128)(2,1)S(1)}, bf16[2048,3584]{1,0:T(8,128)(2,1)S(1)}) custom-call(bf16[64,3584]{1,0:T(8,128)(2,1)S(1)} %get-tuple-element.92.left_ref, bf16[64,2048]{1,0:T(8,128)(2,1)S(1)} %get-tuple-element.74.x_ref.right_ref, ...), custom_call_target="tpu_custom_call", output_to_operand_aliasing={{1}: (2, {}), {2}: (3, {})} | custom-call | bytes 14680064 | tf_op jit(solution)/shard_map/outer/pallas_call | solution.py:477
  55.3 0.0 collective-permute-done.7.refs_3_
  55.3 0.3 gate_grads.1
  55.7 0.3 collective-permute-start.9
  55.9 1.6 %collective-permute-done.9.refs_1_ = bf16[32,7168]{1,0:T(8,128)(2,1)S(1)} collective-permute-done((bf16[32,7168]{1,0:T(8,128)(2,1)S(1)}, bf16[32,7168]{1,0:T(8,128)(2,1)S(1)}, u32[]{:S(2)}, u32[]{:S(2)}) %collective-permute-start.9) | collective-permute-done | bytes 458784 | tf_op jit(solution)/shard_map/ppermute | solution.py:36
  57.5 8.9 %input_terms.1 = (bf16[64,7168]{1,0:T(8,128)(2,1)S(1)}, f32[4,16,2048]{2,1,0:T(8,128)S(1)}, bf16[4,16,2048]{2,1,0:T(8,128)(2,1)S(1)}) custom-call(s32[1]{0:T(128)} %bitcast.place_ref, bf16[32,7168]{1,0:T(8,128)(2,1)S(1)} %get-tuple-element.97.refs_0_, bf16[32,7168]{1,0:T(8,128)(2,1)S(1)} %collective-permute-done.9.refs_1_, ...), custom_call_target="tpu_custom_call" | custom-call | tf_op jit(solution)/shard_map/input_terms/pallas_call | solution.py:387
  66.5 1.6 %collective-permute-start.10 = (bf16[4,16,2048]{2,1,0:T(8,128)(2,1)S(1)}, bf16[4,16,2048]{2,1,0:T(8,128)(2,1)S(1)}, u32[]{:S(2)}, u32[]{:S(2)}) collective-permute-start(bf16[4,16,2048]{2,1,0:T(8,128)(2,1)S(1)} %get-tuple-element.102.refs_0_), channel_id=1, source_target_pairs={{0,4},{4,0},{8,12},{12,8},{16,20},{20,16},{24,28},{28,24},{1,5},{5... | collective-permute-start | bytes 786440 | tf_op jit(solution)/shard_map/ppermute | solution.py:36
  68.0 6.6 %outer.4.refs_0_ = bf16[2048,3584]{1,0:T(8,128)(2,1)} custom-call(bf16[64,2048]{1,0:T(8,128)(2,1)S(1)} %get-tuple-element.63.x_ref.left_ref, bf16[64,7168]{1,0:T(8,128)(2,1)S(1)} %get-tuple-element.103.right_ref, bf16[4,16,2048]{2,1,0:T(8,128)(2,1)S(1)} %get-tuple-element.102.refs_0_), custom_call_target="tpu_custom_call" | custom-call | bytes 14680064 | tf_op jit(solution)/shard_map/outer/pallas_call | solution.py:477
  74.6 0.3 collective-permute-done.10.near_ref
  75.0 1.3 %collective-permute-start.11 = (bf16[16,2048]{1,0:T(8,128)(2,1)S(1)}, bf16[16,2048]{1,0:T(8,128)(2,1)S(1)}, u32[]{:S(2)}, u32[]{:S(2)}) collective-permute-start(bf16[16,2048]{1,0:T(8,128)(2,1)S(1)} %get-tuple-element.105), channel_id=1, source_target_pairs={{0,8},{4,12},{8,0},{12,4},{16,24},{20,28},{24,16},{28,20},{1,9},{5... | collective-permute-start | bytes 196616 | tf_op jit(solution)/shard_map/ppermute | solution.py:36
  76.3 2.9 %collective-permute-start.12 = (bf16[16,2048]{1,0:T(8,128)(2,1)S(1)}, bf16[16,2048]{1,0:T(8,128)(2,1)S(1)}, u32[]{:S(2)}, u32[]{:S(2)}) collective-permute-start(bf16[16,2048]{1,0:T(8,128)(2,1)S(1)} %get-tuple-element.106), channel_id=1, source_target_pairs={{0,16},{4,20},{8,24},{12,28},{16,0},{20,4},{24,8},{28,12},{1,17},{... | collective-permute-start | bytes 196616 | tf_op jit(solution)/shard_map/ppermute | solution.py:36
  79.3 0.2 collective-permute-start.13
  79.5 6.6 %outer.5.refs_3_ = bf16[2048,3584]{1,0:T(8,128)(2,1)} custom-call(bf16[64,2048]{1,0:T(8,128)(2,1)S(1)} %get-tuple-element.63.x_ref.left_ref, bf16[64,7168]{1,0:T(8,128)(2,1)S(1)} %get-tuple-element.103.right_ref, f32[16,2048]{1,0:T(8,128)S(1)} %get-tuple-element.104.refs_0_.total_ref), custom_call_target="tpu_custom_call" | custom-call | bytes 14680064 | tf_op jit(solution)/shard_map/outer/pallas_call | solution.py:477
  86.1 0.0 collective-permute-done.11.refs_0_
  86.1 0.0 collective-permute-done.12.refs_1_
  86.1 0.0 collective-permute-done.13.refs_2_
  86.1 0.6 last_sum.1
  (4 shorter events, 0.1 us)
Async XLA Ops:
  1.4 5.2 %collective-permute-start = (bf16[16,2048]{1,0:T(8,128)(2,1)S(1)}, bf16[16,2048]{1,0:T(8,128)(2,1)S(1)}, u32[]{:S(2)}, u32[]{:S(2)}) collective-permute-start(bf16[16,2048]{1,0:T(8,128)(2,1)S(1)} %pack.1.own_ref), channel_id=1, source_target_pairs={{0,4},{4,0},{8,12},{12,8},{16,20},{20,16},{24,28},{28,24},{1,5},{5... | collective-permute-start | bytes 196616 | tf_op jit(solution)/shard_map/ppermute | solution.py:36
  6.7 15.4 %collective-permute-start.3 = (bf16[32,2048]{1,0:T(8,128)(2,1)S(1)}, bf16[32,2048]{1,0:T(8,128)(2,1)S(1)}, u32[]{:S(2)}, u32[]{:S(2)}) collective-permute-start(bf16[32,2048]{1,0:T(8,128)(2,1)S(1)} %join.1.refs_0_), channel_id=1, source_target_pairs={{0,24},{4,28},{8,16},{12,20},{16,8},{20,12},{24,0},{28,4},{1,25},{... | collective-permute-start | bytes 393224 | tf_op jit(solution)/shard_map/ppermute | solution.py:36
  10.9 11.2 %collective-permute-start.2 = (bf16[32,2048]{1,0:T(8,128)(2,1)S(1)}, bf16[32,2048]{1,0:T(8,128)(2,1)S(1)}, u32[]{:S(2)}, u32[]{:S(2)}) collective-permute-start(bf16[32,2048]{1,0:T(8,128)(2,1)S(1)} %join.1.refs_0_), channel_id=1, source_target_pairs={{0,16},{4,20},{8,24},{12,28},{16,0},{20,4},{24,8},{28,12},{1,17},{... | collective-permute-start | bytes 393224 | tf_op jit(solution)/shard_map/ppermute | solution.py:36
  10.9 11.3 %collective-permute-start.1 = (bf16[32,2048]{1,0:T(8,128)(2,1)S(1)}, bf16[32,2048]{1,0:T(8,128)(2,1)S(1)}, u32[]{:S(2)}, u32[]{:S(2)}) collective-permute-start(bf16[32,2048]{1,0:T(8,128)(2,1)S(1)} %join.1.refs_0_), channel_id=1, source_target_pairs={{0,8},{4,12},{8,0},{12,4},{16,24},{20,28},{24,16},{28,20},{1,9},{5... | collective-permute-start | bytes 393224 | tf_op jit(solution)/shard_map/ppermute | solution.py:36
  27.5 2.5 %collective-permute-start.4 = (f32[32,7168]{1,0:T(8,128)S(1)}, f32[32,7168]{1,0:T(8,128)S(1)}, u32[]{:S(2)}, u32[]{:S(2)}) collective-permute-start(f32[32,7168]{1,0:T(8,128)S(1)} %get-tuple-element.68), channel_id=1, source_target_pairs={{0,1},{1,0},{2,3},{3,2},{4,5},{5,4},{6,7},{7,6},{8,9},{9,8},{10,11... | collective-permute-start | bytes 2752520 | tf_op jit(solution)/shard_map/ppermute | solution.py:36
  30.1 12.6 %collective-permute-start.5 = (bf16[32,7168]{1,0:T(8,128)(2,1)S(1)}, bf16[32,7168]{1,0:T(8,128)(2,1)S(1)}, u32[]{:S(2)}, u32[]{:S(2)}) collective-permute-start(bf16[32,7168]{1,0:T(8,128)(2,1)S(1)} %get-tuple-element.73), channel_id=1, source_target_pairs={{0,2},{2,0},{1,3},{3,1},{4,6},{6,4},{5,7},{7,5},{8,10},{10,8},{9,1... | collective-permute-start | bytes 1376264 | tf_op jit(solution)/shard_map/ppermute | solution.py:36
  39.4 3.6 %collective-permute-start.6 = (f32[32,3584]{1,0:T(8,128)S(1)}, f32[32,3584]{1,0:T(8,128)S(1)}, u32[]{:S(2)}, u32[]{:S(2)}) collective-permute-start(f32[32,3584]{1,0:T(8,128)S(1)} %get-tuple-element.79), channel_id=1, source_target_pairs={{0,1},{1,0},{2,3},{3,2},{4,5},{5,4},{6,7},{7,6},{8,9},{9,8},{10,11... | collective-permute-start | bytes 1376264 | tf_op jit(solution)/shard_map/ppermute | solution.py:36
  42.9 1.9 %collective-permute-start.8 = (bf16[32,3584]{1,0:T(8,128)(2,1)S(1)}, bf16[32,3584]{1,0:T(8,128)(2,1)S(1)}, u32[]{:S(2)}, u32[]{:S(2)}) collective-permute-start(bf16[32,3584]{1,0:T(8,128)(2,1)S(1)} %get-tuple-element.88.refs_0_), channel_id=1, source_target_pairs={{0,1},{1,0},{2,3},{3,2},{4,5},{5,4},{6,7},{7,6},{8,9},{9,8},{10,11... | collective-permute-start | bytes 688136 | tf_op jit(solution)/shard_map/ppermute | solution.py:36
  43.1 12.3 %collective-permute-start.7 = (bf16[32,3584]{1,0:T(8,128)(2,1)S(1)}, bf16[32,3584]{1,0:T(8,128)(2,1)S(1)}, u32[]{:S(2)}, u32[]{:S(2)}) collective-permute-start(bf16[32,3584]{1,0:T(8,128)(2,1)S(1)} %get-tuple-element.87), channel_id=1, source_target_pairs={{0,2},{2,0},{1,3},{3,1},{4,6},{6,4},{5,7},{7,5},{8,10},{10,8},{9,1... | collective-permute-start | bytes 688136 | tf_op jit(solution)/shard_map/ppermute | solution.py:36
  55.7 1.9 %collective-permute-start.9 = (bf16[32,7168]{1,0:T(8,128)(2,1)S(1)}, bf16[32,7168]{1,0:T(8,128)(2,1)S(1)}, u32[]{:S(2)}, u32[]{:S(2)}) collective-permute-start(bf16[32,7168]{1,0:T(8,128)(2,1)S(1)} %get-tuple-element.97.refs_0_), channel_id=1, source_target_pairs={{0,1},{1,0},{2,3},{3,2},{4,5},{5,4},{6,7},{7,6},{8,9},{9,8},{10,11... | collective-permute-start | bytes 1376264 | tf_op jit(solution)/shard_map/ppermute | solution.py:36
  66.5 8.5 %collective-permute-start.10 = (bf16[4,16,2048]{2,1,0:T(8,128)(2,1)S(1)}, bf16[4,16,2048]{2,1,0:T(8,128)(2,1)S(1)}, u32[]{:S(2)}, u32[]{:S(2)}) collective-permute-start(bf16[4,16,2048]{2,1,0:T(8,128)(2,1)S(1)} %get-tuple-element.102.refs_0_), channel_id=1, source_target_pairs={{0,4},{4,0},{8,12},{12,8},{16,20},{20,16},{24,28},{28,24},{1,5},{5... | collective-permute-start | bytes 786440 | tf_op jit(solution)/shard_map/ppermute | solution.py:36
  75.0 11.0 %collective-permute-start.11 = (bf16[16,2048]{1,0:T(8,128)(2,1)S(1)}, bf16[16,2048]{1,0:T(8,128)(2,1)S(1)}, u32[]{:S(2)}, u32[]{:S(2)}) collective-permute-start(bf16[16,2048]{1,0:T(8,128)(2,1)S(1)} %get-tuple-element.105), channel_id=1, source_target_pairs={{0,8},{4,12},{8,0},{12,4},{16,24},{20,28},{24,16},{28,20},{1,9},{5... | collective-permute-start | bytes 196616 | tf_op jit(solution)/shard_map/ppermute | solution.py:36
  76.3 9.7 %collective-permute-start.12 = (bf16[16,2048]{1,0:T(8,128)(2,1)S(1)}, bf16[16,2048]{1,0:T(8,128)(2,1)S(1)}, u32[]{:S(2)}, u32[]{:S(2)}) collective-permute-start(bf16[16,2048]{1,0:T(8,128)(2,1)S(1)} %get-tuple-element.106), channel_id=1, source_target_pairs={{0,16},{4,20},{8,24},{12,28},{16,0},{20,4},{24,8},{28,12},{1,17},{... | collective-permute-start | bytes 196616 | tf_op jit(solution)/shard_map/ppermute | solution.py:36
  79.3 6.8 %collective-permute-start.13 = (bf16[16,2048]{1,0:T(8,128)(2,1)S(1)}, bf16[16,2048]{1,0:T(8,128)(2,1)S(1)}, u32[]{:S(2)}, u32[]{:S(2)}) collective-permute-start(bf16[16,2048]{1,0:T(8,128)(2,1)S(1)} %get-tuple-element.107), channel_id=1, source_target_pairs={{0,24},{4,28},{8,16},{12,20},{16,8},{20,12},{24,0},{28,4},{1,25},{... | collective-permute-start | bytes 196616 | tf_op jit(solution)/shard_map/ppermute | solution.py:36

commit v3 on v2

--- a/solution.py
+++ b/solution.py
@@ -341,27 +341,49 @@
         laid[pl.ds(at, share), :] = ref[...]
 
 
-def output_terms(place, shares, down, held):
+def output_terms(place, shares, grad_all, down, held):
     groups, w = len(shares), len(held)
     total = shares[0].shape[0] * groups
     hidden, features = down.shape
+    tile = tile_of(hidden, 512)
+    n = hidden // tile
+    step = tile_of(features, 512)
 
     def kernel(place_ref, *refs):
-        laid, out = refs[groups + 1 + w : groups + 3 + w]
+        grad_ref = refs[groups]
+        out, grad_down, block = refs[groups + 2 + w : groups + 5 + w]
+        laid, sems = refs[-2:]
         lay(place_ref, refs[:groups], laid)
-        out[...] = jnp.dot(laid[...], refs[groups][...], preferred_element_type=F32)
-
-    shapes, aliases = through(held, groups + 2, 2)
-    results = pl.pallas_call(
-        kernel,
-        out_shape=[pltpu.VMEM((total, hidden), BF16), pltpu.VMEM((total, features), F32)] + shapes,
-        in_specs=[IN_SMEM] + [IN_VMEM] * (groups + 1 + w),
-        out_specs=[IN_VMEM] * (2 + w),
+        copies = []
+        for i in range(n):
+            rows = slice(i * tile, (i + 1) * tile)
+            term = jnp.dot(laid[:, rows], block[rows, :], preferred_element_type=F32)
+            out[...] = out[...] + term if i else term
+            for at in range(0, features, step):
+                block[rows, at : at + step] = contract_rows(
+                    laid[:, rows], grad_ref[:, at : at + step]
+                ).astype(BF16)
+            copies.append(pltpu.make_async_copy(block.at[rows], grad_down.at[rows], sems.at[i]))
+            copies[-1].start()
+        for copy in copies:
+            copy.wait()
+
+    shapes, aliases = through([down, *held], groups + 2, 2)
+    results = pl.pallas_call(
+        kernel,
+        out_shape=[
+            pltpu.VMEM((total, features), F32),
+            jax.ShapeDtypeStruct((hidden, features), BF16),
+        ]
+        + shapes,
+        in_specs=[IN_SMEM] + [IN_VMEM] * (groups + 2 + w),
+        out_specs=[IN_VMEM, ANYWHERE] + [IN_VMEM] * (1 + w),
+        scratch_shapes=[pltpu.VMEM((total, hidden), BF16), pltpu.SemaphoreType.DMA((n,))],
         input_output_aliases=aliases,
         compiler_params=params(4),
         name="output_terms",
-    )(place, *shares, in_vmem(down), *[in_vmem(a) for a in held])
-    return results[0], results[1], results[2:]
+    )(place, *shares, grad_all, in_vmem(down), *[in_vmem(a) for a in held])
+    return results[0], results[1], results[3:]
 
 
 def input_terms(place, shares, gate, up, out_terms, own_rows):
@@ -369,19 +391,24 @@
     total = shares[0].shape[0] * groups
     features, hidden = gate.shape
     parts = total // own_rows
+    tile = tile_of(features, 1024)
 
     def kernel(place_ref, *refs):
         gate_ref, up_ref, out_ref, laid, keep, send = refs[groups:]
         lay(place_ref, refs[:groups], laid)
-        back = contract_cols(laid[:, :hidden], gate_ref[...])
-        back = back + contract_cols(laid[:, hidden:], up_ref[...])
-        for b in range(parts):
-            rows = slice(b * own_rows, (b + 1) * own_rows)
-            both = jnp.concatenate([out_ref[rows, :], back[rows]], axis=0)
-            if b % 2:
-                send[b // 2] = both.astype(BF16)
-            else:
-                keep[b // 2] = both
+        d_gate, d_up = laid[:, :hidden].T, laid[:, hidden:].T
+        for at in range(0, features, tile):
+            cols = slice(at, at + tile)
+            back = jnp.dot(gate_ref[cols, :], d_gate, preferred_element_type=F32)
+            back = back + jnp.dot(up_ref[cols, :], d_up, preferred_element_type=F32)
+            back = back.T
+            for b in range(parts):
+                rows = slice(b * own_rows, (b + 1) * own_rows)
+                both = jnp.concatenate([out_ref[rows, cols], back[rows]], axis=0)
+                if b % 2:
+                    send[b // 2, :, cols] = both.astype(BF16)
+                else:
+                    keep[b // 2, :, cols] = both
 
     shape = (parts // 2, 2 * own_rows, features)
     return pl.pallas_call(
@@ -441,54 +468,71 @@
     )(total, *far, *[in_hbm(a) for a in after])
 
 
-def outer(left, right, first, columns, held=(), after=()):
+def outer_here(left, right, first, columns, after):
     rows = left.shape[1]
-    w = len(held)
-    tile = tile_of(rows, 256 if held else 256)
-    slots = min(3 if held else 4, rows // tile)
+    step = tile_of(columns, 256)
+
+    def kernel(left_ref, right_ref, *refs):
+        out = refs[len(after)]
+
+        @pl.loop(0, columns // step)
+        def _(i):
+            at = pl.multiple_of(i * step, step)
+            out[:, pl.ds(at, step)] = contract_rows(
+                left_ref[...], right_ref[:, pl.ds(first + at, step)]
+            ).astype(BF16)
+
+    return pl.pallas_call(
+        kernel,
+        out_shape=pltpu.VMEM((rows, columns), BF16),
+        in_specs=[IN_VMEM] * 2 + [ANYWHERE] * len(after),
+        out_specs=IN_VMEM,
+        compiler_params=params(8),
+        cost_estimate=cost(moved=rows * columns * 2),
+        name="outer_here",
+    )(left, right, *after)
+
+
+def outer(left, right, first, columns, after):
+    rows = left.shape[1]
     step = tile_of(columns, 512)
+    blocks, at = [], 0
+    for size in (128, 128, 256):
+        if at + size < rows:
+            blocks.append((at, size))
+            at += size
+    while at < rows:
+        size = min(512, rows - at)
+        blocks.append((at, size))
+        at += size
 
     def kernel(left_ref, right_ref, *refs):
-        out, stage, sems = refs[w + len(after)], refs[-2], refs[-1]
-
-        def sent(slot, at):
-            return pltpu.make_async_copy(stage.at[slot], out.at[pl.ds(at, tile)], sems.at[slot])
-
-        @pl.loop(0, rows // tile)
-        def _(i):
-            slot = lax.rem(i, slots)
-
-            @pl.when(i >= slots)
-            def _():
-                sent(slot, 0).wait()
-
-            at = pl.multiple_of(i * tile, tile)
-            part = left_ref[:, pl.ds(at, tile)]
+        out, stage, sems = refs[len(after) :]
+        copies = []
+        for i, (at, size) in enumerate(blocks):
+            block = slice(at, at + size)
             for s in range(0, columns, step):
-                stage[slot, :, s : s + step] = contract_rows(
-                    part, right_ref[:, first + s : first + s + step]
+                stage[block, s : s + step] = contract_rows(
+                    left_ref[:, block], right_ref[:, first + s : first + s + step]
                 ).astype(BF16)
-            sent(slot, at).start()
-
-        for slot in range(slots):
-            sent(slot, 0).wait()
-
-    shapes, aliases = through(held, 2, 1)
-    results = pl.pallas_call(
-        kernel,
-        out_shape=[jax.ShapeDtypeStruct((rows, columns), BF16)] + shapes,
-        in_specs=[IN_VMEM] * (2 + w) + [ANYWHERE] * len(after),
-        out_specs=[ANYWHERE] + [IN_VMEM] * w,
+            copies.append(pltpu.make_async_copy(stage.at[block], out.at[block], sems.at[i]))
+            copies[-1].start()
+        for copy in copies:
+            copy.wait()
+
+    return pl.pallas_call(
+        kernel,
+        out_shape=jax.ShapeDtypeStruct((rows, columns), BF16),
+        in_specs=[IN_VMEM] * 2 + [ANYWHERE] * len(after),
+        out_specs=ANYWHERE,
         scratch_shapes=[
-            pltpu.VMEM((slots, tile, columns), BF16),
-            pltpu.SemaphoreType.DMA((slots,)),
+            pltpu.VMEM((rows, columns), BF16),
+            pltpu.SemaphoreType.DMA((len(blocks),)),
         ],
-        input_output_aliases=aliases,
-        compiler_params=params(4 if held else 12),
+        compiler_params=params(20),
         cost_estimate=cost(moved=rows * columns * 2),
         name="outer",
-    )(left, right, *[in_vmem(a) for a in held], *after)
-    return results[0], results[1:]
+    )(left, right, *after)
 
 
 def per_device(tokens, grad_out, gate_weight, up_weight, down_weight):
@@ -512,25 +556,27 @@
         total, rounded = sums
         return [total] + [swap(rounded, "col", k) for k in range(1, chips)]
 
-    parts, held = first_products(place, tok_all, held, [0, 1], 0, hidden, cores)
-    sums, held = core_sum([over_cores(parts)], held)
+    pieces = []
+    for which in (0, 1):
+        parts, held = first_products(place, tok_all, held, [which], 0, hidden, cores)
+        pieces.append(over_cores(parts))
+    sums, held = core_sum(pieces, held)
     terms = over_chips(sums)
     parts, held = back_products(place, grad_all, down_weight, held, cores)
     acts, held = hidden_units(terms, held)
     shares = over_cores([acts] * cores)
     sums, (*held, down) = core_sum([over_cores(parts)], held)
     back_terms = over_chips(sums)
-    hid_all, out_terms, held = output_terms(place, shares, down, held)
-    grad_down, held = outer(hid_all, grad_all, 0, grad_all.shape[1], held)
+    out_terms, grad_down, held = output_terms(place, shares, grad_all, down, held)
     acts, (gate, up) = gate_grads(terms, back_terms, held)
     shares = over_cores([acts] * cores)
     d_all, keep, send = input_terms(place, shares, gate, up, out_terms, own_rows)
 
     near = swap(send, "row", 1)
-    grad_gate, _ = outer(tok_all, d_all, 0, hidden, (), (send,))
+    grad_gate = outer(tok_all, d_all, 0, hidden, (send,))
     total, rounded = row_sum(keep, near, (grad_gate,))
     far = [swap(rounded[j - 1], "row", 2 * j) for j in range(1, rows // 2)]
-    grad_up, _ = outer(tok_all, d_all, hidden, hidden, (), (total,))
+    grad_up = outer(tok_all, d_all, hidden, hidden, (total,))
     layer_out, grad_tokens = last_sum(total, far, (grad_up,))
     return layer_out, grad_tokens, grad_gate, grad_up, grad_down
 

time: 86.9 us -> 82.9 us (0.954)
  Pallas kernels: 58.2 us -> 54.1 us
    pallas_call x4 -> x3, Pallas kernels: 23.7 us -> 20.5 us  [the longest x2 12.6 us: outer(): pl.pallas_call(kernel, out_shape=jax.ShapeDtypeStruct((rows, columns), BF...]
    pallas_call x1, Pallas kernels: 8.95 us -> 7.84 us  [input_terms(): pl.pallas_call(kernel, out_shape=[pltpu.VMEM((total, 2 * hidden), BF16),...]
    ppermute x14 -> x15, starting transfers between devices: 17.8 us -> 18.4 us  [swap(): return lax.ppermute(array, axis, [(i, i ^ distance) for i in range(size)])]
    ppermute x14 -> x15, waiting for transfers between devices: 9.93 us -> 9.35 us  [swap(): return lax.ppermute(array, axis, [(i, i ^ distance) for i in range(size)])]
    pallas_call x1 -> x2, Pallas kernels: 5.24 us -> 5.4 us  [first_products(): pl.pallas_call(kernel, out_shape=[pltpu.VMEM((share, n * width), F32)] *...]
  transfers between devices with their start and end apart: 14 -> 15, of which waited for: 5 -> 5; matrix products, arithmetic and copies ran while one was open for 0% -> 0% of each run, Pallas kernels for 48% -> 50%
where the time goes in v3:
time: 82.9 us; the launch traced here: 82.7 us
  Pallas kernels  54.1 us (65%)
  starting transfers between devices  18.4 us (22%)
  waiting for transfers between devices  9.35 us (11%)
  between operations  0.84 us (1%)
    ppermute x15, starting transfers between devices, swap(): return lax.ppermute(array, axis, [(i, i ^ distance) for i in range(size)])  18.4 us
    pallas_call x2, Pallas kernels, outer(): pl.pallas_call(kernel, out_shape=jax.ShapeDtypeStruct((rows, columns), BF...  12.6 us
    pallas_call x2, Pallas kernels, load(): pl.pallas_call(kernel, out_shape=[pltpu.VMEM(weight.shape, weight.dtype)]...  10.6 us
    ppermute x15, waiting for transfers between devices, swap(): return lax.ppermute(array, axis, [(i, i ^ distance) for i in range(size)])  9.35 us
    pallas_call x1, Pallas kernels, output_terms(): pl.pallas_call(kernel, out_shape=[pltpu.VMEM((total, features), F32), jax...  7.93 us
    pallas_call x1, Pallas kernels, input_terms(): pl.pallas_call(kernel, out_shape=[pltpu.VMEM((total, 2 * hidden), BF16),...  7.84 us
    pallas_call x1, Pallas kernels, back_products(): pl.pallas_call(kernel, out_shape=[pltpu.VMEM((share, hidden), F32)] * gro...  7.56 us
    pallas_call x2, Pallas kernels, first_products(): pl.pallas_call(kernel, out_shape=[pltpu.VMEM((share, n * width), F32)] *...  5.4 us
  transfers between devices with their start and end apart: 15, of which 5 were waited for; matrix products, arithmetic and copies ran while one was open for 0% of the time, Pallas kernels for 50%

profile of v3, /device:TPU:0, one launch (start us, length us, event | category | flops | bytes accessed | tf_op | source)
XLA Modules:
  0.0 82.7 jit_solution(883310000159425087)
XLA Ops:
  0.6 0.8 pack.1.own_ref
  1.4 3.0 %collective-permute-start = (bf16[16,2048]{1,0:T(8,128)(2,1)S(1)}, bf16[16,2048]{1,0:T(8,128)(2,1)S(1)}, u32[]{:S(2)}, u32[]{:S(2)}) collective-permute-start(bf16[16,2048]{1,0:T(8,128)(2,1)S(1)} %pack.1.own_ref), channel_id=1, source_target_pairs={{0,4},{4,0},{8,12},{12,8},{16,20},{20,16},{24,28},{28,24},{1,5},{5... | collective-permute-start | bytes 196616 | tf_op jit(solution)/shard_map/ppermute | solution.py:36
  4.4 2.2 %collective-permute-done.near_ref = bf16[16,2048]{1,0:T(8,128)(2,1)S(1)} collective-permute-done((bf16[16,2048]{1,0:T(8,128)(2,1)S(1)}, bf16[16,2048]{1,0:T(8,128)(2,1)S(1)}, u32[]{:S(2)}, u32[]{:S(2)}) %collective-permute-start) | collective-permute-done | bytes 65568 | tf_op jit(solution)/shard_map/ppermute | solution.py:36
  6.7 4.2 %collective-permute-start.3 = (bf16[32,2048]{1,0:T(8,128)(2,1)S(1)}, bf16[32,2048]{1,0:T(8,128)(2,1)S(1)}, u32[]{:S(2)}, u32[]{:S(2)}) collective-permute-start(bf16[32,2048]{1,0:T(8,128)(2,1)S(1)} %join.1.refs_0_), channel_id=1, source_target_pairs={{0,24},{4,28},{8,16},{12,20},{16,8},{20,12},{24,0},{28,4},{1,25},{... | collective-permute-start | bytes 393224 | tf_op jit(solution)/shard_map/ppermute | solution.py:36
  10.9 0.0 collective-permute-start.2
  10.9 0.6 collective-permute-start.1
  11.5 5.3 %load_weight.2.refs_0_ = bf16[2048,3584]{1,0:T(8,128)(2,1)S(1)} custom-call(bf16[2048,3584]{1,0:T(8,128)(2,1)} %src.3, bf16[32,2048]{1,0:T(8,128)(2,1)S(1)} %join.1.refs_0_), custom_call_target="tpu_custom_call" | custom-call | bytes 14680064 | tf_op jit(solution)/shard_map/load_weight/pallas_call | solution.py:89
  16.8 5.3 %load_weight.3 = (bf16[2048,3584]{1,0:T(8,128)(2,1)S(1)}, bf16[2048,3584]{1,0:T(8,128)(2,1)S(1)}) custom-call(bf16[2048,3584]{1,0:T(8,128)(2,1)} %src.4, bf16[2048,3584]{1,0:T(8,128)(2,1)S(1)} %load_weight.2.refs_0_), custom_call_target="tpu_custom_call", output_to_operand_aliasing={{1}: (1, {})} | custom-call | bytes 14680064 | tf_op jit(solution)/shard_map/load_weight/pallas_call | solution.py:89
  22.1 0.0 collective-permute-done.3.refs_3_
  22.1 0.0 collective-permute-done.2.refs_2_
  22.1 0.0 collective-permute-done.1.refs_1_
  22.2 2.7 %first_products.2 = (f32[32,3584]{1,0:T(8,128)S(1)}, f32[32,3584]{1,0:T(8,128)S(1)}, bf16[2048,3584]{1,0:T(8,128)(2,1)S(1)}, bf16[2048,3584]{1,0:T(8,128)(2,1)S(1)}, bf16[3584,2048]{1,0:T(8,128)(2,1)S(1)}) custom-call(s32[1]{0:T(128)} %bitcast.place_ref, ...), custom_call_target="tpu_custom_call", output_to_operand_aliasing={{2}: (2, {}), {3}: (3, {}), {4}: (4, {})} | custom-call | tf_op jit(solution)/shard_map/first_products/pallas_call | solution.py:231
  24.9 0.1 collective-permute-start.4
  25.0 2.7 %first_products.3 = (f32[32,3584]{1,0:T(8,128)S(1)}, f32[32,3584]{1,0:T(8,128)S(1)}, bf16[2048,3584]{1,0:T(8,128)(2,1)S(1)}, bf16[2048,3584]{1,0:T(8,128)(2,1)S(1)}, bf16[3584,2048]{1,0:T(8,128)(2,1)S(1)}) custom-call(s32[1]{0:T(128)} %bitcast.place_ref, ...), custom_call_target="tpu_custom_call", output_to_operand_aliasing={{2}: (2, {}), {3}: (3, {}), {4}: (4, {})} | custom-call | tf_op jit(solution)/shard_map/first_products/pallas_call | solution.py:231
  27.7 0.6 collective-permute-start.5
  28.3 0.0 collective-permute-done.4.refs_1_
  28.3 1.4 %collective-permute-done.5.refs_3_ = f32[32,3584]{1,0:T(8,128)S(1)} collective-permute-done((f32[32,3584]{1,0:T(8,128)S(1)}, f32[32,3584]{1,0:T(8,128)S(1)}, u32[]{:S(2)}, u32[]{:S(2)}) %collective-permute-start.5) | collective-permute-done | bytes 458784 | tf_op jit(solution)/shard_map/ppermute | solution.py:36
  29.7 0.1 core_sum.2
  29.8 1.7 %collective-permute-start.6 = (bf16[32,7168]{1,0:T(8,128)(2,1)S(1)}, bf16[32,7168]{1,0:T(8,128)(2,1)S(1)}, u32[]{:S(2)}, u32[]{:S(2)}) collective-permute-start(bf16[32,7168]{1,0:T(8,128)(2,1)S(1)} %get-tuple-element.80), channel_id=1, source_target_pairs={{0,2},{2,0},{1,3},{3,1},{4,6},{6,4},{5,7},{7,5},{8,10},{10,8},{9,1... | collective-permute-start | bytes 1376264 | tf_op jit(solution)/shard_map/ppermute | solution.py:36
  31.6 7.6 %back_products.1 = (f32[32,3584]{1,0:T(8,128)S(1)}, f32[32,3584]{1,0:T(8,128)S(1)}, bf16[2048,3584]{1,0:T(8,128)(2,1)S(1)}, bf16[2048,3584]{1,0:T(8,128)(2,1)S(1)}, bf16[3584,2048]{1,0:T(8,128)(2,1)S(1)}) custom-call(s32[1]{0:T(128)} %bitcast.place_ref, ...), custom_call_target="tpu_custom_call", output_to_operand_aliasing={{2}: (3, {}), {3}: (4, {}), {4}: (5, {})} | custom-call | tf_op jit(solution)/shard_map/back_products/pallas_call | solution.py:200
  39.1 0.1 collective-permute-start.7
  39.3 3.4 %collective-permute-done.6.refs_1_ = bf16[32,7168]{1,0:T(8,128)(2,1)S(1)} collective-permute-done((bf16[32,7168]{1,0:T(8,128)(2,1)S(1)}, bf16[32,7168]{1,0:T(8,128)(2,1)S(1)}, u32[]{:S(2)}, u32[]{:S(2)}) %collective-permute-start.6) | collective-permute-done | bytes 458784 | tf_op jit(solution)/shard_map/ppermute | solution.py:36
  42.7 0.2 hidden_units.1
  42.9 0.1 collective-permute-start.9
  42.9 0.0 collective-permute-done.7.refs_1_
  43.0 0.1 core_sum.3
  43.0 1.7 %collective-permute-start.8 = (bf16[32,3584]{1,0:T(8,128)(2,1)S(1)}, bf16[32,3584]{1,0:T(8,128)(2,1)S(1)}, u32[]{:S(2)}, u32[]{:S(2)}) collective-permute-start(bf16[32,3584]{1,0:T(8,128)(2,1)S(1)} %get-tuple-element.94), channel_id=1, source_target_pairs={{0,2},{2,0},{1,3},{3,1},{4,6},{6,4},{5,7},{7,5},{8,10},{10,8},{9,1... | collective-permute-start | bytes 688136 | tf_op jit(solution)/shard_map/ppermute | solution.py:36
  44.7 0.0 collective-permute-done.9.refs_1_
  44.7 7.9 %output_terms.1 = (f32[64,2048]{1,0:T(8,128)S(1)}, bf16[3584,2048]{1,0:T(8,128)(2,1)}, bf16[3584,2048]{1,0:T(8,128)(2,1)S(1)}, bf16[2048,3584]{1,0:T(8,128)(2,1)S(1)}, bf16[2048,3584]{1,0:T(8,128)(2,1)S(1)}) custom-call(s32[1]{0:T(128)} %bitcast.place_ref, ...), custom_call_target="tpu_custom_call", output_to_operand_aliasing={{2}: (4, {}), {3}: (5, {}), {4}: (6, {})} | custom-call | tf_op jit(solution)/shard_map/output_terms/pallas_call | solution.py:372
  52.7 0.0 collective-permute-done.8.refs_3_
  52.7 0.3 gate_grads.1
  53.0 0.3 collective-permute-start.10
  53.3 1.6 %collective-permute-done.10.refs_1_ = bf16[32,7168]{1,0:T(8,128)(2,1)S(1)} collective-permute-done((bf16[32,7168]{1,0:T(8,128)(2,1)S(1)}, bf16[32,7168]{1,0:T(8,128)(2,1)S(1)}, u32[]{:S(2)}, u32[]{:S(2)}) %collective-permute-start.10) | collective-permute-done | bytes 458784 | tf_op jit(solution)/shard_map/ppermute | solution.py:36
  54.9 7.8 %input_terms.1 = (bf16[64,7168]{1,0:T(8,128)(2,1)S(1)}, f32[4,16,2048]{2,1,0:T(8,128)S(1)}, bf16[4,16,2048]{2,1,0:T(8,128)(2,1)S(1)}) custom-call(s32[1]{0:T(128)} %bitcast.place_ref, bf16[32,7168]{1,0:T(8,128)(2,1)S(1)} %get-tuple-element.101.refs_0_, bf16[32,7168]{1,0:T(8,128)(2,1)S(1)} %collective-permute-done.10.refs_1_, ...), custom_call_target="tpu_custom_call" | custom-call | tf_op jit(solution)/shard_map/input_terms/pallas_call | solution.py:414
  62.7 1.6 %collective-permute-start.11 = (bf16[4,16,2048]{2,1,0:T(8,128)(2,1)S(1)}, bf16[4,16,2048]{2,1,0:T(8,128)(2,1)S(1)}, u32[]{:S(2)}, u32[]{:S(2)}) collective-permute-start(bf16[4,16,2048]{2,1,0:T(8,128)(2,1)S(1)} %get-tuple-element.106.refs_0_), channel_id=1, source_target_pairs={{0,4},{4,0},{8,12},{12,8},{16,20},{20,16},{24,28},{28,24},{1,5},{5... | collective-permute-start | bytes 786440 | tf_op jit(solution)/shard_map/ppermute | solution.py:36
  64.3 6.3 %outer.2.refs_0_ = bf16[2048,3584]{1,0:T(8,128)(2,1)} custom-call(bf16[64,2048]{1,0:T(8,128)(2,1)S(1)} %get-tuple-element.65.x_ref.left_ref, bf16[64,7168]{1,0:T(8,128)(2,1)S(1)} %get-tuple-element.107.right_ref, bf16[4,16,2048]{2,1,0:T(8,128)(2,1)S(1)} %get-tuple-element.106.refs_0_), custom_call_target="tpu_custom_call" | custom-call | bytes 14680064 | tf_op jit(solution)/shard_map/outer/pallas_call | solution.py:523
  70.6 0.6 collective-permute-done.11.near_ref
  71.3 1.3 %collective-permute-start.12 = (bf16[16,2048]{1,0:T(8,128)(2,1)S(1)}, bf16[16,2048]{1,0:T(8,128)(2,1)S(1)}, u32[]{:S(2)}, u32[]{:S(2)}) collective-permute-start(bf16[16,2048]{1,0:T(8,128)(2,1)S(1)} %get-tuple-element.109), channel_id=1, source_target_pairs={{0,8},{4,12},{8,0},{12,4},{16,24},{20,28},{24,16},{28,20},{1,9},{5... | collective-permute-start | bytes 196616 | tf_op jit(solution)/shard_map/ppermute | solution.py:36
  72.6 2.9 %collective-permute-start.13 = (bf16[16,2048]{1,0:T(8,128)(2,1)S(1)}, bf16[16,2048]{1,0:T(8,128)(2,1)S(1)}, u32[]{:S(2)}, u32[]{:S(2)}) collective-permute-start(bf16[16,2048]{1,0:T(8,128)(2,1)S(1)} %get-tuple-element.110), channel_id=1, source_target_pairs={{0,16},{4,20},{8,24},{12,28},{16,0},{20,4},{24,8},{28,12},{1,17},{... | collective-permute-start | bytes 196616 | tf_op jit(solution)/shard_map/ppermute | solution.py:36
  75.5 0.2 collective-permute-start.14
  75.7 6.3 %outer.3.refs_3_ = bf16[2048,3584]{1,0:T(8,128)(2,1)} custom-call(bf16[64,2048]{1,0:T(8,128)(2,1)S(1)} %get-tuple-element.65.x_ref.left_ref, bf16[64,7168]{1,0:T(8,128)(2,1)S(1)} %get-tuple-element.107.right_ref, f32[16,2048]{1,0:T(8,128)S(1)} %get-tuple-element.108.refs_0_.total_ref), custom_call_target="tpu_custom_call" | custom-call | bytes 14680064 | tf_op jit(solution)/shard_map/outer/pallas_call | solution.py:523
  82.0 0.0 collective-permute-done.12.refs_0_
  82.1 0.0 collective-permute-done.13.refs_1_
  82.1 0.0 collective-permute-done.14.refs_2_
  82.1 0.6 last_sum.1
  (4 shorter events, 0.1 us)
Async XLA Ops:
  1.4 5.2 %collective-permute-start = (bf16[16,2048]{1,0:T(8,128)(2,1)S(1)}, bf16[16,2048]{1,0:T(8,128)(2,1)S(1)}, u32[]{:S(2)}, u32[]{:S(2)}) collective-permute-start(bf16[16,2048]{1,0:T(8,128)(2,1)S(1)} %pack.1.own_ref), channel_id=1, source_target_pairs={{0,4},{4,0},{8,12},{12,8},{16,20},{20,16},{24,28},{28,24},{1,5},{5... | collective-permute-start | bytes 196616 | tf_op jit(solution)/shard_map/ppermute | solution.py:36
  6.7 15.4 %collective-permute-start.3 = (bf16[32,2048]{1,0:T(8,128)(2,1)S(1)}, bf16[32,2048]{1,0:T(8,128)(2,1)S(1)}, u32[]{:S(2)}, u32[]{:S(2)}) collective-permute-start(bf16[32,2048]{1,0:T(8,128)(2,1)S(1)} %join.1.refs_0_), channel_id=1, source_target_pairs={{0,24},{4,28},{8,16},{12,20},{16,8},{20,12},{24,0},{28,4},{1,25},{... | collective-permute-start | bytes 393224 | tf_op jit(solution)/shard_map/ppermute | solution.py:36
  10.9 11.2 %collective-permute-start.2 = (bf16[32,2048]{1,0:T(8,128)(2,1)S(1)}, bf16[32,2048]{1,0:T(8,128)(2,1)S(1)}, u32[]{:S(2)}, u32[]{:S(2)}) collective-permute-start(bf16[32,2048]{1,0:T(8,128)(2,1)S(1)} %join.1.refs_0_), channel_id=1, source_target_pairs={{0,16},{4,20},{8,24},{12,28},{16,0},{20,4},{24,8},{28,12},{1,17},{... | collective-permute-start | bytes 393224 | tf_op jit(solution)/shard_map/ppermute | solution.py:36
  10.9 11.3 %collective-permute-start.1 = (bf16[32,2048]{1,0:T(8,128)(2,1)S(1)}, bf16[32,2048]{1,0:T(8,128)(2,1)S(1)}, u32[]{:S(2)}, u32[]{:S(2)}) collective-permute-start(bf16[32,2048]{1,0:T(8,128)(2,1)S(1)} %join.1.refs_0_), channel_id=1, source_target_pairs={{0,8},{4,12},{8,0},{12,4},{16,24},{20,28},{24,16},{28,20},{1,9},{5... | collective-permute-start | bytes 393224 | tf_op jit(solution)/shard_map/ppermute | solution.py:36
  24.9 3.4 %collective-permute-start.4 = (f32[32,3584]{1,0:T(8,128)S(1)}, f32[32,3584]{1,0:T(8,128)S(1)}, u32[]{:S(2)}, u32[]{:S(2)}) collective-permute-start(f32[32,3584]{1,0:T(8,128)S(1)} %get-tuple-element.70), channel_id=1, source_target_pairs={{0,1},{1,0},{2,3},{3,2},{4,5},{5,4},{6,7},{7,6},{8,9},{9,8},{10,11... | collective-permute-start | bytes 1376264 | tf_op jit(solution)/shard_map/ppermute | solution.py:36
  27.7 2.0 %collective-permute-start.5 = (f32[32,3584]{1,0:T(8,128)S(1)}, f32[32,3584]{1,0:T(8,128)S(1)}, u32[]{:S(2)}, u32[]{:S(2)}) collective-permute-start(f32[32,3584]{1,0:T(8,128)S(1)} %get-tuple-element.75), channel_id=1, source_target_pairs={{0,1},{1,0},{2,3},{3,2},{4,5},{5,4},{6,7},{7,6},{8,9},{9,8},{10,11... | collective-permute-start | bytes 1376264 | tf_op jit(solution)/shard_map/ppermute | solution.py:36
  29.8 12.9 %collective-permute-start.6 = (bf16[32,7168]{1,0:T(8,128)(2,1)S(1)}, bf16[32,7168]{1,0:T(8,128)(2,1)S(1)}, u32[]{:S(2)}, u32[]{:S(2)}) collective-permute-start(bf16[32,7168]{1,0:T(8,128)(2,1)S(1)} %get-tuple-element.80), channel_id=1, source_target_pairs={{0,2},{2,0},{1,3},{3,1},{4,6},{6,4},{5,7},{7,5},{8,10},{10,8},{9,1... | collective-permute-start | bytes 1376264 | tf_op jit(solution)/shard_map/ppermute | solution.py:36
  39.1 3.8 %collective-permute-start.7 = (f32[32,3584]{1,0:T(8,128)S(1)}, f32[32,3584]{1,0:T(8,128)S(1)}, u32[]{:S(2)}, u32[]{:S(2)}) collective-permute-start(f32[32,3584]{1,0:T(8,128)S(1)} %get-tuple-element.86), channel_id=1, source_target_pairs={{0,1},{1,0},{2,3},{3,2},{4,5},{5,4},{6,7},{7,6},{8,9},{9,8},{10,11... | collective-permute-start | bytes 1376264 | tf_op jit(solution)/shard_map/ppermute | solution.py:36
  42.9 1.9 %collective-permute-start.9 = (bf16[32,3584]{1,0:T(8,128)(2,1)S(1)}, bf16[32,3584]{1,0:T(8,128)(2,1)S(1)}, u32[]{:S(2)}, u32[]{:S(2)}) collective-permute-start(bf16[32,3584]{1,0:T(8,128)(2,1)S(1)} %get-tuple-element.95.refs_0_), channel_id=1, source_target_pairs={{0,1},{1,0},{2,3},{3,2},{4,5},{5,4},{6,7},{7,6},{8,9},{9,8},{10,11... | collective-permute-start | bytes 688136 | tf_op jit(solution)/shard_map/ppermute | solution.py:36
  43.0 9.7 %collective-permute-start.8 = (bf16[32,3584]{1,0:T(8,128)(2,1)S(1)}, bf16[32,3584]{1,0:T(8,128)(2,1)S(1)}, u32[]{:S(2)}, u32[]{:S(2)}) collective-permute-start(bf16[32,3584]{1,0:T(8,128)(2,1)S(1)} %get-tuple-element.94), channel_id=1, source_target_pairs={{0,2},{2,0},{1,3},{3,1},{4,6},{6,4},{5,7},{7,5},{8,10},{10,8},{9,1... | collective-permute-start | bytes 688136 | tf_op jit(solution)/shard_map/ppermute | solution.py:36
  53.0 1.9 %collective-permute-start.10 = (bf16[32,7168]{1,0:T(8,128)(2,1)S(1)}, bf16[32,7168]{1,0:T(8,128)(2,1)S(1)}, u32[]{:S(2)}, u32[]{:S(2)}) collective-permute-start(bf16[32,7168]{1,0:T(8,128)(2,1)S(1)} %get-tuple-element.101.refs_0_), channel_id=1, source_target_pairs={{0,1},{1,0},{2,3},{3,2},{4,5},{5,4},{6,7},{7,6},{8,9},{9,8},{10,11... | collective-permute-start | bytes 1376264 | tf_op jit(solution)/shard_map/ppermute | solution.py:36
  62.7 8.5 %collective-permute-start.11 = (bf16[4,16,2048]{2,1,0:T(8,128)(2,1)S(1)}, bf16[4,16,2048]{2,1,0:T(8,128)(2,1)S(1)}, u32[]{:S(2)}, u32[]{:S(2)}) collective-permute-start(bf16[4,16,2048]{2,1,0:T(8,128)(2,1)S(1)} %get-tuple-element.106.refs_0_), channel_id=1, source_target_pairs={{0,4},{4,0},{8,12},{12,8},{16,20},{20,16},{24,28},{28,24},{1,5},{5... | collective-permute-start | bytes 786440 | tf_op jit(solution)/shard_map/ppermute | solution.py:36
  71.3 10.8 %collective-permute-start.12 = (bf16[16,2048]{1,0:T(8,128)(2,1)S(1)}, bf16[16,2048]{1,0:T(8,128)(2,1)S(1)}, u32[]{:S(2)}, u32[]{:S(2)}) collective-permute-start(bf16[16,2048]{1,0:T(8,128)(2,1)S(1)} %get-tuple-element.109), channel_id=1, source_target_pairs={{0,8},{4,12},{8,0},{12,4},{16,24},{20,28},{24,16},{28,20},{1,9},{5... | collective-permute-start | bytes 196616 | tf_op jit(solution)/shard_map/ppermute | solution.py:36
  72.6 9.5 %collective-permute-start.13 = (bf16[16,2048]{1,0:T(8,128)(2,1)S(1)}, bf16[16,2048]{1,0:T(8,128)(2,1)S(1)}, u32[]{:S(2)}, u32[]{:S(2)}) collective-permute-start(bf16[16,2048]{1,0:T(8,128)(2,1)S(1)} %get-tuple-element.110), channel_id=1, source_target_pairs={{0,16},{4,20},{8,24},{12,28},{16,0},{20,4},{24,8},{28,12},{1,17},{... | collective-permute-start | bytes 196616 | tf_op jit(solution)/shard_map/ppermute | solution.py:36
  75.5 6.6 %collective-permute-start.14 = (bf16[16,2048]{1,0:T(8,128)(2,1)S(1)}, bf16[16,2048]{1,0:T(8,128)(2,1)S(1)}, u32[]{:S(2)}, u32[]{:S(2)}) collective-permute-start(bf16[16,2048]{1,0:T(8,128)(2,1)S(1)} %get-tuple-element.111), channel_id=1, source_target_pairs={{0,24},{4,28},{8,16},{12,20},{16,8},{20,12},{24,0},{28,4},{1,25},{... | collective-permute-start | bytes 196616 | tf_op jit(solution)/shard_map/ppermute | solution.py:36

commit v4 on v3

--- a/solution.py
+++ b/solution.py
@@ -71,9 +71,9 @@
     return results[0], results[1:]
 
 
-def load(weight, held, after=()):
+def load(weight, held, after=(), share=1):
     parts = 4
-    step = weight.shape[0] // parts
+    step = weight.shape[0] // (share * parts)
 
     def kernel(src, *refs):
         dst, sem = refs[len(held) + len(after)], refs[-1]
@@ -182,7 +182,8 @@
     n, w = hidden // tile, len(weights)
 
     def kernel(place_ref, x_ref, src, *refs):
-        outs, dst, acc, sems = refs[w : w + groups], refs[2 * w + groups - 1], refs[-2], refs[-1]
+        outs, dst = refs[w : w + groups * n], refs[2 * w + groups * n - 1]
+        acc, sems = refs[-2:]
         spans = [slice(b * tile, (b + 1) * tile) for b in range(n)]
         copies = [
             pltpu.make_async_copy(src.at[spans[b]], dst.at[spans[b]], sems.at[b]) for b in range(n)
@@ -194,29 +195,41 @@
             acc[...] = contract_cols(x_ref[...], dst[spans[b], :])
             for j in range(groups):
                 at = pl.multiple_of((place_ref[0] ^ j) * share, share)
-                outs[j][:, spans[b]] = acc[pl.ds(at, share), :]
-
-    shapes, aliases = through(weights, 3, groups)
-    results = pl.pallas_call(
-        kernel,
-        out_shape=[pltpu.VMEM((share, hidden), F32)] * groups + shapes,
+                outs[j * n + b][...] = acc[pl.ds(at, share), :]
+
+    shapes, aliases = through(weights, 3, groups * n)
+    results = pl.pallas_call(
+        kernel,
+        out_shape=[pltpu.VMEM((share, tile), F32)] * (groups * n) + shapes,
         in_specs=[IN_SMEM, IN_VMEM, ANYWHERE] + [IN_VMEM] * w,
-        out_specs=[IN_VMEM] * (groups + w),
+        out_specs=[IN_VMEM] * (groups * n + w),
         scratch_shapes=[pltpu.VMEM((total, tile), F32), pltpu.SemaphoreType.DMA((n,))],
         input_output_aliases=aliases,
         compiler_params=params(4),
         name="back_products",
     )(place, x, in_hbm(source), *[in_vmem(a) for a in weights])
-    return results[:groups], results[groups:]
-
-
-def first_products(place, x, weights, used, offset, width, groups):
+    return [results[b : groups * n : n] for b in range(n)], results[groups * n :]
+
+
+def first_products(place, x, weights, used, offset, width, groups, rest=None):
     total = x.shape[0]
+    source = () if rest is None else (rest[0],)
     share = total // groups
     n, w = len(used), len(weights)
 
     def kernel(place_ref, x_ref, *refs):
-        outs, acc = refs[w : w + groups], refs[-1]
+        acc, sems = refs[-2:]
+        copies = []
+        if source:
+            dst = refs[1 + w + groups + rest[1]]
+            first = dst.shape[0] // rest[2]
+            step = (dst.shape[0] - first) // 4
+            for i in range(4):
+                rows = pl.ds(first + i * step, step)
+                copies.append(pltpu.make_async_copy(refs[0].at[rows], dst.at[rows], sems.at[i]))
+                copies[-1].start()
+        refs = refs[len(source) :]
+        outs = refs[w : w + groups]
         for g in range(n):
             acc[...] = jnp.dot(
                 x_ref[...],
@@ -226,18 +239,20 @@
             for j in range(groups):
                 at = pl.multiple_of((place_ref[0] ^ j) * share, share)
                 outs[j][:, g * width : (g + 1) * width] = acc[pl.ds(at, share), :]
-
-    shapes, aliases = through(weights, 2, groups)
+        for copy in copies:
+            copy.wait()
+
+    shapes, aliases = through(weights, 2 + len(source), groups)
     results = pl.pallas_call(
         kernel,
         out_shape=[pltpu.VMEM((share, n * width), F32)] * groups + shapes,
-        in_specs=[IN_SMEM] + [IN_VMEM] * (1 + w),
+        in_specs=[IN_SMEM, IN_VMEM] + [ANYWHERE] * len(source) + [IN_VMEM] * w,
         out_specs=[IN_VMEM] * (groups + w),
-        scratch_shapes=[pltpu.VMEM((total, width), F32)],
+        scratch_shapes=[pltpu.VMEM((total, width), F32), pltpu.SemaphoreType.DMA((4,))],
         input_output_aliases=aliases,
         compiler_params=params(4),
         name="first_products",
-    )(place, x, *[in_vmem(a) for a in weights])
+    )(place, x, *[in_hbm(a) for a in source], *[in_vmem(a) for a in weights])
     return results[:groups], results[groups:]
 
 
@@ -278,59 +293,58 @@
 
 
 def hidden_units(terms, held):
-    n, w = len(terms), len(held)
-    share, columns = terms[0].shape
-    hidden = columns // 2
+    n, w = len(terms[0]), len(held)
+    share, hidden = terms[0][0].shape
     step = tile_of(hidden, 512)
 
     def kernel(*refs):
         for at in range(0, hidden, step):
             gate_pre = added(refs[:n], slice(at, at + step))
-            up_proj = added(refs[:n], slice(hidden + at, hidden + at + step))
+            up_proj = added(refs[n : 2 * n], slice(at, at + step))
             sigmoid_gate = 1.0 / (1.0 + jnp.exp(-gate_pre))
-            refs[n + w][:, at : at + step] = (gate_pre * sigmoid_gate * up_proj).astype(BF16)
-
-    shapes, aliases = through(held, n, 1)
+            refs[2 * n + w][:, at : at + step] = (gate_pre * sigmoid_gate * up_proj).astype(BF16)
+
+    shapes, aliases = through(held, 2 * n, 1)
     results = pl.pallas_call(
         kernel,
         out_shape=[pltpu.VMEM((share, hidden), BF16)] + shapes,
-        in_specs=[IN_VMEM] * (n + w),
+        in_specs=[IN_VMEM] * (2 * n + w),
         out_specs=[IN_VMEM] * (1 + w),
         input_output_aliases=aliases,
         compiler_params=params(4),
         name="hidden_units",
-    )(*terms, *[in_vmem(a) for a in held])
+    )(*terms[0], *terms[1], *[in_vmem(a) for a in held])
     return results[0], results[1:]
 
 
 def gate_grads(terms, back_terms, held):
-    n, w = len(terms), len(held)
-    share, columns = terms[0].shape
-    hidden = columns // 2
+    n, w = len(back_terms), len(held)
+    share, hidden = back_terms[0].shape
+    columns = 2 * hidden
     step = tile_of(hidden, 512)
 
     def kernel(*refs):
-        out = refs[2 * n + w]
+        out = refs[3 * n + w]
         for at in range(0, hidden, step):
             here, there = slice(at, at + step), slice(hidden + at, hidden + at + step)
-            gate_pre, up_proj = added(refs[:n], here), added(refs[:n], there)
-            d_hidden = added(refs[n : 2 * n], here)
+            gate_pre, up_proj = added(refs[:n], here), added(refs[n : 2 * n], here)
+            d_hidden = added(refs[2 * n : 3 * n], here)
             sigmoid_gate = 1.0 / (1.0 + jnp.exp(-gate_pre))
             out[:, here] = (
                 d_hidden * up_proj * sigmoid_gate * (1.0 + gate_pre * (1.0 - sigmoid_gate))
             ).astype(BF16)
             out[:, there] = (d_hidden * gate_pre * sigmoid_gate).astype(BF16)
 
-    shapes, aliases = through(held, 2 * n, 1)
+    shapes, aliases = through(held, 3 * n, 1)
     results = pl.pallas_call(
         kernel,
         out_shape=[pltpu.VMEM((share, columns), BF16)] + shapes,
-        in_specs=[IN_VMEM] * (2 * n + w),
+        in_specs=[IN_VMEM] * (3 * n + w),
         out_specs=[IN_VMEM] * (1 + w),
         input_output_aliases=aliases,
         compiler_params=params(4),
         name="gate_grads",
-    )(*terms, *back_terms, *[in_vmem(a) for a in held])
+    )(*terms[0], *terms[1], *back_terms, *[in_vmem(a) for a in held])
     return results[0], results[1:]
 
 
@@ -545,7 +559,7 @@
     pair = join(own, swap(own, "row", 1))
     blocks = [pair] + [swap(pair, "row", k) for k in range(2, rows, 2)]
     gate, _ = load(gate_weight, [], (pair,))
-    up, (gate,) = load(up_weight, [gate])
+    up, (gate,) = load(up_weight, [gate], (), 2)
     down, (gate, up,) = make_room(down_weight, [gate, up])
     tok_all, grad_all, held = unpack(blocks, [gate, up, down])
 
@@ -556,16 +570,19 @@
         total, rounded = sums
         return [total] + [swap(rounded, "col", k) for k in range(1, chips)]
 
-    pieces = []
+    parted, terms = [], []
     for which in (0, 1):
-        parts, held = first_products(place, tok_all, held, [which], 0, hidden, cores)
-        pieces.append(over_cores(parts))
-    sums, held = core_sum(pieces, held)
-    terms = over_chips(sums)
-    parts, held = back_products(place, grad_all, down_weight, held, cores)
+        rest = None if which else (up_weight, 1, 2)
+        parts, held = first_products(place, tok_all, held, [which], 0, hidden, cores, rest)
+        parted.append(over_cores(parts))
+    for parts in parted:
+        sums, held = core_sum([parts], held)
+        terms.append(over_chips(sums))
+    back_parts, held = back_products(place, grad_all, down_weight, held, cores)
+    back_parts = [over_cores(parts) for parts in back_parts]
     acts, held = hidden_units(terms, held)
     shares = over_cores([acts] * cores)
-    sums, (*held, down) = core_sum([over_cores(parts)], held)
+    sums, (*held, down) = core_sum(back_parts, held)
     back_terms = over_chips(sums)
     out_terms, grad_down, held = output_terms(place, shares, grad_all, down, held)
     acts, (gate, up) = gate_grads(terms, back_terms, held)

time: 82.9 us -> 81.1 us (0.978)
  waiting for transfers between devices: 9.35 us -> 6.11 us
  starting transfers between devices: 18.4 us -> 20.4 us
    ppermute x15 -> x19, waiting for transfers between devices: 9.35 us -> 6.11 us  [swap(): return lax.ppermute(array, axis, [(i, i ^ distance) for i in range(size)])]
    pallas_call x2, Pallas kernels: 10.6 us -> 8.47 us  [load(): pl.pallas_call(kernel, out_shape=[pltpu.VMEM(weight.shape, weight.dtype)]...]
    ppermute x15 -> x19, starting transfers between devices: 18.4 us -> 20.4 us  [swap(): return lax.ppermute(array, axis, [(i, i ^ distance) for i in range(size)])]
    pallas_call x2, Pallas kernels: 5.4 us -> 6.8 us  [first_products(): pl.pallas_call(kernel, out_shape=[pltpu.VMEM((share, n * width), F32)] *...]
  transfers between devices with their start and end apart: 15 -> 19, of which waited for: 5 -> 5; matrix products, arithmetic and copies ran while one was open for 0% -> 0% of each run, Pallas kernels for 50% -> 49%
where the time goes in v4:
time: 81.1 us; the launch traced here: 80.9 us
  Pallas kernels  53.5 us (66%)
  starting transfers between devices  20.4 us (25%)
  waiting for transfers between devices  6.11 us (8%)
  between operations  0.85 us (1%)
    ppermute x19, starting transfers between devices, swap(): return lax.ppermute(array, axis, [(i, i ^ distance) for i in range(size)])  20.4 us
    pallas_call x2, Pallas kernels, outer(): pl.pallas_call(kernel, out_shape=jax.ShapeDtypeStruct((rows, columns), BF...  12.6 us
    pallas_call x2, Pallas kernels, load(): pl.pallas_call(kernel, out_shape=[pltpu.VMEM(weight.shape, weight.dtype)]...  8.47 us
    pallas_call x1, Pallas kernels, output_terms(): pl.pallas_call(kernel, out_shape=[pltpu.VMEM((total, features), F32), jax...  7.99 us
    pallas_call x1, Pallas kernels, input_terms(): pl.pallas_call(kernel, out_shape=[pltpu.VMEM((total, 2 * hidden), BF16),...  7.84 us
    pallas_call x1, Pallas kernels, back_products(): pl.pallas_call(kernel, out_shape=[pltpu.VMEM((share, tile), F32)] * (grou...  7.56 us
    pallas_call x2, Pallas kernels, first_products(): pl.pallas_call(kernel, out_shape=[pltpu.VMEM((share, n * width), F32)] *...  6.8 us
    ppermute x19, waiting for transfers between devices, swap(): return lax.ppermute(array, axis, [(i, i ^ distance) for i in range(size)])  6.11 us
  transfers between devices with their start and end apart: 19, of which 5 were waited for; matrix products, arithmetic and copies ran while one was open for 0% of the time, Pallas kernels for 49%

profile of v4, /device:TPU:0, one launch (start us, length us, event | category | flops | bytes accessed | tf_op | source)
XLA Modules:
  0.0 80.9 jit_solution(5800077970746285985)
XLA Ops:
  0.6 0.8 pack.1.own_ref
  1.4 3.0 %collective-permute-start = (bf16[16,2048]{1,0:T(8,128)(2,1)S(1)}, bf16[16,2048]{1,0:T(8,128)(2,1)S(1)}, u32[]{:S(2)}, u32[]{:S(2)}) collective-permute-start(bf16[16,2048]{1,0:T(8,128)(2,1)S(1)} %pack.1.own_ref), channel_id=1, source_target_pairs={{0,4},{4,0},{8,12},{12,8},{16,20},{20,16},{24,28},{28,24},{1,5},{5... | collective-permute-start | bytes 196616 | tf_op jit(solution)/shard_map/ppermute | solution.py:36
  4.4 2.2 %collective-permute-done.near_ref = bf16[16,2048]{1,0:T(8,128)(2,1)S(1)} collective-permute-done((bf16[16,2048]{1,0:T(8,128)(2,1)S(1)}, bf16[16,2048]{1,0:T(8,128)(2,1)S(1)}, u32[]{:S(2)}, u32[]{:S(2)}) %collective-permute-start) | collective-permute-done | bytes 65568 | tf_op jit(solution)/shard_map/ppermute | solution.py:36
  6.7 4.2 %collective-permute-start.3 = (bf16[32,2048]{1,0:T(8,128)(2,1)S(1)}, bf16[32,2048]{1,0:T(8,128)(2,1)S(1)}, u32[]{:S(2)}, u32[]{:S(2)}) collective-permute-start(bf16[32,2048]{1,0:T(8,128)(2,1)S(1)} %join.1.refs_0_), channel_id=1, source_target_pairs={{0,24},{4,28},{8,16},{12,20},{16,8},{20,12},{24,0},{28,4},{1,25},{... | collective-permute-start | bytes 393224 | tf_op jit(solution)/shard_map/ppermute | solution.py:36
  10.9 0.0 collective-permute-start.2
  10.9 0.6 collective-permute-start.1
  11.5 5.3 %load_weight.2.refs_0_ = bf16[2048,3584]{1,0:T(8,128)(2,1)S(1)} custom-call(bf16[2048,3584]{1,0:T(8,128)(2,1)} %src.3, bf16[32,2048]{1,0:T(8,128)(2,1)S(1)} %join.1.refs_0_), custom_call_target="tpu_custom_call" | custom-call | bytes 14680064 | tf_op jit(solution)/shard_map/load_weight/pallas_call | solution.py:89
  16.8 3.2 %load_weight.3 = (bf16[2048,3584]{1,0:T(8,128)(2,1)S(1)}, bf16[2048,3584]{1,0:T(8,128)(2,1)S(1)}) custom-call(bf16[2048,3584]{1,0:T(8,128)(2,1)} %refs_0_.1, bf16[2048,3584]{1,0:T(8,128)(2,1)S(1)} %load_weight.2.refs_0_), custom_call_target="tpu_custom_call", output_to_operand_aliasing={{1}: (1, {})} | custom-call | bytes 14680064 | tf_op jit(solution)/shard_map/load_weight/pallas_call | solution.py:89
  20.0 0.0 collective-permute-done.3.refs_3_
  20.0 0.8 collective-permute-done.2.refs_2_
  20.8 0.0 collective-permute-done.1.refs_1_
  20.9 4.1 %first_products.2 = (f32[32,3584]{1,0:T(8,128)S(1)}, f32[32,3584]{1,0:T(8,128)S(1)}, bf16[2048,3584]{1,0:T(8,128)(2,1)S(1)}, bf16[2048,3584]{1,0:T(8,128)(2,1)S(1)}, bf16[3584,2048]{1,0:T(8,128)(2,1)S(1)}) custom-call(s32[1]{0:T(128)} %bitcast.place_ref, ...), custom_call_target="tpu_custom_call", output_to_operand_aliasing={{2}: (3, {}), {3}: (4, {}), {4}: (5, {})} | custom-call | tf_op jit(solution)/shard_map/first_products/pallas_call | solution.py:246
  24.9 0.1 collective-permute-start.4
  25.0 2.7 %first_products.3 = (f32[32,3584]{1,0:T(8,128)S(1)}, f32[32,3584]{1,0:T(8,128)S(1)}, bf16[2048,3584]{1,0:T(8,128)(2,1)S(1)}, bf16[2048,3584]{1,0:T(8,128)(2,1)S(1)}, bf16[3584,2048]{1,0:T(8,128)(2,1)S(1)}) custom-call(s32[1]{0:T(128)} %bitcast.place_ref, ...), custom_call_target="tpu_custom_call", output_to_operand_aliasing={{2}: (2, {}), {3}: (3, {}), {4}: (4, {})} | custom-call | tf_op jit(solution)/shard_map/first_products/pallas_call | solution.py:246
  27.8 0.6 collective-permute-start.6
  28.3 0.0 collective-permute-done.4.refs_1_
  28.3 0.1 core_sum.3
  28.4 1.6 %collective-permute-start.5 = (bf16[32,3584]{1,0:T(8,128)(2,1)S(1)}, bf16[32,3584]{1,0:T(8,128)(2,1)S(1)}, u32[]{:S(2)}, u32[]{:S(2)}) collective-permute-start(bf16[32,3584]{1,0:T(8,128)(2,1)S(1)} %get-tuple-element.89), channel_id=1, source_target_pairs={{0,2},{2,0},{1,3},{3,1},{4,6},{6,4},{5,7},{7,5},{8,10},{10,8},{9,1... | collective-permute-start | bytes 688136 | tf_op jit(solution)/shard_map/ppermute | solution.py:36
  30.0 0.0 collective-permute-done.6.refs_1_
  30.0 0.1 core_sum.4
  30.0 1.4 %collective-permute-start.7 = (bf16[32,3584]{1,0:T(8,128)(2,1)S(1)}, bf16[32,3584]{1,0:T(8,128)(2,1)S(1)}, u32[]{:S(2)}, u32[]{:S(2)}) collective-permute-start(bf16[32,3584]{1,0:T(8,128)(2,1)S(1)} %get-tuple-element.96), channel_id=1, source_target_pairs={{0,2},{2,0},{1,3},{3,1},{4,6},{6,4},{5,7},{7,5},{8,10},{10,8},{9,1... | collective-permute-start | bytes 688136 | tf_op jit(solution)/shard_map/ppermute | solution.py:36
  31.4 7.6 %back_products.1 = (f32[32,896]{1,0:T(8,128)S(1)}, f32[32,896]{1,0:T(8,128)S(1)}, f32[32,896]{1,0:T(8,128)S(1)}, f32[32,896]{1,0:T(8,128)S(1)}, f32[32,896]{1,0:...) custom-call(s32[1]{0:T(128)} %bitcast.place_ref, ...), custom_call_target="tpu_custom_call", output_to_operand_aliasing={{8}: (3, {}), {9}: (4, {}), {10}: (5, {})} | custom-call | tf_op jit(solution)/shard_map/back_products/pallas_call | solution.py:201
  39.0 0.1 collective-permute-start.8
  39.1 0.4 collective-permute-start.9
  39.6 0.1 collective-permute-start.10
  39.6 0.0 collective-permute-done.5.refs_1_
  39.6 0.4 collective-permute-start.11
  40.1 0.8 %collective-permute-done.7.refs_3_ = bf16[32,3584]{1,0:T(8,128)(2,1)S(1)} collective-permute-done((bf16[32,3584]{1,0:T(8,128)(2,1)S(1)}, bf16[32,3584]{1,0:T(8,128)(2,1)S(1)}, u32[]{:S(2)}, u32[]{:S(2)}) %collective-permute-start.7) | collective-permute-done | bytes 229408 | tf_op jit(solution)/shard_map/ppermute | solution.py:36
  40.9 0.2 hidden_units.1
  41.1 0.1 collective-permute-start.13
  41.2 0.0 collective-permute-done.8.refs_1_
  41.2 0.0 collective-permute-done.9.refs_3_
  41.2 0.0 collective-permute-done.10.refs_5_
  41.2 0.0 collective-permute-done.11.refs_7_
  41.2 0.1 core_sum.5
  41.3 1.6 %collective-permute-start.12 = (bf16[32,3584]{1,0:T(8,128)(2,1)S(1)}, bf16[32,3584]{1,0:T(8,128)(2,1)S(1)}, u32[]{:S(2)}, u32[]{:S(2)}) collective-permute-start(bf16[32,3584]{1,0:T(8,128)(2,1)S(1)} %get-tuple-element.116), channel_id=1, source_target_pairs={{0,2},{2,0},{1,3},{3,1},{4,6},{6,4},{5,7},{7,5},{8,10},{10,8},{9,1... | collective-permute-start | bytes 688136 | tf_op jit(solution)/shard_map/ppermute | solution.py:36
  42.9 0.0 collective-permute-done.13.refs_1_
  42.9 8.0 %output_terms.1 = (f32[64,2048]{1,0:T(8,128)S(1)}, bf16[3584,2048]{1,0:T(8,128)(2,1)}, bf16[3584,2048]{1,0:T(8,128)(2,1)S(1)}, bf16[2048,3584]{1,0:T(8,128)(2,1)S(1)}, bf16[2048,3584]{1,0:T(8,128)(2,1)S(1)}) custom-call(s32[1]{0:T(128)} %bitcast.place_ref, ...), custom_call_target="tpu_custom_call", output_to_operand_aliasing={{2}: (4, {}), {3}: (5, {}), {4}: (6, {})} | custom-call | tf_op jit(solution)/shard_map/output_terms/pallas_call | solution.py:386
  50.9 0.0 collective-permute-done.12.refs_5_
  50.9 0.3 gate_grads.1
  51.2 0.2 collective-permute-start.14
  51.5 1.6 %collective-permute-done.14.refs_1_ = bf16[32,7168]{1,0:T(8,128)(2,1)S(1)} collective-permute-done((bf16[32,7168]{1,0:T(8,128)(2,1)S(1)}, bf16[32,7168]{1,0:T(8,128)(2,1)S(1)}, u32[]{:S(2)}, u32[]{:S(2)}) %collective-permute-start.14) | collective-permute-done | bytes 458784 | tf_op jit(solution)/shard_map/ppermute | solution.py:36
  53.1 7.8 %input_terms.1 = (bf16[64,7168]{1,0:T(8,128)(2,1)S(1)}, f32[4,16,2048]{2,1,0:T(8,128)S(1)}, bf16[4,16,2048]{2,1,0:T(8,128)(2,1)S(1)}) custom-call(s32[1]{0:T(128)} %bitcast.place_ref, bf16[32,7168]{1,0:T(8,128)(2,1)S(1)} %get-tuple-element.123.refs_0_, bf16[32,7168]{1,0:T(8,128)(2,1)S(1)} %collective-permute-done.14.refs_1_, ...), custom_call_target="tpu_custom_call" | custom-call | tf_op jit(solution)/shard_map/input_terms/pallas_call | solution.py:428
  60.9 1.5 %collective-permute-start.15 = (bf16[4,16,2048]{2,1,0:T(8,128)(2,1)S(1)}, bf16[4,16,2048]{2,1,0:T(8,128)(2,1)S(1)}, u32[]{:S(2)}, u32[]{:S(2)}) collective-permute-start(bf16[4,16,2048]{2,1,0:T(8,128)(2,1)S(1)} %get-tuple-element.128.refs_0_), channel_id=1, source_target_pairs={{0,4},{4,0},{8,12},{12,8},{16,20},{20,16},{24,28},{28,24},{1,5},{5... | collective-permute-start | bytes 786440 | tf_op jit(solution)/shard_map/ppermute | solution.py:36
  62.5 6.3 %outer.2.refs_0_ = bf16[2048,3584]{1,0:T(8,128)(2,1)} custom-call(bf16[64,2048]{1,0:T(8,128)(2,1)S(1)} %get-tuple-element.76.x_ref.left_ref, bf16[64,7168]{1,0:T(8,128)(2,1)S(1)} %get-tuple-element.129.right_ref, bf16[4,16,2048]{2,1,0:T(8,128)(2,1)S(1)} %get-tuple-element.128.refs_0_), custom_call_target="tpu_custom_call" | custom-call | bytes 14680064 | tf_op jit(solution)/shard_map/outer/pallas_call | solution.py:537
  68.8 0.6 collective-permute-done.15.near_ref
  69.4 0.7 collective-permute-start.16
  70.1 2.9 %collective-permute-start.17 = (bf16[16,2048]{1,0:T(8,128)(2,1)S(1)}, bf16[16,2048]{1,0:T(8,128)(2,1)S(1)}, u32[]{:S(2)}, u32[]{:S(2)}) collective-permute-start(bf16[16,2048]{1,0:T(8,128)(2,1)S(1)} %get-tuple-element.132), channel_id=1, source_target_pairs={{0,16},{4,20},{8,24},{12,28},{16,0},{20,4},{24,8},{28,12},{1,17},{... | collective-permute-start | bytes 196616 | tf_op jit(solution)/shard_map/ppermute | solution.py:36
  73.0 0.8 %collective-permute-start.18 = (bf16[16,2048]{1,0:T(8,128)(2,1)S(1)}, bf16[16,2048]{1,0:T(8,128)(2,1)S(1)}, u32[]{:S(2)}, u32[]{:S(2)}) collective-permute-start(bf16[16,2048]{1,0:T(8,128)(2,1)S(1)} %get-tuple-element.133), channel_id=1, source_target_pairs={{0,24},{4,28},{8,16},{12,20},{16,8},{20,12},{24,0},{28,4},{1,25},{... | collective-permute-start | bytes 196616 | tf_op jit(solution)/shard_map/ppermute | solution.py:36
  73.9 6.3 %outer.3.refs_3_ = bf16[2048,3584]{1,0:T(8,128)(2,1)} custom-call(bf16[64,2048]{1,0:T(8,128)(2,1)S(1)} %get-tuple-element.76.x_ref.left_ref, bf16[64,7168]{1,0:T(8,128)(2,1)S(1)} %get-tuple-element.129.right_ref, f32[16,2048]{1,0:T(8,128)S(1)} %get-tuple-element.130.refs_0_.total_ref), custom_call_target="tpu_custom_call" | custom-call | bytes 14680064 | tf_op jit(solution)/shard_map/outer/pallas_call | solution.py:537
  80.2 0.0 collective-permute-done.16.refs_0_
  80.2 0.0 collective-permute-done.17.refs_1_
  80.2 0.0 collective-permute-done.18.refs_2_
  80.2 0.6 last_sum.1
  (4 shorter events, 0.1 us)
Async XLA Ops:
  1.4 5.2 %collective-permute-start = (bf16[16,2048]{1,0:T(8,128)(2,1)S(1)}, bf16[16,2048]{1,0:T(8,128)(2,1)S(1)}, u32[]{:S(2)}, u32[]{:S(2)}) collective-permute-start(bf16[16,2048]{1,0:T(8,128)(2,1)S(1)} %pack.1.own_ref), channel_id=1, source_target_pairs={{0,4},{4,0},{8,12},{12,8},{16,20},{20,16},{24,28},{28,24},{1,5},{5... | collective-permute-start | bytes 196616 | tf_op jit(solution)/shard_map/ppermute | solution.py:36
  6.7 13.3 %collective-permute-start.3 = (bf16[32,2048]{1,0:T(8,128)(2,1)S(1)}, bf16[32,2048]{1,0:T(8,128)(2,1)S(1)}, u32[]{:S(2)}, u32[]{:S(2)}) collective-permute-start(bf16[32,2048]{1,0:T(8,128)(2,1)S(1)} %join.1.refs_0_), channel_id=1, source_target_pairs={{0,24},{4,28},{8,16},{12,20},{16,8},{20,12},{24,0},{28,4},{1,25},{... | collective-permute-start | bytes 393224 | tf_op jit(solution)/shard_map/ppermute | solution.py:36
  10.9 9.9 %collective-permute-start.2 = (bf16[32,2048]{1,0:T(8,128)(2,1)S(1)}, bf16[32,2048]{1,0:T(8,128)(2,1)S(1)}, u32[]{:S(2)}, u32[]{:S(2)}) collective-permute-start(bf16[32,2048]{1,0:T(8,128)(2,1)S(1)} %join.1.refs_0_), channel_id=1, source_target_pairs={{0,16},{4,20},{8,24},{12,28},{16,0},{20,4},{24,8},{28,12},{1,17},{... | collective-permute-start | bytes 393224 | tf_op jit(solution)/shard_map/ppermute | solution.py:36
  10.9 9.9 %collective-permute-start.1 = (bf16[32,2048]{1,0:T(8,128)(2,1)S(1)}, bf16[32,2048]{1,0:T(8,128)(2,1)S(1)}, u32[]{:S(2)}, u32[]{:S(2)}) collective-permute-start(bf16[32,2048]{1,0:T(8,128)(2,1)S(1)} %join.1.refs_0_), channel_id=1, source_target_pairs={{0,8},{4,12},{8,0},{12,4},{16,24},{20,28},{24,16},{28,20},{1,9},{5... | collective-permute-start | bytes 393224 | tf_op jit(solution)/shard_map/ppermute | solution.py:36
  24.9 3.4 %collective-permute-start.4 = (f32[32,3584]{1,0:T(8,128)S(1)}, f32[32,3584]{1,0:T(8,128)S(1)}, u32[]{:S(2)}, u32[]{:S(2)}) collective-permute-start(f32[32,3584]{1,0:T(8,128)S(1)} %get-tuple-element.81), channel_id=1, source_target_pairs={{0,1},{1,0},{2,3},{3,2},{4,5},{5,4},{6,7},{7,6},{8,9},{9,8},{10,11... | collective-permute-start | bytes 1376264 | tf_op jit(solution)/shard_map/ppermute | solution.py:36
  27.8 2.2 %collective-permute-start.6 = (f32[32,3584]{1,0:T(8,128)S(1)}, f32[32,3584]{1,0:T(8,128)S(1)}, u32[]{:S(2)}, u32[]{:S(2)}) collective-permute-start(f32[32,3584]{1,0:T(8,128)S(1)} %get-tuple-element.91), channel_id=1, source_target_pairs={{0,1},{1,0},{2,3},{3,2},{4,5},{5,4},{6,7},{7,6},{8,9},{9,8},{10,11... | collective-permute-start | bytes 1376264 | tf_op jit(solution)/shard_map/ppermute | solution.py:36
  28.4 11.3 %collective-permute-start.5 = (bf16[32,3584]{1,0:T(8,128)(2,1)S(1)}, bf16[32,3584]{1,0:T(8,128)(2,1)S(1)}, u32[]{:S(2)}, u32[]{:S(2)}) collective-permute-start(bf16[32,3584]{1,0:T(8,128)(2,1)S(1)} %get-tuple-element.89), channel_id=1, source_target_pairs={{0,2},{2,0},{1,3},{3,1},{4,6},{6,4},{5,7},{7,5},{8,10},{10,8},{9,1... | collective-permute-start | bytes 688136 | tf_op jit(solution)/shard_map/ppermute | solution.py:36
  30.0 10.9 %collective-permute-start.7 = (bf16[32,3584]{1,0:T(8,128)(2,1)S(1)}, bf16[32,3584]{1,0:T(8,128)(2,1)S(1)}, u32[]{:S(2)}, u32[]{:S(2)}) collective-permute-start(bf16[32,3584]{1,0:T(8,128)(2,1)S(1)} %get-tuple-element.96), channel_id=1, source_target_pairs={{0,2},{2,0},{1,3},{3,1},{4,6},{6,4},{5,7},{7,5},{8,10},{10,8},{9,1... | collective-permute-start | bytes 688136 | tf_op jit(solution)/shard_map/ppermute | solution.py:36
  39.0 2.2 %collective-permute-start.8 = (f32[32,896]{1,0:T(8,128)S(1)}, f32[32,896]{1,0:T(8,128)S(1)}, u32[]{:S(2)}, u32[]{:S(2)}) collective-permute-start(f32[32,896]{1,0:T(8,128)S(1)} %get-tuple-element.102), channel_id=1, source_target_pairs={{0,1},{1,0},{2,3},{3,2},{4,5},{5,4},{6,7},{7,6},{8,9},{9,8},{10,11... | collective-permute-start | bytes 344072 | tf_op jit(solution)/shard_map/ppermute | solution.py:36
  39.1 2.1 %collective-permute-start.9 = (f32[32,896]{1,0:T(8,128)S(1)}, f32[32,896]{1,0:T(8,128)S(1)}, u32[]{:S(2)}, u32[]{:S(2)}) collective-permute-start(f32[32,896]{1,0:T(8,128)S(1)} %get-tuple-element.104), channel_id=1, source_target_pairs={{0,1},{1,0},{2,3},{3,2},{4,5},{5,4},{6,7},{7,6},{8,9},{9,8},{10,11... | collective-permute-start | bytes 344072 | tf_op jit(solution)/shard_map/ppermute | solution.py:36
  39.6 1.6 %collective-permute-start.10 = (f32[32,896]{1,0:T(8,128)S(1)}, f32[32,896]{1,0:T(8,128)S(1)}, u32[]{:S(2)}, u32[]{:S(2)}) collective-permute-start(f32[32,896]{1,0:T(8,128)S(1)} %get-tuple-element.106), channel_id=1, source_target_pairs={{0,1},{1,0},{2,3},{3,2},{4,5},{5,4},{6,7},{7,6},{8,9},{9,8},{10,11... | collective-permute-start | bytes 344072 | tf_op jit(solution)/shard_map/ppermute | solution.py:36
  39.6 1.6 %collective-permute-start.11 = (f32[32,896]{1,0:T(8,128)S(1)}, f32[32,896]{1,0:T(8,128)S(1)}, u32[]{:S(2)}, u32[]{:S(2)}) collective-permute-start(f32[32,896]{1,0:T(8,128)S(1)} %get-tuple-element.108), channel_id=1, source_target_pairs={{0,1},{1,0},{2,3},{3,2},{4,5},{5,4},{6,7},{7,6},{8,9},{9,8},{10,11... | collective-permute-start | bytes 344072 | tf_op jit(solution)/shard_map/ppermute | solution.py:36
  41.1 1.8 %collective-permute-start.13 = (bf16[32,3584]{1,0:T(8,128)(2,1)S(1)}, bf16[32,3584]{1,0:T(8,128)(2,1)S(1)}, u32[]{:S(2)}, u32[]{:S(2)}) collective-permute-start(bf16[32,3584]{1,0:T(8,128)(2,1)S(1)} %get-tuple-element.117.refs_0_), channel_id=1, source_target_pairs={{0,1},{1,0},{2,3},{3,2},{4,5},{5,4},{6,7},{7,6},{8,9},{9,8},{10,11... | collective-permute-start | bytes 688136 | tf_op jit(solution)/shard_map/ppermute | solution.py:36
  41.3 9.6 %collective-permute-start.12 = (bf16[32,3584]{1,0:T(8,128)(2,1)S(1)}, bf16[32,3584]{1,0:T(8,128)(2,1)S(1)}, u32[]{:S(2)}, u32[]{:S(2)}) collective-permute-start(bf16[32,3584]{1,0:T(8,128)(2,1)S(1)} %get-tuple-element.116), channel_id=1, source_target_pairs={{0,2},{2,0},{1,3},{3,1},{4,6},{6,4},{5,7},{7,5},{8,10},{10,8},{9,1... | collective-permute-start | bytes 688136 | tf_op jit(solution)/shard_map/ppermute | solution.py:36
  51.2 1.9 %collective-permute-start.14 = (bf16[32,7168]{1,0:T(8,128)(2,1)S(1)}, bf16[32,7168]{1,0:T(8,128)(2,1)S(1)}, u32[]{:S(2)}, u32[]{:S(2)}) collective-permute-start(bf16[32,7168]{1,0:T(8,128)(2,1)S(1)} %get-tuple-element.123.refs_0_), channel_id=1, source_target_pairs={{0,1},{1,0},{2,3},{3,2},{4,5},{5,4},{6,7},{7,6},{8,9},{9,8},{10,11... | collective-permute-start | bytes 1376264 | tf_op jit(solution)/shard_map/ppermute | solution.py:36
  60.9 8.5 %collective-permute-start.15 = (bf16[4,16,2048]{2,1,0:T(8,128)(2,1)S(1)}, bf16[4,16,2048]{2,1,0:T(8,128)(2,1)S(1)}, u32[]{:S(2)}, u32[]{:S(2)}) collective-permute-start(bf16[4,16,2048]{2,1,0:T(8,128)(2,1)S(1)} %get-tuple-element.128.refs_0_), channel_id=1, source_target_pairs={{0,4},{4,0},{8,12},{12,8},{16,20},{20,16},{24,28},{28,24},{1,5},{5... | collective-permute-start | bytes 786440 | tf_op jit(solution)/shard_map/ppermute | solution.py:36
  69.4 10.8 %collective-permute-start.16 = (bf16[16,2048]{1,0:T(8,128)(2,1)S(1)}, bf16[16,2048]{1,0:T(8,128)(2,1)S(1)}, u32[]{:S(2)}, u32[]{:S(2)}) collective-permute-start(bf16[16,2048]{1,0:T(8,128)(2,1)S(1)} %get-tuple-element.131), channel_id=1, source_target_pairs={{0,8},{4,12},{8,0},{12,4},{16,24},{20,28},{24,16},{28,20},{1,9},{5... | collective-permute-start | bytes 196616 | tf_op jit(solution)/shard_map/ppermute | solution.py:36
  70.1 10.1 %collective-permute-start.17 = (bf16[16,2048]{1,0:T(8,128)(2,1)S(1)}, bf16[16,2048]{1,0:T(8,128)(2,1)S(1)}, u32[]{:S(2)}, u32[]{:S(2)}) collective-permute-start(bf16[16,2048]{1,0:T(8,128)(2,1)S(1)} %get-tuple-element.132), channel_id=1, source_target_pairs={{0,16},{4,20},{8,24},{12,28},{16,0},{20,4},{24,8},{28,12},{1,17},{... | collective-permute-start | bytes 196616 | tf_op jit(solution)/shard_map/ppermute | solution.py:36
  73.0 7.2 %collective-permute-start.18 = (bf16[16,2048]{1,0:T(8,128)(2,1)S(1)}, bf16[16,2048]{1,0:T(8,128)(2,1)S(1)}, u32[]{:S(2)}, u32[]{:S(2)}) collective-permute-start(bf16[16,2048]{1,0:T(8,128)(2,1)S(1)} %get-tuple-element.133), channel_id=1, source_target_pairs={{0,24},{4,28},{8,16},{12,20},{16,8},{20,12},{24,0},{28,4},{1,25},{... | collective-permute-start | bytes 196616 | tf_op jit(solution)/shard_map/ppermute | solution.py:36

commit v5 on v4

--- a/solution.py
+++ b/solution.py
@@ -361,6 +361,7 @@
     hidden, features = down.shape
     tile = tile_of(hidden, 512)
     n = hidden // tile
+    early = (n + 1) // 2
     step = tile_of(features, 512)
 
     def kernel(place_ref, *refs):
@@ -371,15 +372,20 @@
         copies = []
         for i in range(n):
             rows = slice(i * tile, (i + 1) * tile)
-            term = jnp.dot(laid[:, rows], block[rows, :], preferred_element_type=F32)
-            out[...] = out[...] + term if i else term
+            room = rows
+            if i < early:
+                term = jnp.dot(laid[:, rows], block[rows, :], preferred_element_type=F32)
+                out[...] = out[...] + term if i else term
+            else:
+                room = slice((i - early) * tile, (i - early + 1) * tile)
+                copies[i - early].wait()
             for at in range(0, features, step):
-                block[rows, at : at + step] = contract_rows(
+                block[room, at : at + step] = contract_rows(
                     laid[:, rows], grad_ref[:, at : at + step]
                 ).astype(BF16)
-            copies.append(pltpu.make_async_copy(block.at[rows], grad_down.at[rows], sems.at[i]))
+            copies.append(pltpu.make_async_copy(block.at[room], grad_down.at[rows], sems.at[i]))
             copies[-1].start()
-        for copy in copies:
+        for copy in copies[n - early :]:
             copy.wait()
 
     shapes, aliases = through([down, *held], groups + 2, 2)
@@ -397,7 +403,33 @@
         compiler_params=params(4),
         name="output_terms",
     )(place, *shares, grad_all, in_vmem(down), *[in_vmem(a) for a in held])
-    return results[0], results[1], results[3:]
+    return results[0], results[1], early * tile, results[2:]
+
+
+def more_output_terms(place, shares, out_terms, first, down, held):
+    groups, w = len(shares), len(held)
+    total = shares[0].shape[0] * groups
+    hidden, features = down.shape
+    rows = slice(first, hidden)
+
+    def kernel(place_ref, *refs):
+        before, down_ref = refs[groups : groups + 2]
+        out, laid = refs[groups + 2 + w], refs[-1]
+        lay(place_ref, [ref.at[:, rows] for ref in refs[:groups]], laid)
+        out[...] = before[...] + jnp.dot(laid[...], down_ref[rows, :], preferred_element_type=F32)
+
+    shapes, aliases = through(held, groups + 3, 1)
+    results = pl.pallas_call(
+        kernel,
+        out_shape=[pltpu.VMEM((total, features), F32)] + shapes,
+        in_specs=[IN_SMEM] + [IN_VMEM] * (groups + 2 + w),
+        out_specs=[IN_VMEM] * (1 + w),
+        scratch_shapes=[pltpu.VMEM((total, hidden - first), BF16)],
+        input_output_aliases=aliases,
+        compiler_params=params(4),
+        name="more_output_terms",
+    )(place, *shares, out_terms, in_vmem(down), *[in_vmem(a) for a in held])
+    return results[0], results[1:]
 
 
 def input_terms(place, shares, gate, up, out_terms, own_rows):
@@ -584,9 +616,10 @@
     shares = over_cores([acts] * cores)
     sums, (*held, down) = core_sum(back_parts, held)
     back_terms = over_chips(sums)
-    out_terms, grad_down, held = output_terms(place, shares, grad_all, down, held)
-    acts, (gate, up) = gate_grads(terms, back_terms, held)
-    shares = over_cores([acts] * cores)
+    out_terms, grad_down, first, held = output_terms(place, shares, grad_all, down, held)
+    acts, (down, *held) = gate_grads(terms, back_terms, held)
+    hid_shares, shares = shares, over_cores([acts] * cores)
+    out_terms, (gate, up) = more_output_terms(place, hid_shares, out_terms, first, down, held)
     d_all, keep, send = input_terms(place, shares, gate, up, out_terms, own_rows)
 
     near = swap(send, "row", 1)

time: 81.1 us -> 80.6 us (level)
  waiting for transfers between devices: 6.11 us -> 4.89 us
    ppermute x19, waiting for transfers between devices: 6.11 us -> 4.89 us  [swap(): return lax.ppermute(array, axis, [(i, i ^ distance) for i in range(size)])]
    pallas_call x0 -> x1, Pallas kernels: none -> 1.21 us  [more_output_terms(): pl.pallas_call(kernel, out_shape=[pltpu.VMEM((total, features), F32)] + s...]
  transfers between devices with their start and end apart: 19 -> 19, of which waited for: 5 -> 5; matrix products, arithmetic and copies ran while one was open for 0% -> 0% of each run, Pallas kernels for 49% -> 50%
where the time goes in v5:
time: 80.6 us; the launch traced here: 80.4 us
  Pallas kernels  54 us (67%)
  starting transfers between devices  20.5 us (25%)
  waiting for transfers between devices  4.89 us (6%)
  between operations  1.03 us (1%)
    ppermute x19, starting transfers between devices, swap(): return lax.ppermute(array, axis, [(i, i ^ distance) for i in range(size)])  20.5 us
    pallas_call x2, Pallas kernels, outer(): pl.pallas_call(kernel, out_shape=jax.ShapeDtypeStruct((rows, columns), BF...  12.6 us
    pallas_call x2, Pallas kernels, load(): pl.pallas_call(kernel, out_shape=[pltpu.VMEM(weight.shape, weight.dtype)]...  8.47 us
    pallas_call x1, Pallas kernels, input_terms(): pl.pallas_call(kernel, out_shape=[pltpu.VMEM((total, 2 * hidden), BF16),...  7.84 us
    pallas_call x1, Pallas kernels, back_products(): pl.pallas_call(kernel, out_shape=[pltpu.VMEM((share, tile), F32)] * (grou...  7.56 us
    pallas_call x1, Pallas kernels, output_terms(): pl.pallas_call(kernel, out_shape=[pltpu.VMEM((total, features), F32), jax...  7.3 us
    pallas_call x2, Pallas kernels, first_products(): pl.pallas_call(kernel, out_shape=[pltpu.VMEM((share, n * width), F32)] *...  6.8 us
    ppermute x19, waiting for transfers between devices, swap(): return lax.ppermute(array, axis, [(i, i ^ distance) for i in range(size)])  4.89 us
  transfers between devices with their start and end apart: 19, of which 5 were waited for; matrix products, arithmetic and copies ran while one was open for 0% of the time, Pallas kernels for 50%

profile of v5, /device:TPU:0, one launch (start us, length us, event | category | flops | bytes accessed | tf_op | source)
XLA Modules:
  0.0 80.4 jit_solution(7738682257008653811)
XLA Ops:
  0.6 0.8 pack.1.own_ref
  1.4 3.0 %collective-permute-start = (bf16[16,2048]{1,0:T(8,128)(2,1)S(1)}, bf16[16,2048]{1,0:T(8,128)(2,1)S(1)}, u32[]{:S(2)}, u32[]{:S(2)}) collective-permute-start(bf16[16,2048]{1,0:T(8,128)(2,1)S(1)} %pack.1.own_ref), channel_id=1, source_target_pairs={{0,4},{4,0},{8,12},{12,8},{16,20},{20,16},{24,28},{28,24},{1,5},{5... | collective-permute-start | bytes 196616 | tf_op jit(solution)/shard_map/ppermute | solution.py:36
  4.4 2.2 %collective-permute-done.near_ref = bf16[16,2048]{1,0:T(8,128)(2,1)S(1)} collective-permute-done((bf16[16,2048]{1,0:T(8,128)(2,1)S(1)}, bf16[16,2048]{1,0:T(8,128)(2,1)S(1)}, u32[]{:S(2)}, u32[]{:S(2)}) %collective-permute-start) | collective-permute-done | bytes 65568 | tf_op jit(solution)/shard_map/ppermute | solution.py:36
  6.7 4.2 %collective-permute-start.3 = (bf16[32,2048]{1,0:T(8,128)(2,1)S(1)}, bf16[32,2048]{1,0:T(8,128)(2,1)S(1)}, u32[]{:S(2)}, u32[]{:S(2)}) collective-permute-start(bf16[32,2048]{1,0:T(8,128)(2,1)S(1)} %join.1.refs_0_), channel_id=1, source_target_pairs={{0,24},{4,28},{8,16},{12,20},{16,8},{20,12},{24,0},{28,4},{1,25},{... | collective-permute-start | bytes 393224 | tf_op jit(solution)/shard_map/ppermute | solution.py:36
  10.9 0.0 collective-permute-start.2
  10.9 0.6 collective-permute-start.1
  11.5 5.3 %load_weight.2.refs_0_ = bf16[2048,3584]{1,0:T(8,128)(2,1)S(1)} custom-call(bf16[2048,3584]{1,0:T(8,128)(2,1)} %src.3, bf16[32,2048]{1,0:T(8,128)(2,1)S(1)} %join.1.refs_0_), custom_call_target="tpu_custom_call" | custom-call | bytes 14680064 | tf_op jit(solution)/shard_map/load_weight/pallas_call | solution.py:89
  16.8 3.2 %load_weight.3 = (bf16[2048,3584]{1,0:T(8,128)(2,1)S(1)}, bf16[2048,3584]{1,0:T(8,128)(2,1)S(1)}) custom-call(bf16[2048,3584]{1,0:T(8,128)(2,1)} %refs_0_.1, bf16[2048,3584]{1,0:T(8,128)(2,1)S(1)} %load_weight.2.refs_0_), custom_call_target="tpu_custom_call", output_to_operand_aliasing={{1}: (1, {})} | custom-call | bytes 14680064 | tf_op jit(solution)/shard_map/load_weight/pallas_call | solution.py:89
  20.0 0.0 collective-permute-done.3.refs_3_
  20.0 0.8 collective-permute-done.2.refs_2_
  20.8 0.0 collective-permute-done.1.refs_1_
  20.9 4.1 %first_products.2 = (f32[32,3584]{1,0:T(8,128)S(1)}, f32[32,3584]{1,0:T(8,128)S(1)}, bf16[2048,3584]{1,0:T(8,128)(2,1)S(1)}, bf16[2048,3584]{1,0:T(8,128)(2,1)S(1)}, bf16[3584,2048]{1,0:T(8,128)(2,1)S(1)}) custom-call(s32[1]{0:T(128)} %bitcast.place_ref, ...), custom_call_target="tpu_custom_call", output_to_operand_aliasing={{2}: (3, {}), {3}: (4, {}), {4}: (5, {})} | custom-call | tf_op jit(solution)/shard_map/first_products/pallas_call | solution.py:246
  24.9 0.1 collective-permute-start.4
  25.0 2.7 %first_products.3 = (f32[32,3584]{1,0:T(8,128)S(1)}, f32[32,3584]{1,0:T(8,128)S(1)}, bf16[2048,3584]{1,0:T(8,128)(2,1)S(1)}, bf16[2048,3584]{1,0:T(8,128)(2,1)S(1)}, bf16[3584,2048]{1,0:T(8,128)(2,1)S(1)}) custom-call(s32[1]{0:T(128)} %bitcast.place_ref, ...), custom_call_target="tpu_custom_call", output_to_operand_aliasing={{2}: (2, {}), {3}: (3, {}), {4}: (4, {})} | custom-call | tf_op jit(solution)/shard_map/first_products/pallas_call | solution.py:246
  27.8 0.6 collective-permute-start.6
  28.3 0.0 collective-permute-done.4.refs_1_
  28.3 0.1 core_sum.3
  28.4 1.6 %collective-permute-start.5 = (bf16[32,3584]{1,0:T(8,128)(2,1)S(1)}, bf16[32,3584]{1,0:T(8,128)(2,1)S(1)}, u32[]{:S(2)}, u32[]{:S(2)}) collective-permute-start(bf16[32,3584]{1,0:T(8,128)(2,1)S(1)} %get-tuple-element.94), channel_id=1, source_target_pairs={{0,2},{2,0},{1,3},{3,1},{4,6},{6,4},{5,7},{7,5},{8,10},{10,8},{9,1... | collective-permute-start | bytes 688136 | tf_op jit(solution)/shard_map/ppermute | solution.py:36
  30.0 0.0 collective-permute-done.6.refs_1_
  30.0 0.1 core_sum.4
  30.0 1.4 %collective-permute-start.7 = (bf16[32,3584]{1,0:T(8,128)(2,1)S(1)}, bf16[32,3584]{1,0:T(8,128)(2,1)S(1)}, u32[]{:S(2)}, u32[]{:S(2)}) collective-permute-start(bf16[32,3584]{1,0:T(8,128)(2,1)S(1)} %get-tuple-element.101), channel_id=1, source_target_pairs={{0,2},{2,0},{1,3},{3,1},{4,6},{6,4},{5,7},{7,5},{8,10},{10,8},{9,1... | collective-permute-start | bytes 688136 | tf_op jit(solution)/shard_map/ppermute | solution.py:36
  31.4 7.6 %back_products.1 = (f32[32,896]{1,0:T(8,128)S(1)}, f32[32,896]{1,0:T(8,128)S(1)}, f32[32,896]{1,0:T(8,128)S(1)}, f32[32,896]{1,0:T(8,128)S(1)}, f32[32,896]{1,0:...) custom-call(s32[1]{0:T(128)} %bitcast.place_ref, ...), custom_call_target="tpu_custom_call", output_to_operand_aliasing={{8}: (3, {}), {9}: (4, {}), {10}: (5, {})} | custom-call | tf_op jit(solution)/shard_map/back_products/pallas_call | solution.py:201
  39.0 0.1 collective-permute-start.8
  39.1 0.4 collective-permute-start.9
  39.6 0.1 collective-permute-start.10
  39.6 0.0 collective-permute-done.5.refs_1_
  39.6 0.4 collective-permute-start.11
  40.1 0.8 %collective-permute-done.7.refs_3_ = bf16[32,3584]{1,0:T(8,128)(2,1)S(1)} collective-permute-done((bf16[32,3584]{1,0:T(8,128)(2,1)S(1)}, bf16[32,3584]{1,0:T(8,128)(2,1)S(1)}, u32[]{:S(2)}, u32[]{:S(2)}) %collective-permute-start.7) | collective-permute-done | bytes 229408 | tf_op jit(solution)/shard_map/ppermute | solution.py:36
  40.9 0.2 hidden_units.1
  41.1 0.1 collective-permute-start.13
  41.2 0.0 collective-permute-done.8.refs_1_
  41.2 0.0 collective-permute-done.9.refs_3_
  41.2 0.0 collective-permute-done.10.refs_5_
  41.2 0.0 collective-permute-done.11.refs_7_
  41.2 0.1 core_sum.5
  41.3 1.6 %collective-permute-start.12 = (bf16[32,3584]{1,0:T(8,128)(2,1)S(1)}, bf16[32,3584]{1,0:T(8,128)(2,1)S(1)}, u32[]{:S(2)}, u32[]{:S(2)}) collective-permute-start(bf16[32,3584]{1,0:T(8,128)(2,1)S(1)} %get-tuple-element.121), channel_id=1, source_target_pairs={{0,2},{2,0},{1,3},{3,1},{4,6},{6,4},{5,7},{7,5},{8,10},{10,8},{9,1... | collective-permute-start | bytes 688136 | tf_op jit(solution)/shard_map/ppermute | solution.py:36
  42.9 0.0 collective-permute-done.13.refs_1_
  42.9 7.3 %output_terms.1 = (f32[64,2048]{1,0:T(8,128)S(1)}, bf16[3584,2048]{1,0:T(8,128)(2,1)}, bf16[3584,2048]{1,0:T(8,128)(2,1)S(1)}, bf16[2048,3584]{1,0:T(8,128)(2,1)S(1)}, bf16[2048,3584]{1,0:T(8,128)(2,1)S(1)}) custom-call(s32[1]{0:T(128)} %bitcast.place_ref, ...), custom_call_target="tpu_custom_call", output_to_operand_aliasing={{2}: (4, {}), {3}: (5, {}), {4}: (6, {})} | custom-call | tf_op jit(solution)/shard_map/output_terms/pallas_call | solution.py:392
  50.4 0.0 collective-permute-done.12.refs_5_
  50.4 0.3 gate_grads.1
  50.7 0.3 collective-permute-start.14
  51.0 1.2 %more_output_terms.1 = (f32[64,2048]{1,0:T(8,128)S(1)}, bf16[2048,3584]{1,0:T(8,128)(2,1)S(1)}, bf16[2048,3584]{1,0:T(8,128)(2,1)S(1)}) custom-call(s32[1]{0:T(128)} %bitcast.place_ref, bf16[32,3584]{1,0:T(8,128)(2,1)S(1)} %get-tuple-element.122.refs_0_, ...), custom_call_target="tpu_custom_call", output_to_operand_aliasing={{1}: (5, {}), {2}: (6, {})} | custom-call | tf_op jit(solution)/shard_map/more_output_terms/pallas_call | solution.py:422
  52.2 0.4 collective-permute-done.14.refs_1_
  52.6 7.8 %input_terms.1 = (bf16[64,7168]{1,0:T(8,128)(2,1)S(1)}, f32[4,16,2048]{2,1,0:T(8,128)S(1)}, bf16[4,16,2048]{2,1,0:T(8,128)(2,1)S(1)}) custom-call(s32[1]{0:T(128)} %bitcast.place_ref, bf16[32,7168]{1,0:T(8,128)(2,1)S(1)} %get-tuple-element.129.refs_0_, bf16[32,7168]{1,0:T(8,128)(2,1)S(1)} %collective-permute-done.14.refs_1_, ...), custom_call_target="tpu_custom_call" | custom-call | tf_op jit(solution)/shard_map/input_terms/pallas_call | solution.py:460
  60.4 1.6 %collective-permute-start.15 = (bf16[4,16,2048]{2,1,0:T(8,128)(2,1)S(1)}, bf16[4,16,2048]{2,1,0:T(8,128)(2,1)S(1)}, u32[]{:S(2)}, u32[]{:S(2)}) collective-permute-start(bf16[4,16,2048]{2,1,0:T(8,128)(2,1)S(1)} %get-tuple-element.138.refs_0_), channel_id=1, source_target_pairs={{0,4},{4,0},{8,12},{12,8},{16,20},{20,16},{24,28},{28,24},{1,5},{5... | collective-permute-start | bytes 786440 | tf_op jit(solution)/shard_map/ppermute | solution.py:36
  62.0 6.3 %outer.2.refs_0_ = bf16[2048,3584]{1,0:T(8,128)(2,1)} custom-call(bf16[64,2048]{1,0:T(8,128)(2,1)S(1)} %get-tuple-element.81.x_ref.left_ref, bf16[64,7168]{1,0:T(8,128)(2,1)S(1)} %get-tuple-element.139.right_ref, bf16[4,16,2048]{2,1,0:T(8,128)(2,1)S(1)} %get-tuple-element.138.refs_0_), custom_call_target="tpu_custom_call" | custom-call | bytes 14680064 | tf_op jit(solution)/shard_map/outer/pallas_call | solution.py:569
  68.3 0.6 collective-permute-done.15.near_ref
  68.9 0.1 row_sum.1
  69.0 0.7 collective-permute-start.16
  69.7 2.9 %collective-permute-start.17 = (bf16[16,2048]{1,0:T(8,128)(2,1)S(1)}, bf16[16,2048]{1,0:T(8,128)(2,1)S(1)}, u32[]{:S(2)}, u32[]{:S(2)}) collective-permute-start(bf16[16,2048]{1,0:T(8,128)(2,1)S(1)} %get-tuple-element.142), channel_id=1, source_target_pairs={{0,16},{4,20},{8,24},{12,28},{16,0},{20,4},{24,8},{28,12},{1,17},{... | collective-permute-start | bytes 196616 | tf_op jit(solution)/shard_map/ppermute | solution.py:36
  72.6 0.8 %collective-permute-start.18 = (bf16[16,2048]{1,0:T(8,128)(2,1)S(1)}, bf16[16,2048]{1,0:T(8,128)(2,1)S(1)}, u32[]{:S(2)}, u32[]{:S(2)}) collective-permute-start(bf16[16,2048]{1,0:T(8,128)(2,1)S(1)} %get-tuple-element.143), channel_id=1, source_target_pairs={{0,24},{4,28},{8,16},{12,20},{16,8},{20,12},{24,0},{28,4},{1,25},{... | collective-permute-start | bytes 196616 | tf_op jit(solution)/shard_map/ppermute | solution.py:36
  73.4 6.3 %outer.3.refs_3_ = bf16[2048,3584]{1,0:T(8,128)(2,1)} custom-call(bf16[64,2048]{1,0:T(8,128)(2,1)S(1)} %get-tuple-element.81.x_ref.left_ref, bf16[64,7168]{1,0:T(8,128)(2,1)S(1)} %get-tuple-element.139.right_ref, f32[16,2048]{1,0:T(8,128)S(1)} %get-tuple-element.140.refs_0_.total_ref), custom_call_target="tpu_custom_call" | custom-call | bytes 14680064 | tf_op jit(solution)/shard_map/outer/pallas_call | solution.py:569
  79.7 0.0 collective-permute-done.16.refs_0_
  79.7 0.0 collective-permute-done.17.refs_1_
  79.7 0.0 collective-permute-done.18.refs_2_
  79.7 0.6 last_sum.1
  (3 shorter events, 0.0 us)
Async XLA Ops:
  1.4 5.2 %collective-permute-start = (bf16[16,2048]{1,0:T(8,128)(2,1)S(1)}, bf16[16,2048]{1,0:T(8,128)(2,1)S(1)}, u32[]{:S(2)}, u32[]{:S(2)}) collective-permute-start(bf16[16,2048]{1,0:T(8,128)(2,1)S(1)} %pack.1.own_ref), channel_id=1, source_target_pairs={{0,4},{4,0},{8,12},{12,8},{16,20},{20,16},{24,28},{28,24},{1,5},{5... | collective-permute-start | bytes 196616 | tf_op jit(solution)/shard_map/ppermute | solution.py:36
  6.7 13.3 %collective-permute-start.3 = (bf16[32,2048]{1,0:T(8,128)(2,1)S(1)}, bf16[32,2048]{1,0:T(8,128)(2,1)S(1)}, u32[]{:S(2)}, u32[]{:S(2)}) collective-permute-start(bf16[32,2048]{1,0:T(8,128)(2,1)S(1)} %join.1.refs_0_), channel_id=1, source_target_pairs={{0,24},{4,28},{8,16},{12,20},{16,8},{20,12},{24,0},{28,4},{1,25},{... | collective-permute-start | bytes 393224 | tf_op jit(solution)/shard_map/ppermute | solution.py:36
  10.9 9.9 %collective-permute-start.2 = (bf16[32,2048]{1,0:T(8,128)(2,1)S(1)}, bf16[32,2048]{1,0:T(8,128)(2,1)S(1)}, u32[]{:S(2)}, u32[]{:S(2)}) collective-permute-start(bf16[32,2048]{1,0:T(8,128)(2,1)S(1)} %join.1.refs_0_), channel_id=1, source_target_pairs={{0,16},{4,20},{8,24},{12,28},{16,0},{20,4},{24,8},{28,12},{1,17},{... | collective-permute-start | bytes 393224 | tf_op jit(solution)/shard_map/ppermute | solution.py:36
  10.9 9.9 %collective-permute-start.1 = (bf16[32,2048]{1,0:T(8,128)(2,1)S(1)}, bf16[32,2048]{1,0:T(8,128)(2,1)S(1)}, u32[]{:S(2)}, u32[]{:S(2)}) collective-permute-start(bf16[32,2048]{1,0:T(8,128)(2,1)S(1)} %join.1.refs_0_), channel_id=1, source_target_pairs={{0,8},{4,12},{8,0},{12,4},{16,24},{20,28},{24,16},{28,20},{1,9},{5... | collective-permute-start | bytes 393224 | tf_op jit(solution)/shard_map/ppermute | solution.py:36
  24.9 3.4 %collective-permute-start.4 = (f32[32,3584]{1,0:T(8,128)S(1)}, f32[32,3584]{1,0:T(8,128)S(1)}, u32[]{:S(2)}, u32[]{:S(2)}) collective-permute-start(f32[32,3584]{1,0:T(8,128)S(1)} %get-tuple-element.86), channel_id=1, source_target_pairs={{0,1},{1,0},{2,3},{3,2},{4,5},{5,4},{6,7},{7,6},{8,9},{9,8},{10,11... | collective-permute-start | bytes 1376264 | tf_op jit(solution)/shard_map/ppermute | solution.py:36
  27.8 2.2 %collective-permute-start.6 = (f32[32,3584]{1,0:T(8,128)S(1)}, f32[32,3584]{1,0:T(8,128)S(1)}, u32[]{:S(2)}, u32[]{:S(2)}) collective-permute-start(f32[32,3584]{1,0:T(8,128)S(1)} %get-tuple-element.96), channel_id=1, source_target_pairs={{0,1},{1,0},{2,3},{3,2},{4,5},{5,4},{6,7},{7,6},{8,9},{9,8},{10,11... | collective-permute-start | bytes 1376264 | tf_op jit(solution)/shard_map/ppermute | solution.py:36
  28.4 11.3 %collective-permute-start.5 = (bf16[32,3584]{1,0:T(8,128)(2,1)S(1)}, bf16[32,3584]{1,0:T(8,128)(2,1)S(1)}, u32[]{:S(2)}, u32[]{:S(2)}) collective-permute-start(bf16[32,3584]{1,0:T(8,128)(2,1)S(1)} %get-tuple-element.94), channel_id=1, source_target_pairs={{0,2},{2,0},{1,3},{3,1},{4,6},{6,4},{5,7},{7,5},{8,10},{10,8},{9,1... | collective-permute-start | bytes 688136 | tf_op jit(solution)/shard_map/ppermute | solution.py:36
  30.0 10.9 %collective-permute-start.7 = (bf16[32,3584]{1,0:T(8,128)(2,1)S(1)}, bf16[32,3584]{1,0:T(8,128)(2,1)S(1)}, u32[]{:S(2)}, u32[]{:S(2)}) collective-permute-start(bf16[32,3584]{1,0:T(8,128)(2,1)S(1)} %get-tuple-element.101), channel_id=1, source_target_pairs={{0,2},{2,0},{1,3},{3,1},{4,6},{6,4},{5,7},{7,5},{8,10},{10,8},{9,1... | collective-permute-start | bytes 688136 | tf_op jit(solution)/shard_map/ppermute | solution.py:36
  39.0 2.2 %collective-permute-start.8 = (f32[32,896]{1,0:T(8,128)S(1)}, f32[32,896]{1,0:T(8,128)S(1)}, u32[]{:S(2)}, u32[]{:S(2)}) collective-permute-start(f32[32,896]{1,0:T(8,128)S(1)} %get-tuple-element.107), channel_id=1, source_target_pairs={{0,1},{1,0},{2,3},{3,2},{4,5},{5,4},{6,7},{7,6},{8,9},{9,8},{10,11... | collective-permute-start | bytes 344072 | tf_op jit(solution)/shard_map/ppermute | solution.py:36
  39.1 2.0 %collective-permute-start.9 = (f32[32,896]{1,0:T(8,128)S(1)}, f32[32,896]{1,0:T(8,128)S(1)}, u32[]{:S(2)}, u32[]{:S(2)}) collective-permute-start(f32[32,896]{1,0:T(8,128)S(1)} %get-tuple-element.109), channel_id=1, source_target_pairs={{0,1},{1,0},{2,3},{3,2},{4,5},{5,4},{6,7},{7,6},{8,9},{9,8},{10,11... | collective-permute-start | bytes 344072 | tf_op jit(solution)/shard_map/ppermute | solution.py:36
  39.6 1.6 %collective-permute-start.10 = (f32[32,896]{1,0:T(8,128)S(1)}, f32[32,896]{1,0:T(8,128)S(1)}, u32[]{:S(2)}, u32[]{:S(2)}) collective-permute-start(f32[32,896]{1,0:T(8,128)S(1)} %get-tuple-element.111), channel_id=1, source_target_pairs={{0,1},{1,0},{2,3},{3,2},{4,5},{5,4},{6,7},{7,6},{8,9},{9,8},{10,11... | collective-permute-start | bytes 344072 | tf_op jit(solution)/shard_map/ppermute | solution.py:36
  39.6 1.5 %collective-permute-start.11 = (f32[32,896]{1,0:T(8,128)S(1)}, f32[32,896]{1,0:T(8,128)S(1)}, u32[]{:S(2)}, u32[]{:S(2)}) collective-permute-start(f32[32,896]{1,0:T(8,128)S(1)} %get-tuple-element.113), channel_id=1, source_target_pairs={{0,1},{1,0},{2,3},{3,2},{4,5},{5,4},{6,7},{7,6},{8,9},{9,8},{10,11... | collective-permute-start | bytes 344072 | tf_op jit(solution)/shard_map/ppermute | solution.py:36
  41.1 1.8 %collective-permute-start.13 = (bf16[32,3584]{1,0:T(8,128)(2,1)S(1)}, bf16[32,3584]{1,0:T(8,128)(2,1)S(1)}, u32[]{:S(2)}, u32[]{:S(2)}) collective-permute-start(bf16[32,3584]{1,0:T(8,128)(2,1)S(1)} %get-tuple-element.122.refs_0_), channel_id=1, source_target_pairs={{0,1},{1,0},{2,3},{3,2},{4,5},{5,4},{6,7},{7,6},{8,9},{9,8},{10,11... | collective-permute-start | bytes 688136 | tf_op jit(solution)/shard_map/ppermute | solution.py:36
  41.3 9.1 %collective-permute-start.12 = (bf16[32,3584]{1,0:T(8,128)(2,1)S(1)}, bf16[32,3584]{1,0:T(8,128)(2,1)S(1)}, u32[]{:S(2)}, u32[]{:S(2)}) collective-permute-start(bf16[32,3584]{1,0:T(8,128)(2,1)S(1)} %get-tuple-element.121), channel_id=1, source_target_pairs={{0,2},{2,0},{1,3},{3,1},{4,6},{6,4},{5,7},{7,5},{8,10},{10,8},{9,1... | collective-permute-start | bytes 688136 | tf_op jit(solution)/shard_map/ppermute | solution.py:36
  50.7 1.9 %collective-permute-start.14 = (bf16[32,7168]{1,0:T(8,128)(2,1)S(1)}, bf16[32,7168]{1,0:T(8,128)(2,1)S(1)}, u32[]{:S(2)}, u32[]{:S(2)}) collective-permute-start(bf16[32,7168]{1,0:T(8,128)(2,1)S(1)} %get-tuple-element.129.refs_0_), channel_id=1, source_target_pairs={{0,1},{1,0},{2,3},{3,2},{4,5},{5,4},{6,7},{7,6},{8,9},{9,8},{10,11... | collective-permute-start | bytes 1376264 | tf_op jit(solution)/shard_map/ppermute | solution.py:36
  60.4 8.5 %collective-permute-start.15 = (bf16[4,16,2048]{2,1,0:T(8,128)(2,1)S(1)}, bf16[4,16,2048]{2,1,0:T(8,128)(2,1)S(1)}, u32[]{:S(2)}, u32[]{:S(2)}) collective-permute-start(bf16[4,16,2048]{2,1,0:T(8,128)(2,1)S(1)} %get-tuple-element.138.refs_0_), channel_id=1, source_target_pairs={{0,4},{4,0},{8,12},{12,8},{16,20},{20,16},{24,28},{28,24},{1,5},{5... | collective-permute-start | bytes 786440 | tf_op jit(solution)/shard_map/ppermute | solution.py:36
  69.0 10.8 %collective-permute-start.16 = (bf16[16,2048]{1,0:T(8,128)(2,1)S(1)}, bf16[16,2048]{1,0:T(8,128)(2,1)S(1)}, u32[]{:S(2)}, u32[]{:S(2)}) collective-permute-start(bf16[16,2048]{1,0:T(8,128)(2,1)S(1)} %get-tuple-element.141), channel_id=1, source_target_pairs={{0,8},{4,12},{8,0},{12,4},{16,24},{20,28},{24,16},{28,20},{1,9},{5... | collective-permute-start | bytes 196616 | tf_op jit(solution)/shard_map/ppermute | solution.py:36
  69.7 10.1 %collective-permute-start.17 = (bf16[16,2048]{1,0:T(8,128)(2,1)S(1)}, bf16[16,2048]{1,0:T(8,128)(2,1)S(1)}, u32[]{:S(2)}, u32[]{:S(2)}) collective-permute-start(bf16[16,2048]{1,0:T(8,128)(2,1)S(1)} %get-tuple-element.142), channel_id=1, source_target_pairs={{0,16},{4,20},{8,24},{12,28},{16,0},{20,4},{24,8},{28,12},{1,17},{... | collective-permute-start | bytes 196616 | tf_op jit(solution)/shard_map/ppermute | solution.py:36
  72.6 7.2 %collective-permute-start.18 = (bf16[16,2048]{1,0:T(8,128)(2,1)S(1)}, bf16[16,2048]{1,0:T(8,128)(2,1)S(1)}, u32[]{:S(2)}, u32[]{:S(2)}) collective-permute-start(bf16[16,2048]{1,0:T(8,128)(2,1)S(1)} %get-tuple-element.143), channel_id=1, source_target_pairs={{0,24},{4,28},{8,16},{12,20},{16,8},{20,12},{24,0},{28,4},{1,25},{... | collective-permute-start | bytes 196616 | tf_op jit(solution)/shard_map/ppermute | solution.py:36
